TPU v7x, 128 devices: a whole 4x4x4 slice. The times are simulated.
128 devices in a mesh: replica: 16 (over y, x_lo, core), fsdp: 8 (over x_hi, z).
Axes of the slice: x: 4 (x_hi: 2, x_lo: 2; x = x_hi * 2 + x_lo), y: 4, z: 4, core: 2. Of those that a mesh axis runs over, the one named last changes fastest.
Arguments:
- tokens: bfloat16 [16384, 4096], P(('replica', 'fsdp')), may hold values from -6 to 6
- out_grads: bfloat16 [16384, 14336], P(('replica', 'fsdp')), may hold values from -0.1875 to 0.1875
- block_ids: int32 [8], replicated, may hold values from 0 to 55, as said below
- left_basis: bfloat16 [16, 8, 1024, 1024], P('replica', 'fsdp'), may hold values from -0.1875 to 0.1875
- right_basis: bfloat16 [16, 8, 1024, 1024], P('replica', 'fsdp'), may hold values from -0.1875 to 0.1875
- first_moment: bfloat16 [16, 8, 1024, 1024], P('replica', 'fsdp'), may hold values from -3 to 3
- second_moment: bfloat16 [16, 8, 1024, 1024], P('replica', 'fsdp'), may hold values from 0.0099487305 to 1
- outer_params: float32 [1024, 8192], P('fsdp'), may hold values from -6 to 6
- outer_momentum: float32 [1024, 8192], P('fsdp'), may hold values from -3 to 3
- snapshot: bfloat16 [16, 1024, 8192], P('replica', 'fsdp'), may hold values from -6 to 6
- local_params: bfloat16 [16, 1024, 8192], P('replica', 'fsdp'), may hold values from -6 to 6
- due_rows: int32 [1024], P('fsdp'), may hold values 0 or 1
Outputs:
- update: bfloat16 [16, 8, 1024, 1024], P('replica', 'fsdp')
- first_next: bfloat16 [16, 8, 1024, 1024], P('replica', 'fsdp')
- second_next: bfloat16 [16, 8, 1024, 1024], P('replica', 'fsdp')
- outer_next: float32 [1024, 8192], P('fsdp')
- momentum_next: float32 [1024, 8192], P('fsdp')
- local_next: bfloat16 [16, 1024, 8192], P('replica', 'fsdp')
Inputs may be any that keep to these rules, and one draw needn't show every extreme that they name: `block_ids`: 8 different block numbers of the window; slot s belongs to fsdp index s.
All inputs are finite; a program needn't handle non-finite values. No bound on the sum of `due_rows` on one device may be relied on, other than what follows from the above.
Results may differ from a plain program's by a relative error of at most 0.022.
Values may be sent and summed in bfloat16 or wider, within the bound.
No kernel may reach another device: no remote copies, remote signals or barrier semaphores. Data moves between devices by JAX's collectives and lax.ppermute only.
A program may use at most 192 MiB of HBM per device.

v0:
```python
import jax
import jax.numpy as jnp
from jax import lax
from jax.sharding import PartitionSpec as P

FW = 14336
BLOCK = 1024


def per_device(
    tokens,
    out_grads,
    block_ids,
    left_basis,
    right_basis,
    first_moment,
    second_moment,
    outer_params,
    outer_momentum,
    snapshot,
    local_params,
    due_rows,
):
    columns = FW // BLOCK
    owned = left_basis.shape[1]

    def block_cols(block):
        row_start = block // columns * BLOCK
        col_start = block % columns * BLOCK
        xcols = lax.dynamic_slice_in_dim(tokens, row_start, BLOCK, 1)
        dcols = lax.dynamic_slice_in_dim(out_grads, col_start, BLOCK, 1)
        return (xcols, dcols)

    def block_term(block):
        xcols, dcols = block_cols(block)
        return lax.dot_general(
            xcols, dcols, (((0,), (0,)), ((), ())), preferred_element_type=jnp.float32
        )

    summed = lax.psum_scatter(
        lax.map(block_term, block_ids)
        .reshape(lax.axis_size("fsdp") * (owned * BLOCK), BLOCK)
        .astype(jnp.bfloat16),
        "fsdp",
        scatter_dimension=0,
        tiled=True,
    )
    grad = summed.reshape(owned, BLOCK, BLOCK)
    lefts = left_basis[0]
    rights = right_basis[0]
    half = jnp.einsum("kij,kil->kjl", lefts, grad, preferred_element_type=jnp.float32).astype(
        jnp.bfloat16
    )
    rotated = jnp.einsum("kjl,klm->kjm", half, rights, preferred_element_type=jnp.float32)
    moment_one = 0.95 * first_moment[0].astype(jnp.float32) + 0.05 * rotated
    moment_two = 0.95 * second_moment[0].astype(jnp.float32) + 0.05 * rotated * rotated
    correct = 1.0 - 0.95**10
    direction = (moment_one / correct / (jnp.sqrt(moment_two / correct) + 1e-08)).astype(
        jnp.bfloat16
    )
    back = jnp.einsum("kij,kjl->kil", lefts, direction, preferred_element_type=jnp.float32).astype(
        jnp.bfloat16
    )
    update = jnp.einsum("kil,kml->kim", back, rights, preferred_element_type=jnp.float32).astype(
        jnp.bfloat16
    )
    snap = snapshot[0].astype(jnp.float32)
    pseudo = lax.psum((outer_params - snap).astype(jnp.bfloat16), "replica").astype(
        jnp.float32
    ) / lax.axis_size("replica")
    moment = 0.9 * outer_momentum + pseudo
    stepped = outer_params - 0.7 * (pseudo + 0.9 * moment)
    due = (due_rows == 1)[:, None]
    outer_next = jnp.where(due, stepped, outer_params)
    momentum_next = jnp.where(due, moment, outer_momentum)
    merged = (stepped + (local_params[0].astype(jnp.float32) - snap)).astype(jnp.bfloat16)
    local_next = jnp.where(due, merged, local_params[0])
    return (
        update[None],
        moment_one.astype(jnp.bfloat16)[None],
        moment_two.astype(jnp.bfloat16)[None],
        outer_next,
        momentum_next,
        local_next[None],
    )


def solution(mesh):
    return jax.shard_map(
        per_device,
        mesh=mesh,
        in_specs=(
            P(("replica", "fsdp"), None),
            P(("replica", "fsdp"), None),
            P(),
            P("replica", "fsdp", None, None),
            P("replica", "fsdp", None, None),
            P("replica", "fsdp", None, None),
            P("replica", "fsdp", None, None),
            P("fsdp", None),
            P("fsdp", None),
            P("replica", "fsdp", None),
            P("replica", "fsdp", None),
            P("fsdp"),
        ),
        out_specs=(
            P("replica", "fsdp", None, None),
            P("replica", "fsdp", None, None),
            P("replica", "fsdp", None, None),
            P("fsdp", None),
            P("fsdp", None),
            P("replica", "fsdp", None),
        ),
        check_vma=False,
    )
```

profile of v0, /device:TPU:1, one launch (start us, length us, event | category | flops | bytes accessed | tf_op | source)
XLA Modules:
  0.0 298.4 jit_solution(5368982416282248436)
XLA Ops:
  8.0 0.0 copy-start
  8.0 0.0 copy-start.4
  8.0 0.0 all-reduce.2.cloned.1.call-start
  8.1 4.7 %fusion.3 = bf16[128,8192]{1,0:T(8,128)(2,1)} fusion(f32[128,8192]{1,0:T(8,128)} %param.21, bf16[1,128,8192]{2,1,0:T(8,128)(2,1)} %param.23), kind=kLoop, calls=%fused_computation.8 | loop fusion | flops 3145728 | bytes 8388608 | tf_op jit(solution)/shard_map/convert_element_type | solution.py:68
  12.8 0.0 all-reduce.2.cloned.1.call-update
  12.8 0.0 reduce-scatter.2.cloned.1.call-start
  12.9 0.0 copy-done.4
  12.9 45.4 %while.12 = (s32[]{:T(128)}, bf16[8,1024,1024]{2,1,0:T(8,128)(2,1)}, s32[8]{0:T(128)S(1)}, bf16[128,4096]{1,0:T(8,128)(2,1)}, bf16[128,14336]{1,0:T(8,128)(2,1)}...) while((s32[]{:T(128)}, ...), condition=%wide.region_1.2_spmd, body=%wide.region_0.1_spmd.sunk | while | flops 268435488 | bytes 4718964 | solution.py:41
  12.9 0.6 dynamic_slice.28
  15.5 3.1 %bitcast_dynamic-update-slice_fusion.2 = bf16[8,1024,1024]{2,1,0:T(8,128)(2,1)} fusion(bf16[8,1024,1024]{2,1,0:T(8,128)(2,1)} %get-tuple-element.135, s32[]{:T(128)S(6)} %copy.21, bf16[128,14336]{1,0:T(8,128)(2,1)} %get-tuple-element.152, s32[]{:T(128)S(6)} %select_n.55, bf16[128,4096]{1,0:T(8,128)(2,1)} %get-tuple-element.151, s32[]{:T(128)S(6)} %select_n.57), kind=kOutput, calls=%fused_computation.clone.1 | convolution fusion | flops 268435456 | bytes 4718604 | tf_op jit(solution)/shard_map/while/body/eval_jaxpr/dot_general | solution.py:36
  18.6 0.6 dynamic_slice.28
  21.1 3.1 %bitcast_dynamic-update-slice_fusion.2 = bf16[8,1024,1024]{2,1,0:T(8,128)(2,1)} fusion(bf16[8,1024,1024]{2,1,0:T(8,128)(2,1)} %get-tuple-element.135, s32[]{:T(128)S(6)} %copy.21, bf16[128,14336]{1,0:T(8,128)(2,1)} %get-tuple-element.152, s32[]{:T(128)S(6)} %select_n.55, bf16[128,4096]{1,0:T(8,128)(2,1)} %get-tuple-element.151, s32[]{:T(128)S(6)} %select_n.57), kind=kOutput, calls=%fused_computation.clone.1 | convolution fusion | flops 268435456 | bytes 4718604 | tf_op jit(solution)/shard_map/while/body/eval_jaxpr/dot_general | solution.py:36
  24.2 0.6 dynamic_slice.28
  26.8 3.1 %bitcast_dynamic-update-slice_fusion.2 = bf16[8,1024,1024]{2,1,0:T(8,128)(2,1)} fusion(bf16[8,1024,1024]{2,1,0:T(8,128)(2,1)} %get-tuple-element.135, s32[]{:T(128)S(6)} %copy.21, bf16[128,14336]{1,0:T(8,128)(2,1)} %get-tuple-element.152, s32[]{:T(128)S(6)} %select_n.55, bf16[128,4096]{1,0:T(8,128)(2,1)} %get-tuple-element.151, s32[]{:T(128)S(6)} %select_n.57), kind=kOutput, calls=%fused_computation.clone.1 | convolution fusion | flops 268435456 | bytes 4718604 | tf_op jit(solution)/shard_map/while/body/eval_jaxpr/dot_general | solution.py:36
  29.9 0.6 dynamic_slice.28
  32.5 3.1 %bitcast_dynamic-update-slice_fusion.2 = bf16[8,1024,1024]{2,1,0:T(8,128)(2,1)} fusion(bf16[8,1024,1024]{2,1,0:T(8,128)(2,1)} %get-tuple-element.135, s32[]{:T(128)S(6)} %copy.21, bf16[128,14336]{1,0:T(8,128)(2,1)} %get-tuple-element.152, s32[]{:T(128)S(6)} %select_n.55, bf16[128,4096]{1,0:T(8,128)(2,1)} %get-tuple-element.151, s32[]{:T(128)S(6)} %select_n.57), kind=kOutput, calls=%fused_computation.clone.1 | convolution fusion | flops 268435456 | bytes 4718604 | tf_op jit(solution)/shard_map/while/body/eval_jaxpr/dot_general | solution.py:36
  35.6 0.6 dynamic_slice.28
  38.1 3.1 %bitcast_dynamic-update-slice_fusion.2 = bf16[8,1024,1024]{2,1,0:T(8,128)(2,1)} fusion(bf16[8,1024,1024]{2,1,0:T(8,128)(2,1)} %get-tuple-element.135, s32[]{:T(128)S(6)} %copy.21, bf16[128,14336]{1,0:T(8,128)(2,1)} %get-tuple-element.152, s32[]{:T(128)S(6)} %select_n.55, bf16[128,4096]{1,0:T(8,128)(2,1)} %get-tuple-element.151, s32[]{:T(128)S(6)} %select_n.57), kind=kOutput, calls=%fused_computation.clone.1 | convolution fusion | flops 268435456 | bytes 4718604 | tf_op jit(solution)/shard_map/while/body/eval_jaxpr/dot_general | solution.py:36
  41.3 0.6 dynamic_slice.28
  43.9 3.1 %bitcast_dynamic-update-slice_fusion.2 = bf16[8,1024,1024]{2,1,0:T(8,128)(2,1)} fusion(bf16[8,1024,1024]{2,1,0:T(8,128)(2,1)} %get-tuple-element.135, s32[]{:T(128)S(6)} %copy.21, bf16[128,14336]{1,0:T(8,128)(2,1)} %get-tuple-element.152, s32[]{:T(128)S(6)} %select_n.55, bf16[128,4096]{1,0:T(8,128)(2,1)} %get-tuple-element.151, s32[]{:T(128)S(6)} %select_n.57), kind=kOutput, calls=%fused_computation.clone.1 | convolution fusion | flops 268435456 | bytes 4718604 | tf_op jit(solution)/shard_map/while/body/eval_jaxpr/dot_general | solution.py:36
  47.0 0.6 dynamic_slice.28
  49.5 3.1 %bitcast_dynamic-update-slice_fusion.2 = bf16[8,1024,1024]{2,1,0:T(8,128)(2,1)} fusion(bf16[8,1024,1024]{2,1,0:T(8,128)(2,1)} %get-tuple-element.135, s32[]{:T(128)S(6)} %copy.21, bf16[128,14336]{1,0:T(8,128)(2,1)} %get-tuple-element.152, s32[]{:T(128)S(6)} %select_n.55, bf16[128,4096]{1,0:T(8,128)(2,1)} %get-tuple-element.151, s32[]{:T(128)S(6)} %select_n.57), kind=kOutput, calls=%fused_computation.clone.1 | convolution fusion | flops 268435456 | bytes 4718604 | tf_op jit(solution)/shard_map/while/body/eval_jaxpr/dot_general | solution.py:36
  52.6 0.6 dynamic_slice.28
  55.2 3.1 %bitcast_dynamic-update-slice_fusion.2 = bf16[8,1024,1024]{2,1,0:T(8,128)(2,1)} fusion(bf16[8,1024,1024]{2,1,0:T(8,128)(2,1)} %get-tuple-element.135, s32[]{:T(128)S(6)} %copy.21, bf16[128,14336]{1,0:T(8,128)(2,1)} %get-tuple-element.152, s32[]{:T(128)S(6)} %select_n.55, bf16[128,4096]{1,0:T(8,128)(2,1)} %get-tuple-element.151, s32[]{:T(128)S(6)} %select_n.57), kind=kOutput, calls=%fused_computation.clone.1 | convolution fusion | flops 268435456 | bytes 4718604 | tf_op jit(solution)/shard_map/while/body/eval_jaxpr/dot_general | solution.py:36
  58.3 0.0 copy-start.5
  58.3 0.0 reduce-scatter.2.cloned.1.call-update
  58.3 0.6 copy-done.5
  58.9 115.7 %all-reduce.2.cloned.1.call-done = bf16[128,8192]{1,0:T(8,128)(2,1)} async-done(((bf16[128,8192]{1,0:T(8,128)(2,1)}), bf16[128,8192]{1,0:T(8,128)(2,1)}) %all-reduce.2.cloned.1.call-update) | async-done | bytes 2097168 | tf_op jit(solution)/shard_map/psum | solution.py:68
  174.6 0.0 copy-start.1
  174.6 0.0 copy-start.2
  174.6 0.0 copy-start.3
  174.7 7.3 %fusion.13 = bf16[1,128,8192]{2,1,0:T(8,128)(2,1)} fusion(bf16[1,128,8192]{2,1,0:T(8,128)(2,1)} %param.23, bf16[1,128,8192]{2,1,0:T(8,128)(2,1)} %param.24, pred[128]{0:T(512)(128)(4,1)S(1)} %broadcast_compare_fusion, f32[128,8192]{1,0:T(8,128)} %param.21, f32[128,8192]{1,0:T(8,128)} %param.22, bf16[128,8192]{1,0:T(8,128)(2,1)} %all-reduce.2.cloned.1.call-done), kind=kLoop, calls=%fused_computation.22 | loop fusion | flops 14680064 | bytes 16777344 | tf_op jit(solution)/shard_map/broadcast_in_dim | solution.py:84
  181.9 0.0 copy-done.1
  181.9 1.2 copy-done.2
  183.2 0.6 copy-done.3
  183.8 4.8 %fusion.7 = (f32[128,8192]{1,0:T(8,128)}, f32[128,8192]{1,0:T(8,128)}) fusion(f32[128,8192]{1,0:T(8,128)S(1)} %copy-done.2, bf16[128,8192]{1,0:T(8,128)(2,1)S(1)} %copy-done.3, pred[128]{0:T(512)(128)(4,1)S(1)} %broadcast_compare_fusion, f32[128,8192]{1,0:T(8,128)S(1)} %copy-done.1), kind=kLoop, calls=%fused_computation.14 | loop fusion | flops 10485760 | bytes 18874496 | tf_op jit(solution)/shard_map/jit(_where)/select_n | solution.py:75
  188.5 74.2 %reduce-scatter.2.cloned.1.call-done = bf16[1024,1024]{1,0:T(8,128)(2,1)} async-done(((bf16[8192,1024]{1,0:T(8,128)(2,1)}), bf16[1024,1024]{1,0:T(8,128)(2,1)}) %reduce-scatter.2.cloned.1.call-update) | async-done | bytes 2097168 | tf_op jit(solution)/shard_map/reduce_scatter | solution.py:40
  262.8 0.0 copy-done
  262.8 8.7 %fusion.16 = f32[1024,1024]{1,0:T(8,128)} fusion(bf16[1,1,1024,1024]{3,2,1,0:T(8,128)(2,1)S(1)} %copy-done, bf16[1024,1024]{1,0:T(8,128)(2,1)} %reduce-scatter.2.cloned.1.call-done, bf16[1,1,1024,1024]{3,2,1,0:T(8,128)(2,1)} %param.17), kind=kOutput, calls=%fused_computation.25 | convolution fusion | flops 4296015872 | bytes 10485760 | tf_op jit(solution)/shard_map/kjl,klm->kjm/dot_general | solution.py:54
  271.5 12.5 %convert_bitcast_fusion = bf16[1,1,1024,1024]{3,2,1,0:T(8,128)(2,1)} fusion(bf16[1,1,1024,1024]{3,2,1,0:T(8,128)(2,1)S(1)} %copy-done, bf16[1,1,1024,1024]{3,2,1,0:T(8,128)(2,1)} %param.17, f32[1024,1024]{1,0:T(8,128)} %fusion.16, bf16[1,1,1024,1024]{3,2,1,0:T(8,128)(2,1)} %param.19, bf16[1,1,1024,1024]{3,2,1,0:T(8,128)(2,1)} %param.20), kind=kOutput, calls=%fused_computation.31 | convolution fusion | flops 4310695936 | bytes 14680064 | tf_op jit(solution)/shard_map/kil,kml->kim/dot_general | solution.py:64
  284.0 6.9 %fusion.11 = (bf16[1,1,1024,1024]{3,2,1,0:T(8,128)(2,1)}, bf16[1,1,1024,1024]{3,2,1,0:T(8,128)(2,1)}) fusion(f32[1024,1024]{1,0:T(8,128)} %fusion.16, bf16[1,1,1024,1024]{3,2,1,0:T(8,128)(2,1)} %param.20, bf16[1,1,1024,1024]{3,2,1,0:T(8,128)(2,1)} %param.19), kind=kLoop, calls=%fused_computation.20 | loop fusion | flops 10485760 | bytes 12582912 | tf_op jit(solution)/shard_map/broadcast_in_dim | solution.py:81
  (2 shorter events, 0.0 us)
Async XLA Ops:
  8.0 254.8 %copy-start = (bf16[1,1,1024,1024]{3,2,1,0:T(8,128)(2,1)S(1)}, bf16[1,1,1024,1024]{3,2,1,0:T(8,128)(2,1)}, u32[]{:S(2)}) copy-start(bf16[1,1,1024,1024]{3,2,1,0:T(8,128)(2,1)} %param.18) | copy-start | bytes 6291460
  8.0 4.9 %copy-start.4 = (s32[8]{0:T(128)S(1)}, s32[8]{0:T(128)}, u32[]{:S(2)}) copy-start(s32[8]{0:T(128)} %param.16) | copy-start | bytes 100
  8.0 166.6 %all-reduce.2.cloned.1.call-start = ((), (), s32[]{:S(2)}) async-start(), calls=%async_computation.2 | async-start | bytes 4194304 | tf_op jit(solution)/shard_map/psum | solution.py:68
  12.8 249.9 %reduce-scatter.2.cloned.1.call-start = ((), (), s32[]{:S(2)}) async-start(), calls=%async_computation.1 | async-start | bytes 18874368 | tf_op jit(solution)/shard_map/reduce_scatter | solution.py:40
  58.3 0.7 copy-start.5
  174.6 7.3 %copy-start.1 = (f32[128,8192]{1,0:T(8,128)S(1)}, f32[128,8192]{1,0:T(8,128)}, u32[]{:S(2)}) copy-start(f32[128,8192]{1,0:T(8,128)} %param.21) | copy-start | bytes 12582916
  174.6 8.5 %copy-start.2 = (f32[128,8192]{1,0:T(8,128)S(1)}, f32[128,8192]{1,0:T(8,128)}, u32[]{:S(2)}) copy-start(f32[128,8192]{1,0:T(8,128)} %param.22) | copy-start | bytes 12582916
  174.6 9.1 %copy-start.3 = (bf16[128,8192]{1,0:T(8,128)(2,1)S(1)}, bf16[128,8192]{1,0:T(8,128)(2,1)}, u32[]{:S(2)}) copy-start(bf16[128,8192]{1,0:T(8,128)(2,1)} %all-reduce.2.cloned.1.call-done) | copy-start | bytes 6291460
Sparse Core Ops, SparseCore 0:
  12.9 161.6 all-reduce.1
Sparse Core Ops, SparseCore 1:
  58.4 204.3 reduce-scatter.1
where the time goes:
time: 301 us; the launch traced here: 298 us
  waiting for transfers between devices  190 us (63%)
  matrix products  46.1 us (15%)
  other arithmetic  23.7 us (8%)
  loops' own time  15.9 us (5%)
  between operations  15.5 us (5%)
  local copies, waits for them, and re-layouts  7.13 us (2%)
    psum x1, waiting for transfers between devices, per_device(): lax.psum((outer_params - snap).astype(jnp.bfloat16), 'replica')  116 us
    reduce_scatter x1, waiting for transfers between devices, per_device(): lax.psum_scatter(lax.map(block_term, block_ids).reshape(lax.axis_size('fs...  74.2 us
    dot_general x8, matrix products, block_term(): lax.dot_general(xcols, dcols, (((0,), (0,)), ((), ())), preferred_element...  24.8 us
    another operation x1, loops' own time, per_device(): lax.map(block_term, block_ids)  15.9 us
    dot_general x1, matrix products, per_device(): jnp.einsum('kil,kml->kim', back, rights, preferred_element_type=jnp.float32)  12.5 us
    dot_general x1, matrix products, per_device(): jnp.einsum('kjl,klm->kjm', half, rights, preferred_element_type=jnp.float32)  8.75 us
    broadcast_in_dim x1, other arithmetic, per_device(): local_next[None]  7.28 us
    broadcast_in_dim x1, other arithmetic, per_device(): moment_two.astype(jnp.bfloat16)[None]  6.92 us
  transfers between devices with their start and end apart: 2, of which 2 were waited for; matrix products, arithmetic and copies ran while one was open for 14% of the time, Pallas kernels for 0%

commit v1 on v0

v1 whole, which is shorter than its diff:
```python
import jax
import jax.numpy as jnp
from jax import lax
from jax.sharding import PartitionSpec as P

FW = 14336
BLOCK = 1024
AXES = ("replica", "fsdp")
SHIFTS = ((1, 2), (1, 1), (1, 3), (0, 2), (1, 0), (0, 1), (0, 3))


def place(index):
    replica, fsdp = divmod(index, 8)
    return replica // 4, replica // 2 % 2, replica % 2, fsdp // 4, fsdp % 4


def index_of(y, x_lo, core, x_hi, z):
    return ((y % 4 * 2 + x_lo % 2) * 2 + core % 2) * 8 + x_hi % 2 * 4 + z % 4


def moved(array, y=0, x_lo=0, core=0, x_hi=0, z=0):
    pairs = []
    for source in range(128):
        at = place(source)
        pairs.append((source, index_of(at[0] + y, at[1] + x_lo, at[2] + core, at[3] + x_hi, at[4] + z)))
    return lax.ppermute(array, AXES, pairs)


def per_device(
    tokens,
    out_grads,
    block_ids,
    left_basis,
    right_basis,
    first_moment,
    second_moment,
    outer_params,
    outer_momentum,
    snapshot,
    local_params,
    due_rows,
):
    columns = FW // BLOCK
    me = lax.axis_index("fsdp")
    x_hi, z = me // 4, me % 4
    replica = lax.axis_index("replica")
    y, core = replica // 4, replica % 2

    def factors(owner):
        block = block_ids[owner]
        xcols = lax.dynamic_slice_in_dim(tokens, block // columns * BLOCK, BLOCK, 1)
        dcols = lax.dynamic_slice_in_dim(out_grads, block % columns * BLOCK, BLOCK, 1)
        return jnp.concatenate([xcols, dcols], axis=1)

    got = []
    for dx, dz in SHIFTS:
        owner = (x_hi + dx) % 2 * 4 + (z + dz) % 4
        got.append(moved(factors(owner), x_hi=dx, z=dz))
    got.append(factors(me))
    both = jnp.concatenate(got, axis=0)
    grad = lax.dot_general(
        both[:, :BLOCK], both[:, BLOCK:], (((0,), (0,)), ((), ())), preferred_element_type=jnp.float32
    ).astype(jnp.bfloat16)
    left = left_basis[0, 0]
    right = right_basis[0, 0]
    f32 = jnp.float32
    half = lax.dot_general(left, grad, (((0,), (0,)), ((), ())), preferred_element_type=f32).astype(jnp.bfloat16)
    rotated = jnp.dot(half, right, preferred_element_type=f32)
    moment_one = 0.95 * first_moment[0, 0].astype(f32) + 0.05 * rotated
    moment_two = 0.95 * second_moment[0, 0].astype(f32) + 0.05 * rotated * rotated
    correct = 1.0 - 0.95**10
    direction = (moment_one / correct / (jnp.sqrt(moment_two / correct) + 1e-08)).astype(jnp.bfloat16)
    back = jnp.dot(left, direction, preferred_element_type=f32).astype(jnp.bfloat16)
    update = lax.dot_general(back, right, (((1,), (1,)), ((), ())), preferred_element_type=f32).astype(jnp.bfloat16)

    snap = snapshot[0].astype(f32)
    diff = (outer_params - snap).astype(jnp.bfloat16).reshape(2, 4, 16, 8192)
    other = moved(lax.dynamic_index_in_dim(diff, 1 - core, 0, False), core=1)
    pair = (lax.dynamic_index_in_dim(diff, core, 0, False).astype(f32) + other.astype(f32)).astype(jnp.bfloat16)
    parts = [lax.dynamic_index_in_dim(pair, y, 0, False)]
    for dy in (1, 2, 3):
        parts.append(moved(lax.dynamic_index_in_dim(pair, (y + dy) % 4, 0, False), y=dy))
    plane = sum(p.astype(f32) for p in parts).astype(jnp.bfloat16)
    total = (plane.astype(f32) + moved(plane, x_lo=1).astype(f32)).astype(jnp.bfloat16)
    rows = jnp.zeros((4, 16, 8192), jnp.bfloat16)
    rows = lax.dynamic_update_index_in_dim(rows, total, y, 0)
    for dy in (1, 2, 3):
        rows = lax.dynamic_update_index_in_dim(rows, moved(total, y=dy), (y - dy) % 4, 0)
    other = moved(rows, core=1)
    whole = jnp.where(core == 0, jnp.stack([rows, other]), jnp.stack([other, rows])).reshape(128, 8192)
    pseudo = whole.astype(f32) / lax.axis_size("replica")
    moment = 0.9 * outer_momentum + pseudo
    stepped = outer_params - 0.7 * (pseudo + 0.9 * moment)
    due = (due_rows == 1)[:, None]
    outer_next = jnp.where(due, stepped, outer_params)
    momentum_next = jnp.where(due, moment, outer_momentum)
    merged = (stepped + (local_params[0].astype(f32) - snap)).astype(jnp.bfloat16)
    local_next = jnp.where(due, merged, local_params[0])
    return (
        update[None, None],
        moment_one.astype(jnp.bfloat16)[None, None],
        moment_two.astype(jnp.bfloat16)[None, None],
        outer_next,
        momentum_next,
        local_next[None],
    )


def solution(mesh):
    return jax.shard_map(
        per_device,
        mesh=mesh,
        in_specs=(
            P(("replica", "fsdp"), None),
            P(("replica", "fsdp"), None),
            P(),
            P("replica", "fsdp", None, None),
            P("replica", "fsdp", None, None),
            P("replica", "fsdp", None, None),
            P("replica", "fsdp", None, None),
            P("fsdp", None),
            P("fsdp", None),
            P("replica", "fsdp", None),
            P("replica", "fsdp", None),
            P("fsdp"),
        ),
        out_specs=(
            P("replica", "fsdp", None, None),
            P("replica", "fsdp", None, None),
            P("replica", "fsdp", None, None),
            P("fsdp", None),
            P("fsdp", None),
            P("replica", "fsdp", None),
        ),
        check_vma=False,
    )
```

time: 301 us -> 160 us (0.53)
  waiting for transfers between devices: 190 us -> 41.8 us
  starting transfers between devices: 0.08 us -> 26.2 us
  matrix products: 46.1 us -> 25.1 us
  loops' own time: 15.9 us -> 0 us
  other arithmetic: 23.7 us -> 36.2 us
  local copies, waits for them, and re-layouts: 7.13 us -> 13.1 us
    psum x1 -> x0, waiting for transfers between devices: 116 us -> none  [per_device(): lax.psum((outer_params - snap).astype(jnp.bfloat16), 'replica')]
    reduce_scatter x1 -> x0, waiting for transfers between devices: 74.2 us -> none  [per_device(): lax.psum_scatter(lax.map(block_term, block_ids).reshape(lax.axis_size('fs...]
    ppermute x0 -> x16, waiting for transfers between devices: none -> 41.8 us  [moved(): return lax.ppermute(array, AXES, pairs)]
    ppermute x0 -> x16, starting transfers between devices: none -> 26.2 us  [moved(): return lax.ppermute(array, AXES, pairs)]
    dot_general x10 -> x3, matrix products: 46.1 us -> 25.1 us  [the longest x1 12.5 us: per_device(): lax.dot_general(back, right, (((1,), (1,)), ((), ())), preferred_element_...]
    another operation x1 -> x0, loops' own time: 15.9 us -> none  [per_device(): lax.map(block_term, block_ids)]
    concatenate x0 -> x8, other arithmetic: none -> 7.94 us  [the longest x7 7.9 us: factors(): return jnp.concatenate([xcols, dcols], axis=1)]
    unnamed x12 -> x21, local copies, waits for them, and re-layouts: 2.47 us -> 6.11 us
  transfers between devices with their start and end apart: 2 -> 16, of which waited for: 2 -> 9; matrix products, arithmetic and copies ran while one was open for 14% -> 32% of each run, Pallas kernels for 0% -> 0%
where the time goes in v1:
time: 160 us; the launch traced here: 159 us
  waiting for transfers between devices  41.8 us (26%)
  other arithmetic  36.2 us (23%)
  starting transfers between devices  26.2 us (16%)
  matrix products  25.1 us (16%)
  between operations  17 us (11%)
  local copies, waits for them, and re-layouts  13.1 us (8%)
    ppermute x16, waiting for transfers between devices, moved(): return lax.ppermute(array, AXES, pairs)  41.8 us
    ppermute x16, starting transfers between devices, moved(): return lax.ppermute(array, AXES, pairs)  26.2 us
    dot_general x1, matrix products, per_device(): lax.dot_general(back, right, (((1,), (1,)), ((), ())), preferred_element_...  12.5 us
    dot_general x1, matrix products, per_device(): rotated = jnp.dot(half, right, preferred_element_type=f32)  8.81 us
    concatenate x7, other arithmetic, factors(): return jnp.concatenate([xcols, dcols], axis=1)  7.9 us
    select_n x1, other arithmetic, per_device(): momentum_next = jnp.where(due, moment, outer_momentum)  7.1 us
    broadcast_in_dim x1, other arithmetic, per_device(): moment_two.astype(jnp.bfloat16)[None, None]  6.93 us
    unnamed x21, local copies, waits for them, and re-layouts  6.11 us
  transfers between devices with their start and end apart: 16, of which 9 were waited for; matrix products, arithmetic and copies ran while one was open for 32% of the time, Pallas kernels for 0%

profile of v1, /device:TPU:1, one launch (start us, length us, event | category | flops | bytes accessed | tf_op | source)
XLA Modules:
  0.0 159.5 jit_solution(10357106014634976032)
XLA Ops:
  0.6 0.0 copy-start
  0.8 1.7 %fusion.55 = (s32[1]{0:T(128)}, s32[1]{0:T(128)}, s32[1]{0:T(128)}, s32[1]{0:T(128)}, s32[1]{0:T(128)}, /*index=5*/s32[1]{0:T(128)}, s32[1]{0:T(128)}, s32[1]{0:T(128)}) fusion(s32[8]{0:T(128)} %param.14, s32[]{:T(128)S(6)} %select_n.305, s32[]{:T(128)S(6)} %select_n.295, s32[]{:T(128)S(6)} %select_n.290, s32[]{:T(128)S(6)} %select_n.284, s32[]{:T(128)S(6)} %select_n.278, ...), kind=kLoop, calls=%fused_computation.89 | loop fusion | bytes 96 | tf_op jit(solution)/shard_map/dynamic_slice | solution.py:50
  18.4 3.8 %constant_dynamic-slice_fusion = (bf16[128,1024]{1,0:T(8,128)(2,1)S(1)}, bf16[128,1024]{1,0:T(8,128)(2,1)}, bf16[128,1024]{1,0:T(8,128)(2,1)S(1)}, bf16[128,1024...) fusion(bf16[128,14336]{1,0:T(8,128)(2,1)} %param.13, ...), kind=kLoop, calls=%fused_computation.68 | loop fusion | bytes 8388672 | tf_op jit(solution)/shard_map/dynamic_slice | solution.py:52
  22.2 0.8 pad_maximum_fusion
  23.0 6.9 %collective-permute-start = (bf16[128,2048]{1,0:T(8,128)(2,1)}, bf16[128,2048]{1,0:T(8,128)(2,1)}, u32[]{:S(2)}, u32[]{:S(2)}) collective-permute-start(bf16[128,2048]{1,0:T(8,128)(2,1)} %pad_maximum_fusion), channel_id=1, source_target_pairs={{0,6},{1,7},{2,4},{3,5},{4,2},{5,3},{6,0},{7,1},{8,14},{9,15},{10,... | collective-permute-start | bytes 1572872 | tf_op jit(solution)/shard_map/ppermute | solution.py:26
  29.9 0.8 pad_maximum_fusion.1
  30.7 0.7 collective-permute-start.1
  31.4 0.8 pad_maximum_fusion.2
  32.3 4.4 %collective-permute-start.2 = (bf16[128,2048]{1,0:T(8,128)(2,1)}, bf16[128,2048]{1,0:T(8,128)(2,1)}, u32[]{:S(2)}, u32[]{:S(2)}) collective-permute-start(bf16[128,2048]{1,0:T(8,128)(2,1)} %pad_maximum_fusion.2), channel_id=1, source_target_pairs={{0,7},{1,4},{2,5},{3,6},{4,3},{5,0},{6,1},{7,2},{8,15},{9,12},{10,... | collective-permute-start | bytes 1572872 | tf_op jit(solution)/shard_map/ppermute | solution.py:26
  36.6 0.8 pad_maximum_fusion.3
  37.5 0.0 collective-permute-start.3
  37.5 0.8 pad_maximum_fusion.4
  38.3 0.2 collective-permute-start.4
  38.5 4.6 %fusion = bf16[128,8192]{1,0:T(8,128)(2,1)} fusion(f32[128,8192]{1,0:T(8,128)} %param.19, bf16[1,128,8192]{2,1,0:T(8,128)(2,1)} %param.21), kind=kLoop, calls=%fused_computation.4 | loop fusion | flops 3145728 | bytes 8388608 | tf_op jit(solution)/shard_map/convert_element_type | solution.py:77
  43.1 1.3 dynamic-slice_bitcast_fusion
  44.4 1.9 %pad_maximum_fusion.5 = bf16[128,2048]{1,0:T(8,128)(2,1)} fusion(bf16[128,1024]{1,0:T(8,128)(2,1)} %get-tuple-element.13, bf16[128,1024]{1,0:T(8,128)(2,1)} %get-tuple-element.45), kind=kLoop, calls=%fused_computation.46 | loop fusion | flops 1048576 | bytes 1048576 | tf_op jit(solution)/shard_map/concatenate | solution.py:53
  46.3 1.9 %pad_maximum_fusion.6 = bf16[128,2048]{1,0:T(8,128)(2,1)} fusion(bf16[128,1024]{1,0:T(8,128)(2,1)} %get-tuple-element.19, bf16[128,1024]{1,0:T(8,128)(2,1)} %get-tuple-element.39), kind=kLoop, calls=%fused_computation.47 | loop fusion | flops 1048576 | bytes 1048576 | tf_op jit(solution)/shard_map/concatenate | solution.py:53
  48.2 0.0 copy-done.6
  48.3 0.0 copy-start.3
  48.3 0.0 collective-permute-done
  48.4 0.7 collective-permute-start.5
  49.1 1.1 constant_dynamic-update-slice_fusion.6
  50.2 3.0 %collective-permute-done.1 = bf16[128,2048]{1,0:T(8,128)(2,1)} collective-permute-done((bf16[128,2048]{1,0:T(8,128)(2,1)}, bf16[128,2048]{1,0:T(8,128)(2,1)}, u32[]{:S(2)}, u32[]{:S(2)}) %collective-permute-start.1) | collective-permute-done | bytes 524320 | tf_op jit(solution)/shard_map/ppermute | solution.py:26
  53.2 0.2 collective-permute-start.6
  53.4 1.1 constant_dynamic-update-slice_fusion.5
  54.5 10.7 %collective-permute-done.2 = bf16[128,2048]{1,0:T(8,128)(2,1)} collective-permute-done((bf16[128,2048]{1,0:T(8,128)(2,1)}, bf16[128,2048]{1,0:T(8,128)(2,1)}, u32[]{:S(2)}, u32[]{:S(2)}) %collective-permute-start.2) | collective-permute-done | bytes 524320 | tf_op jit(solution)/shard_map/ppermute | solution.py:26
  65.1 2.8 %collective-permute-start.7 = (bf16[4,16,8192]{2,1,0:T(8,128)(2,1)S(1)}, bf16[4,16,8192]{2,1,0:T(8,128)(2,1)S(1)}, u32[]{:S(2)}, u32[]{:S(2)}) collective-permute-start(bf16[4,16,8192]{2,1,0:T(8,128)(2,1)S(1)} %dynamic-slice_bitcast_fusion), channel_id=1, source_target_pairs={{0,8},{1,9},{2,10},{3,11},{4,12},{5,13},{6,14},{7,15},{8,0},{9,1},... | collective-permute-start | bytes 3145736 | tf_op jit(solution)/shard_map/ppermute | solution.py:26
  67.9 1.1 constant_dynamic-update-slice_fusion.4
  69.0 0.0 collective-permute-done.3
  69.0 1.1 constant_dynamic-update-slice_fusion.3
  70.1 5.9 %collective-permute-done.4 = bf16[128,2048]{1,0:T(8,128)(2,1)} collective-permute-done((bf16[128,2048]{1,0:T(8,128)(2,1)}, bf16[128,2048]{1,0:T(8,128)(2,1)}, u32[]{:S(2)}, u32[]{:S(2)}) %collective-permute-start.4) | collective-permute-done | bytes 524320 | tf_op jit(solution)/shard_map/ppermute | solution.py:26
  75.9 1.1 constant_dynamic-update-slice_fusion.2
  77.0 0.0 collective-permute-done.5
  77.1 0.2 collective-permute-done.6
  77.4 0.0 collective-permute-done.7
  77.4 0.2 fusion.16
  77.7 0.1 dynamic-slice_bitcast_fusion.3
  77.7 2.8 %collective-permute-start.10 = (bf16[16,8192]{1,0:T(8,128)(2,1)S(1)}, bf16[16,8192]{1,0:T(8,128)(2,1)S(1)}, u32[]{:S(2)}, u32[]{:S(2)}) collective-permute-start(bf16[16,8192]{1,0:T(8,128)(2,1)S(1)} %get-tuple-element.21), channel_id=1, source_target_pairs={{0,96},{1,97},{2,98},{3,99},{4,100},{5,101},{6,102},{7,103},{8,104... | collective-permute-start | bytes 786440 | tf_op jit(solution)/shard_map/ppermute | solution.py:26
  80.6 0.3 collective-permute-start.9
  80.9 0.7 collective-permute-start.8
  81.6 3.8 %fusion.13 = bf16[1024,1024]{1,0:T(8,128)(2,1)} fusion(bf16[1024,2048]{1,0:T(8,128)(2,1)S(1)} %maximum_dynamic-update-slice_fusion), kind=kOutput, calls=%fused_computation.21 | convolution fusion | flops 2147483648 | bytes 6291456 | tf_op jit(solution)/shard_map/dot_general | solution.py:61
  85.4 0.5 collective-permute-done.10
  85.8 2.5 %collective-permute-done.9 = bf16[16,8192]{1,0:T(8,128)(2,1)S(1)} collective-permute-done((bf16[16,8192]{1,0:T(8,128)(2,1)S(1)}, bf16[16,8192]{1,0:T(8,128)(2,1)S(1)}, u32[]{:S(2)}, u32[]{:S(2)}) %collective-permute-start.9) | collective-permute-done | bytes 262176 | tf_op jit(solution)/shard_map/ppermute | solution.py:26
  88.3 7.6 %collective-permute-done.8 = bf16[16,8192]{1,0:T(8,128)(2,1)S(1)} collective-permute-done((bf16[16,8192]{1,0:T(8,128)(2,1)S(1)}, bf16[16,8192]{1,0:T(8,128)(2,1)S(1)}, u32[]{:S(2)}, u32[]{:S(2)}) %collective-permute-start.8) | collective-permute-done | bytes 262176 | tf_op jit(solution)/shard_map/ppermute | solution.py:26
  95.9 0.1 fusion.46
  96.0 1.5 collective-permute-start.11
  97.6 8.8 %fusion.19 = f32[1024,1024]{1,0:T(8,128)} fusion(bf16[1,1,1024,1024]{3,2,1,0:T(8,128)(2,1)S(1)} %copy-done, bf16[1,1,1024,1024]{3,2,1,0:T(8,128)(2,1)} %param.15, bf16[1024,1024]{1,0:T(8,128)(2,1)} %fusion.13), kind=kOutput, calls=%fused_computation.29 | convolution fusion | flops 4296015872 | bytes 10485760 | tf_op jit(solution)/shard_map/dot_general | solution.py:68
  106.4 0.0 collective-permute-done.11
  106.4 0.1 broadcast_in_dim.50
  106.5 1.0 bitcast_dynamic-update-slice_fusion.3
  107.5 0.1 collective-permute-start.12
  107.6 6.9 %fusion.10 = (bf16[1,1,1024,1024]{3,2,1,0:T(8,128)(2,1)}, bf16[1,1,1024,1024]{3,2,1,0:T(8,128)(2,1)}) fusion(f32[1024,1024]{1,0:T(8,128)} %fusion.19, bf16[1,1,1024,1024]{3,2,1,0:T(8,128)(2,1)} %param.18, bf16[1,1,1024,1024]{3,2,1,0:T(8,128)(2,1)} %param.17), kind=kLoop, calls=%fused_computation.18 | loop fusion | flops 10485760 | bytes 12582912 | tf_op jit(solution)/shard_map/broadcast_in_dim | solution.py:102
  114.5 0.4 collective-permute-start.13
  114.9 2.2 %collective-permute-start.14 = (bf16[16,8192]{1,0:T(8,128)(2,1)S(1)}, bf16[16,8192]{1,0:T(8,128)(2,1)S(1)}, u32[]{:S(2)}, u32[]{:S(2)}) collective-permute-start(bf16[16,8192]{1,0:T(8,128)(2,1)S(1)} %get-tuple-element.7), channel_id=1, source_target_pairs={{0,96},{1,97},{2,98},{3,99},{4,100},{5,101},{6,102},{7,103},{8,104... | collective-permute-start | bytes 786440 | tf_op jit(solution)/shard_map/ppermute | solution.py:26
  117.2 0.0 collective-permute-done.12
  117.2 5.9 %collective-permute-done.13 = bf16[16,8192]{1,0:T(8,128)(2,1)S(1)} collective-permute-done((bf16[16,8192]{1,0:T(8,128)(2,1)S(1)}, bf16[16,8192]{1,0:T(8,128)(2,1)S(1)}, u32[]{:S(2)}, u32[]{:S(2)}) %collective-permute-start.13) | collective-permute-done | bytes 262176 | tf_op jit(solution)/shard_map/ppermute | solution.py:26
  123.1 5.6 %collective-permute-done.14 = bf16[16,8192]{1,0:T(8,128)(2,1)S(1)} collective-permute-done((bf16[16,8192]{1,0:T(8,128)(2,1)S(1)}, bf16[16,8192]{1,0:T(8,128)(2,1)S(1)}, u32[]{:S(2)}, u32[]{:S(2)}) %collective-permute-start.14) | collective-permute-done | bytes 262176 | tf_op jit(solution)/shard_map/ppermute | solution.py:26
  128.7 2.2 %collective-permute-start.15 = (bf16[4,16,8192]{2,1,0:T(8,128)(2,1)S(1)}, bf16[4,16,8192]{2,1,0:T(8,128)(2,1)}, u32[]{:S(2)}, u32[]{:S(2)}) collective-permute-start(bf16[4,16,8192]{2,1,0:T(8,128)(2,1)S(1)} %bitcast_dynamic-update-slice_fusion), channel_id=1, source_target_pairs={{0,8},{1,9},{2,10},{3,11},{4,12},{5,13},{6,14},{7,15},{8,0},{9,1},... | collective-permute-start | bytes 3145736 | tf_op jit(solution)/shard_map/ppermute | solution.py:26
  131.0 12.5 %convert_bitcast_fusion = bf16[1,1,1024,1024]{3,2,1,0:T(8,128)(2,1)} fusion(bf16[1,1,1024,1024]{3,2,1,0:T(8,128)(2,1)S(1)} %copy-done, bf16[1,1,1024,1024]{3,2,1,0:T(8,128)(2,1)} %param.15, f32[1024,1024]{1,0:T(8,128)} %fusion.19, bf16[1,1,1024,1024]{3,2,1,0:T(8,128)(2,1)} %param.17, bf16[1,1,1024,1024]{3,2,1,0:T(8,128)(2,1)} %param.18), kind=kOutput, calls=%fused_computation.35 | convolution fusion | flops 4310695936 | bytes 14680064 | tf_op jit(solution)/shard_map/dot_general | solution.py:74
  143.5 0.0 collective-permute-done.15
  143.5 2.2 %convert_multiply_fusion = f32[2,4,16,8192]{3,2,1,0:T(8,128)S(1)} fusion(bf16[1,4,16,8192]{3,2,1,0:T(8,128)(2,1)} %bitcast.44, bf16[1,4,16,8192]{3,2,1,0:T(8,128)(2,1)S(1)} %bitcast.127, pred[]{:T(512)S(6)} %eq.42), kind=kLoop, calls=%fused_computation.13 | loop fusion | flops 5242880 | bytes 6291457 | tf_op jit(solution)/shard_map/div | solution.py:91
  145.7 0.6 copy-done.2
  146.3 7.1 %fusion.6 = (f32[128,8192]{1,0:T(8,128)}, f32[128,8192]{1,0:T(8,128)}) fusion(f32[128,8192]{1,0:T(8,128)} %param.20, f32[2,4,16,8192]{3,2,1,0:T(8,128)S(1)} %convert_multiply_fusion, pred[128]{0:T(512)(128)(4,1)S(1)} %broadcast_compare_fusion, f32[128,8192]{1,0:T(8,128)S(1)} %copy-done.2), kind=kLoop, calls=%fused_computation.12 | loop fusion | flops 8388608 | bytes 20971648 | tf_op jit(solution)/shard_map/jit(_where)/select_n | solution.py:96
  153.4 6.0 %fusion.12 = bf16[1,128,8192]{2,1,0:T(8,128)(2,1)} fusion(bf16[1,128,8192]{2,1,0:T(8,128)(2,1)S(1)} %copy-done.4, bf16[1,128,8192]{2,1,0:T(8,128)(2,1)} %param.22, pred[128]{0:T(512)(128)(4,1)S(1)} %broadcast_compare_fusion, f32[128,8192]{1,0:T(8,128)S(1)} %copy-done.2, f32[128,8192]{1,0:T(8,128)} %param.20, f32[2,4,16,8192]{3,2,1,0:T(8,128)S(1)} %convert_multiply_fusion), kind=kLoop, calls=%fused_computation.20 | loop fusion | flops 12582912 | bytes 18874496 | tf_op jit(solution)/shard_map/broadcast_in_dim | solution.py:105
  (17 shorter events, 0.2 us)
Async XLA Ops:
  0.6 96.9 %copy-start = (bf16[1,1,1024,1024]{3,2,1,0:T(8,128)(2,1)S(1)}, bf16[1,1,1024,1024]{3,2,1,0:T(8,128)(2,1)}, u32[]{:S(2)}) copy-start(bf16[1,1,1024,1024]{3,2,1,0:T(8,128)(2,1)} %param.16) | copy-start | bytes 6291460
  23.0 25.4 %collective-permute-start = (bf16[128,2048]{1,0:T(8,128)(2,1)}, bf16[128,2048]{1,0:T(8,128)(2,1)}, u32[]{:S(2)}, u32[]{:S(2)}) collective-permute-start(bf16[128,2048]{1,0:T(8,128)(2,1)} %pad_maximum_fusion), channel_id=1, source_target_pairs={{0,6},{1,7},{2,4},{3,5},{4,2},{5,3},{6,0},{7,1},{8,14},{9,15},{10,... | collective-permute-start | bytes 1572872 | tf_op jit(solution)/shard_map/ppermute | solution.py:26
  30.7 22.5 %collective-permute-start.1 = (bf16[128,2048]{1,0:T(8,128)(2,1)}, bf16[128,2048]{1,0:T(8,128)(2,1)}, u32[]{:S(2)}, u32[]{:S(2)}) collective-permute-start(bf16[128,2048]{1,0:T(8,128)(2,1)} %pad_maximum_fusion.1), channel_id=1, source_target_pairs={{0,5},{1,6},{2,7},{3,4},{4,1},{5,2},{6,3},{7,0},{8,13},{9,14},{10,... | collective-permute-start | bytes 1572872 | tf_op jit(solution)/shard_map/ppermute | solution.py:26
  32.3 32.9 %collective-permute-start.2 = (bf16[128,2048]{1,0:T(8,128)(2,1)}, bf16[128,2048]{1,0:T(8,128)(2,1)}, u32[]{:S(2)}, u32[]{:S(2)}) collective-permute-start(bf16[128,2048]{1,0:T(8,128)(2,1)} %pad_maximum_fusion.2), channel_id=1, source_target_pairs={{0,7},{1,4},{2,5},{3,6},{4,3},{5,0},{6,1},{7,2},{8,15},{9,12},{10,... | collective-permute-start | bytes 1572872 | tf_op jit(solution)/shard_map/ppermute | solution.py:26
  37.5 31.5 %collective-permute-start.3 = (bf16[128,2048]{1,0:T(8,128)(2,1)}, bf16[128,2048]{1,0:T(8,128)(2,1)}, u32[]{:S(2)}, u32[]{:S(2)}) collective-permute-start(bf16[128,2048]{1,0:T(8,128)(2,1)} %pad_maximum_fusion.3), channel_id=1, source_target_pairs={{0,2},{1,3},{2,0},{3,1},{4,6},{5,7},{6,4},{7,5},{8,10},{9,11},{10,... | collective-permute-start | bytes 1572872 | tf_op jit(solution)/shard_map/ppermute | solution.py:26
  38.3 37.6 %collective-permute-start.4 = (bf16[128,2048]{1,0:T(8,128)(2,1)}, bf16[128,2048]{1,0:T(8,128)(2,1)}, u32[]{:S(2)}, u32[]{:S(2)}) collective-permute-start(bf16[128,2048]{1,0:T(8,128)(2,1)} %pad_maximum_fusion.4), channel_id=1, source_target_pairs={{0,4},{1,5},{2,6},{3,7},{4,0},{5,1},{6,2},{7,3},{8,12},{9,13},{10,... | collective-permute-start | bytes 1572872 | tf_op jit(solution)/shard_map/ppermute | solution.py:26
  43.1 5.1 %copy-start.6 = (s32[128]{0:T(128)S(1)}, s32[128]{0:T(128)}, u32[]{:S(2)}) copy-start(s32[128]{0:T(128)} %param.23) | copy-start | bytes 1540
  48.3 29.0 %copy-start.5 = (bf16[128,1024]{1,0:T(8,128)(2,1)S(1)}, bf16[128,1024]{1,0:T(8,128)(2,1)}, u32[]{:S(2)}) copy-start(bf16[128,1024]{1,0:T(8,128)(2,1)} %get-tuple-element.46) | copy-start | bytes 786436
  48.3 29.1 %copy-start.3 = (bf16[128,8192]{1,0:T(8,128)(2,1)S(1)}, bf16[128,8192]{1,0:T(8,128)(2,1)}, u32[]{:S(2)}) copy-start(bf16[128,8192]{1,0:T(8,128)(2,1)} %fusion) | copy-start | bytes 6291460
  48.4 28.7 %collective-permute-start.5 = (bf16[128,2048]{1,0:T(8,128)(2,1)}, bf16[128,2048]{1,0:T(8,128)(2,1)S(1)}, u32[]{:S(2)}, u32[]{:S(2)}) collective-permute-start(bf16[128,2048]{1,0:T(8,128)(2,1)} %pad_maximum_fusion.5), channel_id=1, source_target_pairs={{0,1},{1,2},{2,3},{3,0},{4,5},{5,6},{6,7},{7,4},{8,9},{9,10},{10,1... | collective-permute-start | bytes 1572872 | tf_op jit(solution)/shard_map/ppermute | solution.py:26
  53.2 24.1 %collective-permute-start.6 = (bf16[128,2048]{1,0:T(8,128)(2,1)}, bf16[128,2048]{1,0:T(8,128)(2,1)S(1)}, u32[]{:S(2)}, u32[]{:S(2)}) collective-permute-start(bf16[128,2048]{1,0:T(8,128)(2,1)} %pad_maximum_fusion.6), channel_id=1, source_target_pairs={{0,3},{1,0},{2,1},{3,2},{4,7},{5,4},{6,5},{7,6},{8,11},{9,8},{10,9... | collective-permute-start | bytes 1572872 | tf_op jit(solution)/shard_map/ppermute | solution.py:26
  65.1 12.3 %collective-permute-start.7 = (bf16[4,16,8192]{2,1,0:T(8,128)(2,1)S(1)}, bf16[4,16,8192]{2,1,0:T(8,128)(2,1)S(1)}, u32[]{:S(2)}, u32[]{:S(2)}) collective-permute-start(bf16[4,16,8192]{2,1,0:T(8,128)(2,1)S(1)} %dynamic-slice_bitcast_fusion), channel_id=1, source_target_pairs={{0,8},{1,9},{2,10},{3,11},{4,12},{5,13},{6,14},{7,15},{8,0},{9,1},... | collective-permute-start | bytes 3145736 | tf_op jit(solution)/shard_map/ppermute | solution.py:26
  77.7 8.1 %collective-permute-start.10 = (bf16[16,8192]{1,0:T(8,128)(2,1)S(1)}, bf16[16,8192]{1,0:T(8,128)(2,1)S(1)}, u32[]{:S(2)}, u32[]{:S(2)}) collective-permute-start(bf16[16,8192]{1,0:T(8,128)(2,1)S(1)} %get-tuple-element.21), channel_id=1, source_target_pairs={{0,96},{1,97},{2,98},{3,99},{4,100},{5,101},{6,102},{7,103},{8,104... | collective-permute-start | bytes 786440 | tf_op jit(solution)/shard_map/ppermute | solution.py:26
  80.6 7.7 %collective-permute-start.9 = (bf16[16,8192]{1,0:T(8,128)(2,1)S(1)}, bf16[16,8192]{1,0:T(8,128)(2,1)S(1)}, u32[]{:S(2)}, u32[]{:S(2)}) collective-permute-start(bf16[16,8192]{1,0:T(8,128)(2,1)S(1)} %get-tuple-element.22), channel_id=1, source_target_pairs={{0,64},{1,65},{2,66},{3,67},{4,68},{5,69},{6,70},{7,71},{8,72},{9,... | collective-permute-start | bytes 786440 | tf_op jit(solution)/shard_map/ppermute | solution.py:26
  80.9 15.0 %collective-permute-start.8 = (bf16[16,8192]{1,0:T(8,128)(2,1)S(1)}, bf16[16,8192]{1,0:T(8,128)(2,1)S(1)}, u32[]{:S(2)}, u32[]{:S(2)}) collective-permute-start(bf16[16,8192]{1,0:T(8,128)(2,1)S(1)} %get-tuple-element.20), channel_id=1, source_target_pairs={{0,32},{1,33},{2,34},{3,35},{4,36},{5,37},{6,38},{7,39},{8,40},{9,... | collective-permute-start | bytes 786440 | tf_op jit(solution)/shard_map/ppermute | solution.py:26
  96.0 10.4 %collective-permute-start.11 = (bf16[16,8192]{1,0:T(8,128)(2,1)S(1)}, bf16[16,8192]{1,0:T(8,128)(2,1)}, u32[]{:S(2)}, u32[]{:S(2)}) collective-permute-start(bf16[16,8192]{1,0:T(8,128)(2,1)S(1)} %fusion.46), channel_id=1, source_target_pairs={{0,16},{1,17},{2,18},{3,19},{4,20},{5,21},{6,22},{7,23},{8,24},{9,... | collective-permute-start | bytes 786440 | tf_op jit(solution)/shard_map/ppermute | solution.py:26
  107.5 9.7 %collective-permute-start.12 = (bf16[16,8192]{1,0:T(8,128)(2,1)S(1)}, bf16[16,8192]{1,0:T(8,128)(2,1)S(1)}, u32[]{:S(2)}, u32[]{:S(2)}) collective-permute-start(bf16[16,8192]{1,0:T(8,128)(2,1)S(1)} %get-tuple-element.7), channel_id=1, source_target_pairs={{0,32},{1,33},{2,34},{3,35},{4,36},{5,37},{6,38},{7,39},{8,40},{9,... | collective-permute-start | bytes 786440 | tf_op jit(solution)/shard_map/ppermute | solution.py:26
  114.5 8.6 %collective-permute-start.13 = (bf16[16,8192]{1,0:T(8,128)(2,1)S(1)}, bf16[16,8192]{1,0:T(8,128)(2,1)S(1)}, u32[]{:S(2)}, u32[]{:S(2)}) collective-permute-start(bf16[16,8192]{1,0:T(8,128)(2,1)S(1)} %get-tuple-element.7), channel_id=1, source_target_pairs={{0,64},{1,65},{2,66},{3,67},{4,68},{5,69},{6,70},{7,71},{8,72},{9,... | collective-permute-start | bytes 786440 | tf_op jit(solution)/shard_map/ppermute | solution.py:26
  114.9 13.8 %collective-permute-start.14 = (bf16[16,8192]{1,0:T(8,128)(2,1)S(1)}, bf16[16,8192]{1,0:T(8,128)(2,1)S(1)}, u32[]{:S(2)}, u32[]{:S(2)}) collective-permute-start(bf16[16,8192]{1,0:T(8,128)(2,1)S(1)} %get-tuple-element.7), channel_id=1, source_target_pairs={{0,96},{1,97},{2,98},{3,99},{4,100},{5,101},{6,102},{7,103},{8,104... | collective-permute-start | bytes 786440 | tf_op jit(solution)/shard_map/ppermute | solution.py:26
  128.7 14.8 %collective-permute-start.15 = (bf16[4,16,8192]{2,1,0:T(8,128)(2,1)S(1)}, bf16[4,16,8192]{2,1,0:T(8,128)(2,1)}, u32[]{:S(2)}, u32[]{:S(2)}) collective-permute-start(bf16[4,16,8192]{2,1,0:T(8,128)(2,1)S(1)} %bitcast_dynamic-update-slice_fusion), channel_id=1, source_target_pairs={{0,8},{1,9},{2,10},{3,11},{4,12},{5,13},{6,14},{7,15},{8,0},{9,1},... | collective-permute-start | bytes 3145736 | tf_op jit(solution)/shard_map/ppermute | solution.py:26
  143.5 2.8 %copy-start.2 = (f32[128,8192]{1,0:T(8,128)S(1)}, f32[128,8192]{1,0:T(8,128)}, u32[]{:S(2)}) copy-start(f32[128,8192]{1,0:T(8,128)} %param.19) | copy-start | bytes 12582916
  146.3 7.1 %copy-start.4 = (bf16[1,128,8192]{2,1,0:T(8,128)(2,1)S(1)}, bf16[1,128,8192]{2,1,0:T(8,128)(2,1)}, u32[]{:S(2)}) copy-start(bf16[1,128,8192]{2,1,0:T(8,128)(2,1)} %param.21) | copy-start | bytes 6291460
  153.4 6.1 %copy-start.1 = (bf16[1,1,1024,1024]{3,2,1,0:T(8,128)(2,1)S(1)}, bf16[1,1,1024,1024]{3,2,1,0:T(8,128)(2,1)}, u32[]{:S(2)}) copy-start(bf16[1,1,1024,1024]{3,2,1,0:T(8,128)(2,1)} %param.16) | copy-start | bytes 6291460

commit v2 on v1

v2 whole, which is shorter than its diff:
```python
import functools

import jax
import jax.numpy as jnp
from jax import lax
from jax.experimental import pallas as pl
from jax.experimental.pallas import tpu as pltpu
from jax.sharding import PartitionSpec as P

FW = 14336
BLOCK = 1024
TOK = 128
AXES = ("replica", "fsdp")
SHIFTS = ((1, 2), (1, 1), (1, 3), (0, 2), (1, 0), (0, 1), (0, 3))
EARLY = 5
CORRECT = 1.0 - 0.95**10
F32 = jnp.float32
BF16 = jnp.bfloat16
VM = pl.BlockSpec(memory_space=pltpu.VMEM)
ANY = pl.BlockSpec(memory_space=pl.ANY)


def place(index):
    replica, fsdp = divmod(index, 8)
    return replica // 4, replica // 2 % 2, replica % 2, fsdp // 4, fsdp % 4


def index_of(y, x_lo, core, x_hi, z):
    return ((y % 4 * 2 + x_lo % 2) * 2 + core % 2) * 8 + x_hi % 2 * 4 + z % 4


def moved(array, where):
    return lax.ppermute(array, AXES, [(s, index_of(*where(*place(s)))) for s in range(128)])


def to_owner(array, dx, dz):
    return moved(array, lambda y, x_lo, core, x_hi, z: (y, x_lo, core, x_hi + dx, z + dz))


def to_core(array):
    return moved(array, lambda y, x_lo, core, x_hi, z: (y, x_lo, core + 1, x_hi, z))


def to_x(array):
    return moved(array, lambda y, x_lo, core, x_hi, z: (y, x_lo + 1, core, x_hi, z))


def to_y(array, flips):
    return moved(array, lambda y, x_lo, core, x_hi, z: (y ^ flips[core], x_lo, core, x_hi, z))


def vmem(array):
    return pltpu.with_memory_space_constraint(array, pltpu.VMEM)


def hbm(array):
    return pltpu.with_memory_space_constraint(array, pltpu.HBM)


def pick_kernel(ids, tokens, out_grads, *rest):
    outs, (held, sems, out_sems) = rest[:-3], rest[-3:]
    columns = FW // BLOCK
    me = lax.axis_index("fsdp")
    x_hi, z = me // 4, me % 4
    copies = []
    for i, (dx, dz) in enumerate(SHIFTS + ((0, 0),)):
        owner = (x_hi + dx) % 2 * 4 + (z + dz) % 4
        block = ids[owner]
        row = pl.multiple_of(block // columns * BLOCK, BLOCK)
        col = pl.multiple_of(block % columns * BLOCK, BLOCK)
        for k, (source, at) in enumerate(((tokens, row), (out_grads, col))):
            copy = pltpu.make_async_copy(
                source.at[:, pl.ds(at, BLOCK)], held.at[i, :, pl.ds(k * BLOCK, BLOCK)], sems.at[2 * i + k]
            )
            copy.start()
            copies.append(copy)
    stores = []
    for i, out in enumerate(outs):
        copies[2 * i].wait()
        copies[2 * i + 1].wait()
        store = pltpu.make_async_copy(held.at[i], out, out_sems.at[i])
        store.start()
        stores.append(store)
    for store in stores:
        store.wait()


def pick(block_ids, tokens, out_grads):
    n = len(SHIFTS) + 1
    return pl.pallas_call(
        pick_kernel,
        out_shape=[pltpu.HBM((TOK, 2 * BLOCK), BF16)] * n,
        in_specs=[pl.BlockSpec(memory_space=pltpu.SMEM), ANY, ANY],
        out_specs=[ANY] * n,
        scratch_shapes=[
            pltpu.VMEM((n, TOK, 2 * BLOCK), BF16),
            pltpu.SemaphoreType.DMA((2 * n,)),
            pltpu.SemaphoreType.DMA((n,)),
        ],
        compiler_params=pltpu.CompilerParams(vmem_limit_bytes=6 << 20),
        cost_estimate=pl.CostEstimate(flops=0, bytes_accessed=8 << 20, transcendentals=0),
        name="pick",
    )(block_ids, hbm(tokens), hbm(out_grads))


def rotate(bufs, left, right, yt, zz):
    step = 256

    @pl.loop(0, BLOCK // step)
    def _(j):
        at = pl.ds(pl.multiple_of(j * step, step), step)
        xs = jnp.concatenate([b[:, :BLOCK] for b in bufs], axis=0)
        ds = jnp.concatenate([b[:, BLOCK:] for b in bufs], axis=0)
        yt[at, :] = jnp.dot(xs, left[:, at], preferred_element_type=F32).T.astype(BF16)
        zz[:, at] = jnp.dot(ds, right[:, at], preferred_element_type=F32).astype(BF16)


def early_kernel(n, *refs):
    sources, (left, right, acc, yt, zz, bufs, sems) = refs[:n], refs[n:]
    copies = [pltpu.make_async_copy(source, bufs.at[i], sems.at[i]) for i, source in enumerate(sources)]
    for copy in copies:
        copy.start()
    for copy in copies:
        copy.wait()
    bufs = [bufs.at[i] for i in range(n)]
    rotate(bufs, left, right, yt, zz)

    @pl.loop(0, 4)
    def _(i):
        at = pl.ds(pl.multiple_of(i * 256, 256), 256)
        acc[at, :] = jnp.dot(yt[at, :], zz[...], preferred_element_type=F32)


def early(bufs, left, right):
    n = len(bufs)
    return pl.pallas_call(
        functools.partial(early_kernel, n),
        out_shape=pltpu.VMEM((BLOCK, BLOCK), F32),
        in_specs=[ANY] * n + [VM] * 2,
        out_specs=VM,
        scratch_shapes=[
            pltpu.VMEM((BLOCK, n * TOK), BF16),
            pltpu.VMEM((n * TOK, BLOCK), BF16),
            pltpu.VMEM((n, TOK, 2 * BLOCK), BF16),
            pltpu.SemaphoreType.DMA((n,)),
        ],
        compiler_params=pltpu.CompilerParams(vmem_limit_bytes=20 << 20),
        cost_estimate=pl.CostEstimate(flops=6 * n * TOK * BLOCK * BLOCK, bytes_accessed=4 << 20, transcendentals=0),
        name="early",
    )(*[hbm(a) for a in bufs], vmem(left), vmem(right))


def final_kernel(n, *refs):
    bufs = refs[:n]
    acc, left, right, first, second, update, first_next, second_next = refs[n : n + 8]
    yt, zz, direction, m_out, v_out, u_out, sems = refs[n + 8 :]
    rotate(bufs, left, right, yt, zz)
    rows = 64

    def moment_copies(i):
        at = pl.ds(pl.multiple_of(i * rows, rows), rows)
        return (
            pltpu.make_async_copy(m_out.at[at, :], first_next.at[at, :], sems.at[i]),
            pltpu.make_async_copy(v_out.at[at, :], second_next.at[at, :], sems.at[16 + i]),
        )

    @pl.loop(0, BLOCK // rows)
    def _(i):
        at = pl.ds(pl.multiple_of(i * rows, rows), rows)
        rotated = acc[at, :] + jnp.dot(yt[at, :], zz[...], preferred_element_type=F32)
        m = 0.95 * first[at, :].astype(F32) + 0.05 * rotated
        v = 0.95 * second[at, :].astype(F32) + 0.05 * rotated * rotated
        m_out[at, :] = m.astype(BF16)
        v_out[at, :] = v.astype(BF16)
        scaled = v * (1.0 / CORRECT)
        root = scaled * lax.rsqrt(scaled) + 1e-08
        direction[at, :] = (m * (1.0 / CORRECT) * pl.reciprocal(root, approx=True)).astype(BF16)
        for copy in moment_copies(i):
            copy.start()

    def update_copy(i):
        at = pl.ds(pl.multiple_of(i * 256, 256), 256)
        return pltpu.make_async_copy(u_out.at[at, :], update.at[at, :], sems.at[32 + i])

    @pl.loop(0, 4)
    def _(i):
        at = pl.ds(pl.multiple_of(i * 256, 256), 256)
        back = jnp.dot(left[at, :], direction[...], preferred_element_type=F32).astype(BF16)
        u_out[at, :] = lax.dot_general(
            back, right[...], (((1,), (1,)), ((), ())), preferred_element_type=F32
        ).astype(BF16)
        update_copy(i).start()

    @pl.loop(0, BLOCK // rows)
    def _(i):
        for copy in moment_copies(i):
            copy.wait()

    @pl.loop(0, 4)
    def _(i):
        update_copy(i).wait()


def final(bufs, acc, left, right, first, second):
    n = len(bufs)
    square = jax.ShapeDtypeStruct((BLOCK, BLOCK), BF16)
    block = pltpu.VMEM((BLOCK, BLOCK), BF16)
    return pl.pallas_call(
        functools.partial(final_kernel, n),
        out_shape=[square] * 3,
        in_specs=[VM] * (n + 5),
        out_specs=[ANY] * 3,
        scratch_shapes=[
            pltpu.VMEM((BLOCK, n * TOK), BF16),
            pltpu.VMEM((n * TOK, BLOCK), BF16),
            block,
            block,
            block,
            block,
            pltpu.SemaphoreType.DMA((36,)),
        ],
        compiler_params=pltpu.CompilerParams(vmem_limit_bytes=20 << 20),
        cost_estimate=pl.CostEstimate(
            flops=(6 * n * TOK + 4 * BLOCK) * BLOCK * BLOCK, bytes_accessed=6 << 20, transcendentals=2 << 20
        ),
        name="final",
    )(*[vmem(a) for a in bufs], *[vmem(a) for a in (acc, left, right, first, second)])


def outer_kernel(core, mine, other, params, momentum, snap, local, due, params_next, momentum_next, local_next):
    own = (pl.program_id(0) // 4 == core[0]).astype(F32)
    total = own * mine[...].astype(F32) + (1.0 - own) * other[...].astype(F32)
    pseudo = total * (1.0 / 16)
    old, old_momentum = params[...], momentum[...]
    moment = 0.9 * old_momentum + pseudo
    stepped = old - 0.7 * (pseudo + 0.9 * moment)
    on = jnp.broadcast_to(due[:, :1], old.shape) == 1
    params_next[...] = jnp.where(on, stepped, old)
    momentum_next[...] = jnp.where(on, moment, old_momentum)
    kept = local[...].astype(F32)
    local_next[...] = jnp.where(on, stepped + (kept - snap[...].astype(F32)), kept).astype(BF16)


def outer(core, mine, other, params, momentum, snap, local, due):
    width = params.shape[1]
    whole = pl.BlockSpec((16, width), lambda i, c: (i, 0))
    part = pl.BlockSpec((16, width), lambda i, c: (i % 4, 0))
    return pl.pallas_call(
        outer_kernel,
        out_shape=[
            jax.ShapeDtypeStruct(params.shape, F32),
            jax.ShapeDtypeStruct(params.shape, F32),
            jax.ShapeDtypeStruct(params.shape, BF16),
        ],
        grid_spec=pltpu.PrefetchScalarGridSpec(
            num_scalar_prefetch=1,
            grid=(8,),
            in_specs=[part, part, whole, whole, whole, whole, pl.BlockSpec((16, 128), lambda i, c: (i, 0))],
            out_specs=[whole, whole, whole],
        ),
        compiler_params=pltpu.CompilerParams(vmem_limit_bytes=16 << 20),
        cost_estimate=pl.CostEstimate(flops=10 << 20, bytes_accessed=26 << 20, transcendentals=0),
        name="outer",
    )(core, mine, other, params, momentum, snap, local, due)


def after(array, others):
    return lax.optimization_barrier((array, *others))[0]


def added(one, two):
    return (one.astype(F32) + two.astype(F32)).astype(BF16)


def joined(mine, other, at):
    return lax.select(at == 0, jnp.concatenate([mine, other]), jnp.concatenate([other, mine]))


def per_device(
    tokens,
    out_grads,
    block_ids,
    left_basis,
    right_basis,
    first_moment,
    second_moment,
    outer_params,
    outer_momentum,
    snapshot,
    local_params,
    due_rows,
):
    replica = lax.axis_index("replica")
    y, core = replica // 4, replica % 2
    low, high = y % 2, y // 2
    at_a = jnp.where(core == 0, low ^ high, high)
    at_b = jnp.where(core == 0, high, low)

    def part(array, at):
        size = array.shape[0] // 2
        return lax.dynamic_slice_in_dim(array, at * size, size, 0)

    sends = pick(block_ids, tokens, out_grads)
    got = [to_owner(a, dx, dz) for a, (dx, dz) in zip(sends, SHIFTS)]
    left, right = left_basis[0, 0], right_basis[0, 0]

    def difference(half):
        at = half * 64
        params = lax.dynamic_slice_in_dim(outer_params, at, 64, 0)
        return (params - lax.dynamic_slice_in_dim(snapshot[0], at, 64, 0).astype(F32)).astype(BF16)

    def along_y(pair):
        quad = added(part(pair, at_a), to_y(part(pair, 1 - at_a), (1, 3)))
        return added(part(quad, at_b), to_y(part(quad, 1 - at_b), (3, 1)))

    def along_x(octet):
        total = added(octet, to_x(octet))
        return joined(total, to_y(total, (3, 1)), at_b)

    def nothing(rows):
        return lambda array: jnp.zeros((rows, array.shape[1]), BF16)

    always = replica >= 0
    pair = added(difference(core), to_core(difference(1 - core)))
    octet = lax.cond(always, along_y, nothing(16), after(pair, sends))
    rows = lax.cond(always, along_x, nothing(32), after(octet, got[:2]))
    rows = after(rows, got[2:4])
    rows = joined(rows, to_y(rows, (1, 3)), at_a)
    other = to_core(rows)
    due = jnp.broadcast_to(due_rows[:, None], (due_rows.shape[0], 128))
    outer_next, momentum_next, local_next = outer(
        core[None], rows, other, outer_params, outer_momentum, snapshot[0], local_params[0], due
    )

    acc = early([sends[-1]] + got[:EARLY], left, right)
    update, first_next, second_next = final(
        got[EARLY:], acc, left, right, first_moment[0, 0], second_moment[0, 0]
    )
    return (
        update[None, None],
        first_next[None, None],
        second_next[None, None],
        outer_next,
        momentum_next,
        local_next[None],
    )


def solution(mesh):
    return jax.shard_map(
        per_device,
        mesh=mesh,
        in_specs=(
            P(("replica", "fsdp"), None),
            P(("replica", "fsdp"), None),
            P(),
            P("replica", "fsdp", None, None),
            P("replica", "fsdp", None, None),
            P("replica", "fsdp", None, None),
            P("replica", "fsdp", None, None),
            P("fsdp", None),
            P("fsdp", None),
            P("replica", "fsdp", None),
            P("replica", "fsdp", None),
            P("fsdp"),
        ),
        out_specs=(
            P("replica", "fsdp", None, None),
            P("replica", "fsdp", None, None),
            P("replica", "fsdp", None, None),
            P("fsdp", None),
            P("fsdp", None),
            P("replica", "fsdp", None),
        ),
        check_vma=False,
    )
```

time: 160 us -> 113 us (0.71)
  Pallas kernels: 0 us -> 32.4 us
  other arithmetic: 36.2 us -> 9.18 us
  matrix products: 25.1 us -> 0 us
  between operations: 17 us -> 0.84 us
  local copies, waits for them, and re-layouts: 13.1 us -> 3.39 us
  waiting for transfers between devices: 41.8 us -> 38.8 us
    pallas_call x0 -> x4, Pallas kernels: none -> 32.4 us  [the longest x1 13.2 us: final(): pl.pallas_call(functools.partial(final_kernel, n), out_shape=[square] * 3...]
    dot_general x3 -> x0, matrix products: 25.1 us -> none  [the longest x1 12.5 us: per_device(): lax.dot_general(back, right, (((1,), (1,)), ((), ())), preferred_element_...]
    broadcast_in_dim x2 -> x0, other arithmetic: 13 us -> none  [the longest x1 6.93 us: per_device(): moment_two.astype(jnp.bfloat16)[None, None]]
    concatenate x8 -> x0, other arithmetic: 7.94 us -> none  [the longest x7 7.9 us: factors(): return jnp.concatenate([xcols, dcols], axis=1)]
    dynamic_slice x2, local copies, waits for them, and re-layouts: 5.46 us -> 0.87 us  [part(): return lax.dynamic_slice_in_dim(array, at * size, size, 0)]
    unnamed x21 -> x22, local copies, waits for them, and re-layouts: 6.11 us -> 1.64 us
    select_n x1 -> x2, other arithmetic: 7.1 us -> 2.66 us  [joined(): lax.select(at == 0, jnp.concatenate([mine, other]), jnp.concatenate([othe...]
    ppermute x16 -> x14, waiting for transfers between devices: 41.8 us -> 38.8 us  [moved(): lax.ppermute(array, AXES, [(s, index_of(*where(*place(s)))) for s in rang...]
  transfers between devices with their start and end apart: 16 -> 14, of which waited for: 9 -> 6; matrix products, arithmetic and copies ran while one was open for 32% -> 7% of each run, Pallas kernels for 0% -> 23%
where the time goes in v2:
time: 113 us; the launch traced here: 112 us
  waiting for transfers between devices  38.8 us (34%)
  Pallas kernels  32.4 us (29%)
  starting transfers between devices  27.2 us (24%)
  other arithmetic  9.18 us (8%)
  local copies, waits for them, and re-layouts  3.39 us (3%)
    ppermute x14, waiting for transfers between devices, moved(): lax.ppermute(array, AXES, [(s, index_of(*where(*place(s)))) for s in rang...  38.8 us
    ppermute x14, starting transfers between devices, moved(): lax.ppermute(array, AXES, [(s, index_of(*where(*place(s)))) for s in rang...  27.2 us
    pallas_call x1, Pallas kernels, final(): pl.pallas_call(functools.partial(final_kernel, n), out_shape=[square] * 3...  13.2 us
    pallas_call x1, Pallas kernels, early(): pl.pallas_call(functools.partial(early_kernel, n), out_shape=pltpu.VMEM((...  8.6 us
    pallas_call x1, Pallas kernels, outer(): pl.pallas_call(outer_kernel, out_shape=[jax.ShapeDtypeStruct(params.shape...  6.27 us
    convert_element_type x4, other arithmetic, added(): return (one.astype(F32) + two.astype(F32)).astype(BF16)  4.48 us
    pallas_call x1, Pallas kernels, pick(): pl.pallas_call(pick_kernel, out_shape=[pltpu.HBM((TOK, 2 * BLOCK), BF16)]...  4.31 us
    select_n x2, other arithmetic, joined(): lax.select(at == 0, jnp.concatenate([mine, other]), jnp.concatenate([othe...  2.66 us
  transfers between devices with their start and end apart: 14, of which 6 were waited for; matrix products, arithmetic and copies ran while one was open for 7% of the time, Pallas kernels for 23%

profile of v2, /device:TPU:1, one launch (start us, length us, event | category | flops | bytes accessed | tf_op | source)
XLA Modules:
  0.0 111.9 jit_solution(1929653245945064320)
XLA Ops:
  0.6 0.0 copy-start.4
  0.7 2.0 %fusion = bf16[64,8192]{1,0:T(8,128)(2,1)S(1)} fusion(f32[128,8192]{1,0:T(8,128)} %params.1, s32[]{:T(128)S(6)} %select_n.64, bf16[1,128,8192]{2,1,0:T(8,128)(2,1)} %param.25), kind=kLoop, calls=%fused_computation.7 | loop fusion | flops 1572864 | bytes 4194308 | tf_op jit(solution)/shard_map/convert_element_type | solution.py:310
  2.7 0.0 copy-start.1
  2.7 1.5 %collective-permute-start.11 = (bf16[64,8192]{1,0:T(8,128)(2,1)S(1)}, bf16[64,8192]{1,0:T(8,128)(2,1)}, u32[]{:S(2)}, u32[]{:S(2)}) collective-permute-start(bf16[64,8192]{1,0:T(8,128)(2,1)S(1)} %fusion), channel_id=1, source_target_pairs={{0,8},{1,9},{2,10},{3,11},{4,12},{5,13},{6,14},{7,15},{8,0},{9,1},... | collective-permute-start | bytes 3145736 | tf_op jit(solution)/shard_map/ppermute | solution.py:33
  4.2 0.0 copy-done.4
  4.2 4.3 %pick.1 = (bf16[128,2048]{1,0:T(8,128)(2,1)}, bf16[128,2048]{1,0:T(8,128)(2,1)}, bf16[128,2048]{1,0:T(8,128)(2,1)}, bf16[128,2048]{1,0:T(8,128)(2,1)}, bf16[128,...) custom-call(s32[8]{0:T(128)S(1)} %copy-done.4, ...), custom_call_target="tpu_custom_call" | custom-call | bytes 8388608 | tf_op jit(solution)/shard_map/pick/pallas_call | solution.py:90
  8.5 6.2 %collective-permute-start.6 = (bf16[128,2048]{1,0:T(8,128)(2,1)}, bf16[128,2048]{1,0:T(8,128)(2,1)}, u32[]{:S(2)}, u32[]{:S(2)}) collective-permute-start(bf16[128,2048]{1,0:T(8,128)(2,1)} %get-tuple-element.47), channel_id=1, source_target_pairs={{0,6},{1,7},{2,4},{3,5},{4,2},{5,3},{6,0},{7,1},{8,14},{9,15},{10,... | collective-permute-start | bytes 1572872 | tf_op jit(solution)/shard_map/ppermute | solution.py:33
  14.8 0.7 collective-permute-start.7
  15.4 4.4 %collective-permute-start.8 = (bf16[128,2048]{1,0:T(8,128)(2,1)}, bf16[128,2048]{1,0:T(8,128)(2,1)}, u32[]{:S(2)}, u32[]{:S(2)}) collective-permute-start(bf16[128,2048]{1,0:T(8,128)(2,1)} %get-tuple-element.49), channel_id=1, source_target_pairs={{0,7},{1,4},{2,5},{3,6},{4,3},{5,0},{6,1},{7,2},{8,15},{9,12},{10,... | collective-permute-start | bytes 1572872 | tf_op jit(solution)/shard_map/ppermute | solution.py:33
  19.8 0.0 collective-permute-start.9
  19.8 0.0 collective-permute-done.11
  19.8 0.0 copy-done.1
  19.8 2.2 %add_convert_fusion.3 = bf16[64,8192]{1,0:T(8,128)(2,1)S(1)} fusion(bf16[64,8192]{1,0:T(8,128)(2,1)} %collective-permute-done.11, f32[128,8192]{1,0:T(8,128)} %params.1, s32[]{:T(128)S(6)} %select_n.63, bf16[1,128,8192]{2,1,0:T(8,128)(2,1)S(1)} %copy-done.1), kind=kLoop, calls=%fused_computation.10 | loop fusion | flops 3670016 | bytes 5242884 | tf_op jit(solution)/shard_map/convert_element_type | solution.py:272
  22.1 19.5 %conditional.2 = (bf16[16,8192]{1,0:T(8,128)(2,1)S(1)}) conditional(s32[]{:T(128)} %convert_element_type.58, () %tuple.24, (s32[]{:T(128)}, bf16[64,8192]{1,0:T(8,128)(2,1)S(1)}, s32[]{:T(128)}) %tuple.26), branch_computations={%region_0.1_spmd, %region_1.2_spmd} | conditional | flops 1572882 | bytes 9175380 | solution.py:325
  22.1 0.8 constant_dynamic-slice_fusion.1
  23.0 2.7 %collective-permute-start = (bf16[32,8192]{1,0:T(8,128)(2,1)}, bf16[32,8192]{1,0:T(8,128)(2,1)}, u32[]{:S(2)}, u32[]{:S(2)}) collective-permute-start(bf16[32,8192]{1,0:T(8,128)(2,1)} %constant_dynamic-slice_fusion.1), channel_id=1, source_target_pairs={{0,32},{1,33},{2,34},{3,35},{4,36},{5,37},{6,38},{7,39},{8,104},{9... | collective-permute-start | bytes 1572872 | tf_op jit(solution)/shard_map/cond/branch_1_fun/ppermute | solution.py:33
  25.7 7.2 %collective-permute-done = bf16[32,8192]{1,0:T(8,128)(2,1)} collective-permute-done((bf16[32,8192]{1,0:T(8,128)(2,1)}, bf16[32,8192]{1,0:T(8,128)(2,1)}, u32[]{:S(2)}, u32[]{:S(2)}) %collective-permute-start) | collective-permute-done | bytes 524320 | tf_op jit(solution)/shard_map/cond/branch_1_fun/ppermute | solution.py:33
  32.9 1.2 %add_convert_fusion = bf16[32,8192]{1,0:T(8,128)(2,1)S(1)} fusion(bf16[32,8192]{1,0:T(8,128)(2,1)} %collective-permute-done, bf16[64,8192]{1,0:T(8,128)(2,1)S(1)} %get-tuple-element.13, s32[]{:T(128)S(6)} %select_n.40), kind=kLoop, calls=%fused_computation | loop fusion | flops 1048576 | bytes 1572868 | tf_op jit(solution)/shard_map/cond/branch_1_fun/convert_element_type | solution.py:272
  34.0 0.0 copy-start.10
  34.0 0.8 copy-done.10
  34.9 0.1 collective-permute-start.1
  35.0 5.6 %collective-permute-done.1 = bf16[16,8192]{1,0:T(8,128)(2,1)S(1)} collective-permute-done((bf16[16,8192]{1,0:T(8,128)(2,1)S(1)}, bf16[16,8192]{1,0:T(8,128)(2,1)S(1)}, u32[]{:S(2)}, u32[]{:S(2)}) %collective-permute-start.1) | collective-permute-done | bytes 262176 | tf_op jit(solution)/shard_map/cond/branch_1_fun/ppermute | solution.py:33
  40.6 1.0 add_convert_fusion.1
  41.6 0.0 collective-permute-done.6.refs_1_
  41.6 0.0 collective-permute-done.7.refs_2_
  41.6 20.7 %conditional.3 = (bf16[32,8192]{1,0:T(8,128)(2,1)}) conditional(s32[]{:T(128)} %convert_element_type.58, () %tuple.23, (s32[]{:T(128)}, bf16[16,8192]{1,0:T(8,128)(2,1)S(1)}) %tuple.28), branch_computations={%region_2.3_spmd, %region_3.4_spmd} | conditional | flops 2883585 | bytes 3932258 | solution.py:326
  41.6 0.4 collective-permute-start.2
  42.0 13.8 %collective-permute-done.2 = bf16[16,8192]{1,0:T(8,128)(2,1)S(1)} collective-permute-done((bf16[16,8192]{1,0:T(8,128)(2,1)S(1)}, bf16[16,8192]{1,0:T(8,128)(2,1)S(1)}, u32[]{:S(2)}, u32[]{:S(2)}) %collective-permute-start.2) | collective-permute-done | bytes 262176 | tf_op jit(solution)/shard_map/cond/branch_1_fun/ppermute | solution.py:33
  55.8 0.1 add_convert_fusion.2
  55.8 1.4 %collective-permute-start.3 = (bf16[16,8192]{1,0:T(8,128)(2,1)S(1)}, bf16[16,8192]{1,0:T(8,128)(2,1)S(1)}, u32[]{:S(2)}, u32[]{:S(2)}) collective-permute-start(bf16[16,8192]{1,0:T(8,128)(2,1)S(1)} %add_convert_fusion.2), channel_id=1, source_target_pairs={{0,96},{1,97},{2,98},{3,99},{4,100},{5,101},{6,102},{7,103},{8,40}... | collective-permute-start | bytes 786440 | tf_op jit(solution)/shard_map/cond/branch_1_fun/ppermute | solution.py:33
  57.2 4.2 %collective-permute-done.3 = bf16[16,8192]{1,0:T(8,128)(2,1)S(1)} collective-permute-done((bf16[16,8192]{1,0:T(8,128)(2,1)S(1)}, bf16[16,8192]{1,0:T(8,128)(2,1)S(1)}, u32[]{:S(2)}, u32[]{:S(2)}) %collective-permute-start.3) | collective-permute-done | bytes 262176 | tf_op jit(solution)/shard_map/cond/branch_1_fun/ppermute | solution.py:33
  61.4 0.9 maximum_select_fusion
  62.3 0.0 collective-permute-done.8.refs_3_
  62.3 0.0 collective-permute-done.9.refs_4_
  62.3 2.7 %collective-permute-start.12 = (bf16[32,8192]{1,0:T(8,128)(2,1)}, bf16[32,8192]{1,0:T(8,128)(2,1)}, u32[]{:S(2)}, u32[]{:S(2)}) collective-permute-start(bf16[32,8192]{1,0:T(8,128)(2,1)} %get-tuple-element.62), channel_id=1, source_target_pairs={{0,32},{1,33},{2,34},{3,35},{4,36},{5,37},{6,38},{7,39},{8,104},{9... | collective-permute-start | bytes 1572872 | tf_op jit(solution)/shard_map/ppermute | solution.py:33
  65.1 0.8 collective-permute-start.4
  65.9 1.8 %collective-permute-start.5 = (bf16[128,2048]{1,0:T(8,128)(2,1)}, bf16[128,2048]{1,0:T(8,128)(2,1)S(1)}, u32[]{:S(2)}, u32[]{:S(2)}) collective-permute-start(bf16[128,2048]{1,0:T(8,128)(2,1)} %get-tuple-element.45), channel_id=1, source_target_pairs={{0,3},{1,0},{2,1},{3,2},{4,7},{5,4},{6,5},{7,6},{8,11},{9,8},{10,9... | collective-permute-start | bytes 1572872 | tf_op jit(solution)/shard_map/ppermute | solution.py:33
  67.7 1.7 %collective-permute-start.10 = (bf16[128,2048]{1,0:T(8,128)(2,1)}, bf16[128,2048]{1,0:T(8,128)(2,1)}, u32[]{:S(2)}, u32[]{:S(2)}) collective-permute-start(bf16[128,2048]{1,0:T(8,128)(2,1)} %get-tuple-element.51), channel_id=1, source_target_pairs={{0,4},{1,5},{2,6},{3,7},{4,0},{5,1},{6,2},{7,3},{8,12},{9,13},{10,... | collective-permute-start | bytes 1572872 | tf_op jit(solution)/shard_map/ppermute | solution.py:33
  69.5 0.0 copy-start.5
  69.5 2.7 %collective-permute-done.12 = bf16[32,8192]{1,0:T(8,128)(2,1)} collective-permute-done((bf16[32,8192]{1,0:T(8,128)(2,1)}, bf16[32,8192]{1,0:T(8,128)(2,1)}, u32[]{:S(2)}, u32[]{:S(2)}) %collective-permute-start.12) | collective-permute-done | bytes 524320 | tf_op jit(solution)/shard_map/ppermute | solution.py:33
  72.1 1.8 %maximum_select_fusion.1.mine = bf16[64,8192]{1,0:T(8,128)(2,1)S(1)} fusion(bf16[32,8192]{1,0:T(8,128)(2,1)} %collective-permute-done.12, bf16[32,8192]{1,0:T(8,128)(2,1)} %get-tuple-element.62, pred[]{:T(512)S(6)} %eq.14), kind=kLoop, calls=%fused_computation.11 | loop fusion | flops 4718592 | bytes 2097153 | tf_op jit(solution)/shard_map/select_n | solution.py:276
  73.9 2.7 %collective-permute-start.13 = (bf16[64,8192]{1,0:T(8,128)(2,1)S(1)}, bf16[64,8192]{1,0:T(8,128)(2,1)S(1)}, u32[]{:S(2)}, u32[]{:S(2)}) collective-permute-start(bf16[64,8192]{1,0:T(8,128)(2,1)S(1)} %maximum_select_fusion.1.mine), channel_id=1, source_target_pairs={{0,8},{1,9},{2,10},{3,11},{4,12},{5,13},{6,14},{7,15},{8,0},{9,1},... | collective-permute-start | bytes 3145736 | tf_op jit(solution)/shard_map/ppermute | solution.py:33
  76.6 5.3 %collective-permute-done.10.refs_5_ = bf16[128,2048]{1,0:T(8,128)(2,1)} collective-permute-done((bf16[128,2048]{1,0:T(8,128)(2,1)}, bf16[128,2048]{1,0:T(8,128)(2,1)}, u32[]{:S(2)}, u32[]{:S(2)}) %collective-permute-start.10) | collective-permute-done | bytes 524320 | tf_op jit(solution)/shard_map/ppermute | solution.py:33
  81.9 0.0 copy-done.5
  81.9 0.0 copy-start.6
  81.9 1.6 %copy-done.6 = bf16[1,1,1024,1024]{3,2,1,0:T(8,128)(2,1)S(1)} copy-done((bf16[1,1,1024,1024]{3,2,1,0:T(8,128)(2,1)S(1)}, bf16[1,1,1024,1024]{3,2,1,0:T(8,128)(2,1)}, u32[]{:S(2)}) %copy-start.6) | copy-done | bytes 2097176
  83.5 8.6 %early.1.refs_2_ = f32[1024,1024]{1,0:T(8,128)S(1)} custom-call(bf16[128,2048]{1,0:T(8,128)(2,1)} %get-tuple-element.46.refs_0_, bf16[128,2048]{1,0:T(8,128)(2,1)} %collective-permute-done.6.refs_1_, bf16[128,2048]{1,0:T(8,128)(2,1)} %collective-permute-done.7.refs_2_, bf16[128,2048]{1,0:T(8,128)(2,1)} %collective-permute-done.8.refs_3_, ...), custom_call_target="tpu_custom_call" | custom-call | flops 4831838208 | bytes 4194304 | tf_op jit(solution)/shard_map/early/pallas_call | solution.py:136
  92.1 0.0 collective-permute-done.4.refs_0_
  92.1 0.0 collective-permute-done.5.refs_1_
  92.1 0.0 copy-done.7
  92.1 0.0 copy-done.8
  92.1 0.0 copy-done.9
  92.2 0.0 copy-start.11
  92.2 0.0 copy-start
  92.2 0.0 copy-start.2
  92.2 0.0 copy-start.3
  92.2 13.2 %final.1 = (bf16[1024,1024]{1,0:T(8,128)(2,1)}, bf16[1024,1024]{1,0:T(8,128)(2,1)}, bf16[1024,1024]{1,0:T(8,128)(2,1)}) custom-call(bf16[128,2048]{1,0:T(8,128)(2,1)S(1)} %collective-permute-done.4.refs_0_, bf16[128,2048]{1,0:T(8,128)(2,1)S(1)} %collective-permute-done.5.refs_1_, f32[1024,1024]{1,0:T(8,128)S(1)} %early.1.refs_2_, ...), custom_call_target="tpu_custom_call" | custom-call | flops 5905580032 | bytes 6291456 | tf_op jit(solution)/shard_map/final/pallas_call | solution.py:208
  105.5 0.0 collective-permute-done.13.other
  105.5 0.0 copy-done.11
  105.5 0.1 broadcast_in_dim.25.due
  105.5 0.0 copy-done
  105.6 0.0 copy-done.2
  105.6 0.0 copy-done.3
  105.6 6.3 %outer.1 = (f32[128,8192]{1,0:T(8,128)}, f32[128,8192]{1,0:T(8,128)}, bf16[128,8192]{1,0:T(8,128)(2,1)}) custom-call(s32[1]{0:T(128)} %bitcast.7.core, bf16[64,8192]{1,0:T(8,128)(2,1)S(1)} %maximum_select_fusion.1.mine, bf16[64,8192]{1,0:T(8,128)(2,1)S(1)} %collective-permute-done.13.other, f32[128,8192]{1,0:T(8,128)S(1)} %copy-done, ...), custom_call_target="tpu_custom_call" | custom-call | flops 10485760 | bytes 27262976 | tf_op jit(solution)/shard_map/outer/pallas_call | solution.py:248
  (4 shorter events, 0.0 us)
Async XLA Ops:
  0.6 3.6 %copy-start.4 = (s32[8]{0:T(128)S(1)}, s32[8]{0:T(128)}, u32[]{:S(2)}) copy-start(s32[8]{0:T(128)} %ids.1) | copy-start | bytes 100
  2.7 17.1 %copy-start.1 = (bf16[1,128,8192]{2,1,0:T(8,128)(2,1)S(1)}, bf16[1,128,8192]{2,1,0:T(8,128)(2,1)}, u32[]{:S(2)}) copy-start(bf16[1,128,8192]{2,1,0:T(8,128)(2,1)} %param.25) | copy-start | bytes 6291460
  2.7 17.1 %collective-permute-start.11 = (bf16[64,8192]{1,0:T(8,128)(2,1)S(1)}, bf16[64,8192]{1,0:T(8,128)(2,1)}, u32[]{:S(2)}, u32[]{:S(2)}) collective-permute-start(bf16[64,8192]{1,0:T(8,128)(2,1)S(1)} %fusion), channel_id=1, source_target_pairs={{0,8},{1,9},{2,10},{3,11},{4,12},{5,13},{6,14},{7,15},{8,0},{9,1},... | collective-permute-start | bytes 3145736 | tf_op jit(solution)/shard_map/ppermute | solution.py:33
  8.5 33.0 %collective-permute-start.6 = (bf16[128,2048]{1,0:T(8,128)(2,1)}, bf16[128,2048]{1,0:T(8,128)(2,1)}, u32[]{:S(2)}, u32[]{:S(2)}) collective-permute-start(bf16[128,2048]{1,0:T(8,128)(2,1)} %get-tuple-element.47), channel_id=1, source_target_pairs={{0,6},{1,7},{2,4},{3,5},{4,2},{5,3},{6,0},{7,1},{8,14},{9,15},{10,... | collective-permute-start | bytes 1572872 | tf_op jit(solution)/shard_map/ppermute | solution.py:33
  14.8 26.8 %collective-permute-start.7 = (bf16[128,2048]{1,0:T(8,128)(2,1)}, bf16[128,2048]{1,0:T(8,128)(2,1)}, u32[]{:S(2)}, u32[]{:S(2)}) collective-permute-start(bf16[128,2048]{1,0:T(8,128)(2,1)} %get-tuple-element.48), channel_id=1, source_target_pairs={{0,5},{1,6},{2,7},{3,4},{4,1},{5,2},{6,3},{7,0},{8,13},{9,14},{10,... | collective-permute-start | bytes 1572872 | tf_op jit(solution)/shard_map/ppermute | solution.py:33
  15.4 46.9 %collective-permute-start.8 = (bf16[128,2048]{1,0:T(8,128)(2,1)}, bf16[128,2048]{1,0:T(8,128)(2,1)}, u32[]{:S(2)}, u32[]{:S(2)}) collective-permute-start(bf16[128,2048]{1,0:T(8,128)(2,1)} %get-tuple-element.49), channel_id=1, source_target_pairs={{0,7},{1,4},{2,5},{3,6},{4,3},{5,0},{6,1},{7,2},{8,15},{9,12},{10,... | collective-permute-start | bytes 1572872 | tf_op jit(solution)/shard_map/ppermute | solution.py:33
  19.8 42.5 %collective-permute-start.9 = (bf16[128,2048]{1,0:T(8,128)(2,1)}, bf16[128,2048]{1,0:T(8,128)(2,1)}, u32[]{:S(2)}, u32[]{:S(2)}) collective-permute-start(bf16[128,2048]{1,0:T(8,128)(2,1)} %get-tuple-element.50), channel_id=1, source_target_pairs={{0,2},{1,3},{2,0},{3,1},{4,6},{5,7},{6,4},{7,5},{8,10},{9,11},{10,... | collective-permute-start | bytes 1572872 | tf_op jit(solution)/shard_map/ppermute | solution.py:33
  23.0 9.9 %collective-permute-start = (bf16[32,8192]{1,0:T(8,128)(2,1)}, bf16[32,8192]{1,0:T(8,128)(2,1)}, u32[]{:S(2)}, u32[]{:S(2)}) collective-permute-start(bf16[32,8192]{1,0:T(8,128)(2,1)} %constant_dynamic-slice_fusion.1), channel_id=1, source_target_pairs={{0,32},{1,33},{2,34},{3,35},{4,36},{5,37},{6,38},{7,39},{8,104},{9... | collective-permute-start | bytes 1572872 | tf_op jit(solution)/shard_map/cond/branch_1_fun/ppermute | solution.py:33
  34.0 0.8 copy-start.10
  34.9 5.7 %collective-permute-start.1 = (bf16[16,8192]{1,0:T(8,128)(2,1)S(1)}, bf16[16,8192]{1,0:T(8,128)(2,1)S(1)}, u32[]{:S(2)}, u32[]{:S(2)}) collective-permute-start(bf16[16,8192]{1,0:T(8,128)(2,1)S(1)} %constant_dynamic-slice_fusion), channel_id=1, source_target_pairs={{0,96},{1,97},{2,98},{3,99},{4,100},{5,101},{6,102},{7,103},{8,40}... | collective-permute-start | bytes 786440 | tf_op jit(solution)/shard_map/cond/branch_1_fun/ppermute | solution.py:33
  41.6 14.2 %collective-permute-start.2 = (bf16[16,8192]{1,0:T(8,128)(2,1)S(1)}, bf16[16,8192]{1,0:T(8,128)(2,1)S(1)}, u32[]{:S(2)}, u32[]{:S(2)}) collective-permute-start(bf16[16,8192]{1,0:T(8,128)(2,1)S(1)} %get-tuple-element.20), channel_id=1, source_target_pairs={{0,16},{1,17},{2,18},{3,19},{4,20},{5,21},{6,22},{7,23},{8,24},{9,... | collective-permute-start | bytes 786440 | tf_op jit(solution)/shard_map/cond/branch_1_fun/ppermute | solution.py:33
  55.8 5.6 %collective-permute-start.3 = (bf16[16,8192]{1,0:T(8,128)(2,1)S(1)}, bf16[16,8192]{1,0:T(8,128)(2,1)S(1)}, u32[]{:S(2)}, u32[]{:S(2)}) collective-permute-start(bf16[16,8192]{1,0:T(8,128)(2,1)S(1)} %add_convert_fusion.2), channel_id=1, source_target_pairs={{0,96},{1,97},{2,98},{3,99},{4,100},{5,101},{6,102},{7,103},{8,40}... | collective-permute-start | bytes 786440 | tf_op jit(solution)/shard_map/cond/branch_1_fun/ppermute | solution.py:33
  62.3 9.8 %collective-permute-start.12 = (bf16[32,8192]{1,0:T(8,128)(2,1)}, bf16[32,8192]{1,0:T(8,128)(2,1)}, u32[]{:S(2)}, u32[]{:S(2)}) collective-permute-start(bf16[32,8192]{1,0:T(8,128)(2,1)} %get-tuple-element.62), channel_id=1, source_target_pairs={{0,32},{1,33},{2,34},{3,35},{4,36},{5,37},{6,38},{7,39},{8,104},{9... | collective-permute-start | bytes 1572872 | tf_op jit(solution)/shard_map/ppermute | solution.py:33
  65.1 27.1 %collective-permute-start.4 = (bf16[128,2048]{1,0:T(8,128)(2,1)}, bf16[128,2048]{1,0:T(8,128)(2,1)S(1)}, u32[]{:S(2)}, u32[]{:S(2)}) collective-permute-start(bf16[128,2048]{1,0:T(8,128)(2,1)} %get-tuple-element.44), channel_id=1, source_target_pairs={{0,1},{1,2},{2,3},{3,0},{4,5},{5,6},{6,7},{7,4},{8,9},{9,10},{10,1... | collective-permute-start | bytes 1572872 | tf_op jit(solution)/shard_map/ppermute | solution.py:33
  65.9 26.2 %collective-permute-start.5 = (bf16[128,2048]{1,0:T(8,128)(2,1)}, bf16[128,2048]{1,0:T(8,128)(2,1)S(1)}, u32[]{:S(2)}, u32[]{:S(2)}) collective-permute-start(bf16[128,2048]{1,0:T(8,128)(2,1)} %get-tuple-element.45), channel_id=1, source_target_pairs={{0,3},{1,0},{2,1},{3,2},{4,7},{5,4},{6,5},{7,6},{8,11},{9,8},{10,9... | collective-permute-start | bytes 1572872 | tf_op jit(solution)/shard_map/ppermute | solution.py:33
  67.7 14.2 %collective-permute-start.10 = (bf16[128,2048]{1,0:T(8,128)(2,1)}, bf16[128,2048]{1,0:T(8,128)(2,1)}, u32[]{:S(2)}, u32[]{:S(2)}) collective-permute-start(bf16[128,2048]{1,0:T(8,128)(2,1)} %get-tuple-element.51), channel_id=1, source_target_pairs={{0,4},{1,5},{2,6},{3,7},{4,0},{5,1},{6,2},{7,3},{8,12},{9,13},{10,... | collective-permute-start | bytes 1572872 | tf_op jit(solution)/shard_map/ppermute | solution.py:33
  69.5 12.4 %copy-start.5 = (bf16[1,1,1024,1024]{3,2,1,0:T(8,128)(2,1)S(1)}, bf16[1,1,1024,1024]{3,2,1,0:T(8,128)(2,1)}, u32[]{:S(2)}) copy-start(bf16[1,1,1024,1024]{3,2,1,0:T(8,128)(2,1)} %param.19) | copy-start | bytes 6291460
  73.9 31.5 %collective-permute-start.13 = (bf16[64,8192]{1,0:T(8,128)(2,1)S(1)}, bf16[64,8192]{1,0:T(8,128)(2,1)S(1)}, u32[]{:S(2)}, u32[]{:S(2)}) collective-permute-start(bf16[64,8192]{1,0:T(8,128)(2,1)S(1)} %maximum_select_fusion.1.mine), channel_id=1, source_target_pairs={{0,8},{1,9},{2,10},{3,11},{4,12},{5,13},{6,14},{7,15},{8,0},{9,1},... | collective-permute-start | bytes 3145736 | tf_op jit(solution)/shard_map/ppermute | solution.py:33
  81.9 1.6 %copy-start.6 = (bf16[1,1,1024,1024]{3,2,1,0:T(8,128)(2,1)S(1)}, bf16[1,1,1024,1024]{3,2,1,0:T(8,128)(2,1)}, u32[]{:S(2)}) copy-start(bf16[1,1,1024,1024]{3,2,1,0:T(8,128)(2,1)} %param.20) | copy-start | bytes 6291460
  83.5 8.6 %copy-start.7 = (bf16[1,1,1024,1024]{3,2,1,0:T(8,128)(2,1)S(1)}, bf16[1,1,1024,1024]{3,2,1,0:T(8,128)(2,1)}, u32[]{:S(2)}) copy-start(bf16[1,1,1024,1024]{3,2,1,0:T(8,128)(2,1)} %param.20) | copy-start | bytes 6291460
  83.5 8.6 %copy-start.8 = (bf16[1,1,1024,1024]{3,2,1,0:T(8,128)(2,1)S(1)}, bf16[1,1,1024,1024]{3,2,1,0:T(8,128)(2,1)}, u32[]{:S(2)}) copy-start(bf16[1,1,1024,1024]{3,2,1,0:T(8,128)(2,1)} %param.21) | copy-start | bytes 6291460
  83.5 8.7 %copy-start.9 = (bf16[1,1,1024,1024]{3,2,1,0:T(8,128)(2,1)S(1)}, bf16[1,1,1024,1024]{3,2,1,0:T(8,128)(2,1)}, u32[]{:S(2)}) copy-start(bf16[1,1,1024,1024]{3,2,1,0:T(8,128)(2,1)} %param.22) | copy-start | bytes 6291460
  92.2 13.3 %copy-start.11 = (s32[128]{0:T(128)S(1)}, s32[128]{0:T(128)}, u32[]{:S(2)}) copy-start(s32[128]{0:T(128)} %param.27) | copy-start | bytes 1540
  92.2 13.4 %copy-start = (f32[128,8192]{1,0:T(8,128)S(1)}, f32[128,8192]{1,0:T(8,128)}, u32[]{:S(2)}) copy-start(f32[128,8192]{1,0:T(8,128)} %params.1) | copy-start | bytes 12582916
  92.2 13.4 %copy-start.2 = (f32[128,8192]{1,0:T(8,128)S(1)}, f32[128,8192]{1,0:T(8,128)}, u32[]{:S(2)}) copy-start(f32[128,8192]{1,0:T(8,128)} %momentum.1) | copy-start | bytes 12582916
  92.2 13.4 %copy-start.3 = (bf16[1,128,8192]{2,1,0:T(8,128)(2,1)S(1)}, bf16[1,128,8192]{2,1,0:T(8,128)(2,1)}, u32[]{:S(2)}) copy-start(bf16[1,128,8192]{2,1,0:T(8,128)(2,1)} %param.26) | copy-start | bytes 6291460

commit v3 on v2

--- a/solution.py
+++ b/solution.py
@@ -11,8 +11,8 @@
 BLOCK = 1024
 TOK = 128
 AXES = ("replica", "fsdp")
-SHIFTS = ((1, 2), (1, 1), (1, 3), (0, 2), (1, 0), (0, 1), (0, 3))
-EARLY = 5
+SHIFTS = ((1, 2), (1, 1), (1, 3), (0, 2), (0, 1), (0, 3), (1, 0))
+FIRST = 4
 CORRECT = 1.0 - 0.95**10
 F32 = jnp.float32
 BF16 = jnp.bfloat16
@@ -57,13 +57,13 @@
     return pltpu.with_memory_space_constraint(array, pltpu.HBM)
 
 
-def pick_kernel(ids, tokens, out_grads, *rest):
+def pick_kernel(shifts, ids, tokens, out_grads, *rest):
     outs, (held, sems, out_sems) = rest[:-3], rest[-3:]
     columns = FW // BLOCK
     me = lax.axis_index("fsdp")
     x_hi, z = me // 4, me % 4
     copies = []
-    for i, (dx, dz) in enumerate(SHIFTS + ((0, 0),)):
+    for i, (dx, dz) in enumerate(shifts):
         owner = (x_hi + dx) % 2 * 4 + (z + dz) % 4
         block = ids[owner]
         row = pl.multiple_of(block // columns * BLOCK, BLOCK)
@@ -85,10 +85,10 @@
         store.wait()
 
 
-def pick(block_ids, tokens, out_grads):
-    n = len(SHIFTS) + 1
+def pick(block_ids, tokens, out_grads, shifts):
+    n = len(shifts)
     return pl.pallas_call(
-        pick_kernel,
+        functools.partial(pick_kernel, shifts),
         out_shape=[pltpu.HBM((TOK, 2 * BLOCK), BF16)] * n,
         in_specs=[pl.BlockSpec(memory_space=pltpu.SMEM), ANY, ANY],
         out_specs=[ANY] * n,
@@ -115,72 +115,101 @@
         zz[:, at] = jnp.dot(ds, right[:, at], preferred_element_type=F32).astype(BF16)
 
 
-def early_kernel(n, *refs):
-    sources, (left, right, acc, yt, zz, bufs, sems) = refs[:n], refs[n:]
-    copies = [pltpu.make_async_copy(source, bufs.at[i], sems.at[i]) for i, source in enumerate(sources)]
+def early_kernel(n, more, *refs):
+    sources, (left_in, right_in), refs = refs[:n], refs[n : n + 2], refs[n + 2 :]
+    acc_in, refs = (refs[0], refs[1:]) if more else (None, refs)
+    acc_out, yt, zz, held, left, right, acc, sems = refs
+    copies = [pltpu.make_async_copy(source, held.at[i], sems.at[i]) for i, source in enumerate(sources)]
+    copies.append(pltpu.make_async_copy(left_in, left, sems.at[n]))
+    copies.append(pltpu.make_async_copy(right_in, right, sems.at[n + 1]))
+    if more:
+        copies.append(pltpu.make_async_copy(acc_in, acc, sems.at[n + 2]))
     for copy in copies:
         copy.start()
-    for copy in copies:
+    for copy in copies[: n + 2]:
         copy.wait()
-    bufs = [bufs.at[i] for i in range(n)]
-    rotate(bufs, left, right, yt, zz)
+    rotate([held.at[i] for i in range(n)], left, right, yt, zz)
+    if more:
+        copies[-1].wait()
+
+    def store(i):
+        at = pl.ds(pl.multiple_of(i * 256, 256), 256)
+        return pltpu.make_async_copy(acc.at[at, :], acc_out.at[at, :], sems.at[n + 3 + i])
 
     @pl.loop(0, 4)
     def _(i):
         at = pl.ds(pl.multiple_of(i * 256, 256), 256)
-        acc[at, :] = jnp.dot(yt[at, :], zz[...], preferred_element_type=F32)
-
-
-def early(bufs, left, right):
+        term = jnp.dot(yt[at, :], zz[...], preferred_element_type=F32)
+        acc[at, :] = acc[at, :] + term if more else term
+        store(i).start()
+
+    @pl.loop(0, 4)
+    def _(i):
+        store(i).wait()
+
+
+def early(bufs, left, right, acc=()):
     n = len(bufs)
+    block = pltpu.VMEM((BLOCK, BLOCK), BF16)
     return pl.pallas_call(
-        functools.partial(early_kernel, n),
-        out_shape=pltpu.VMEM((BLOCK, BLOCK), F32),
-        in_specs=[ANY] * n + [VM] * 2,
-        out_specs=VM,
+        functools.partial(early_kernel, n, len(acc)),
+        out_shape=pltpu.HBM((BLOCK, BLOCK), F32),
+        in_specs=[ANY] * (n + 2 + len(acc)),
+        out_specs=ANY,
         scratch_shapes=[
             pltpu.VMEM((BLOCK, n * TOK), BF16),
             pltpu.VMEM((n * TOK, BLOCK), BF16),
             pltpu.VMEM((n, TOK, 2 * BLOCK), BF16),
-            pltpu.SemaphoreType.DMA((n,)),
+            block,
+            block,
+            pltpu.VMEM((BLOCK, BLOCK), F32),
+            pltpu.SemaphoreType.DMA((n + 7,)),
         ],
         compiler_params=pltpu.CompilerParams(vmem_limit_bytes=20 << 20),
         cost_estimate=pl.CostEstimate(flops=6 * n * TOK * BLOCK * BLOCK, bytes_accessed=4 << 20, transcendentals=0),
         name="early",
-    )(*[hbm(a) for a in bufs], vmem(left), vmem(right))
+    )(*[hbm(a) for a in (*bufs, left, right, *acc)])
 
 
 def final_kernel(n, *refs):
-    bufs = refs[:n]
-    acc, left, right, first, second, update, first_next, second_next = refs[n : n + 8]
-    yt, zz, direction, m_out, v_out, u_out, sems = refs[n + 8 :]
-    rotate(bufs, left, right, yt, zz)
-    rows = 64
+    operands, (update, first_next, second_next) = refs[: n + 5], refs[n + 5 : n + 8]
+    held, yt, zz, direction, m_out, v_out, u_out, left, right, acc, first, second, sems, in_sems = refs[n + 8 :]
+    places = [held.at[i] for i in range(n)] + [left, right, acc, first, second]
+    loads = [pltpu.make_async_copy(a, b, in_sems.at[i]) for i, (a, b) in enumerate(zip(operands, places))]
+    for load in loads:
+        load.start()
+    for load in loads[: n + 2]:
+        load.wait()
+    rotate(places[:n], left, right, yt, zz)
+    for load in loads[n + 2 :]:
+        load.wait()
+    rows = 256
 
     def moment_copies(i):
         at = pl.ds(pl.multiple_of(i * rows, rows), rows)
         return (
             pltpu.make_async_copy(m_out.at[at, :], first_next.at[at, :], sems.at[i]),
-            pltpu.make_async_copy(v_out.at[at, :], second_next.at[at, :], sems.at[16 + i]),
+            pltpu.make_async_copy(v_out.at[at, :], second_next.at[at, :], sems.at[4 + i]),
         )
 
     @pl.loop(0, BLOCK // rows)
     def _(i):
         at = pl.ds(pl.multiple_of(i * rows, rows), rows)
         rotated = acc[at, :] + jnp.dot(yt[at, :], zz[...], preferred_element_type=F32)
-        m = 0.95 * first[at, :].astype(F32) + 0.05 * rotated
-        v = 0.95 * second[at, :].astype(F32) + 0.05 * rotated * rotated
+        share = 0.05 * rotated
+        m = 0.95 * first[at, :].astype(F32) + share
+        v = 0.95 * second[at, :].astype(F32) + share * rotated
         m_out[at, :] = m.astype(BF16)
         v_out[at, :] = v.astype(BF16)
-        scaled = v * (1.0 / CORRECT)
-        root = scaled * lax.rsqrt(scaled) + 1e-08
-        direction[at, :] = (m * (1.0 / CORRECT) * pl.reciprocal(root, approx=True)).astype(BF16)
+        scaled = v * CORRECT
+        root = scaled * lax.rsqrt(scaled) + CORRECT * 1e-08
+        direction[at, :] = (m * pltpu.reciprocal(root, approx=True)).astype(BF16)
         for copy in moment_copies(i):
             copy.start()
 
     def update_copy(i):
         at = pl.ds(pl.multiple_of(i * 256, 256), 256)
-        return pltpu.make_async_copy(u_out.at[at, :], update.at[at, :], sems.at[32 + i])
+        return pltpu.make_async_copy(u_out.at[at, :], update.at[at, :], sems.at[8 + i])
 
     @pl.loop(0, 4)
     def _(i):
@@ -208,29 +237,29 @@
     return pl.pallas_call(
         functools.partial(final_kernel, n),
         out_shape=[square] * 3,
-        in_specs=[VM] * (n + 5),
+        in_specs=[ANY] * (n + 5),
         out_specs=[ANY] * 3,
         scratch_shapes=[
+            pltpu.VMEM((n, TOK, 2 * BLOCK), BF16),
             pltpu.VMEM((BLOCK, n * TOK), BF16),
             pltpu.VMEM((n * TOK, BLOCK), BF16),
-            block,
-            block,
-            block,
-            block,
-            pltpu.SemaphoreType.DMA((36,)),
+            *[block] * 6,
+            pltpu.VMEM((BLOCK, BLOCK), F32),
+            *[block] * 2,
+            pltpu.SemaphoreType.DMA((12,)),
+            pltpu.SemaphoreType.DMA((n + 5,)),
         ],
-        compiler_params=pltpu.CompilerParams(vmem_limit_bytes=20 << 20),
+        compiler_params=pltpu.CompilerParams(vmem_limit_bytes=28 << 20),
         cost_estimate=pl.CostEstimate(
             flops=(6 * n * TOK + 4 * BLOCK) * BLOCK * BLOCK, bytes_accessed=6 << 20, transcendentals=2 << 20
         ),
         name="final",
-    )(*[vmem(a) for a in bufs], *[vmem(a) for a in (acc, left, right, first, second)])
-
-
-def outer_kernel(core, mine, other, params, momentum, snap, local, due, params_next, momentum_next, local_next):
-    own = (pl.program_id(0) // 4 == core[0]).astype(F32)
-    total = own * mine[...].astype(F32) + (1.0 - own) * other[...].astype(F32)
-    pseudo = total * (1.0 / 16)
+    )(*[hbm(a) for a in (*bufs, left, right, acc, first, second)])
+
+
+def outer_kernel(half, total, params, momentum, snap, local, due, *rest):
+    params_next, momentum_next, local_next = rest[-3:]
+    pseudo = total[...].astype(F32) * (1.0 / 16)
     old, old_momentum = params[...], momentum[...]
     moment = 0.9 * old_momentum + pseudo
     stepped = old - 0.7 * (pseudo + 0.9 * moment)
@@ -241,27 +270,29 @@
     local_next[...] = jnp.where(on, stepped + (kept - snap[...].astype(F32)), kept).astype(BF16)
 
 
-def outer(core, mine, other, params, momentum, snap, local, due):
+def outer(half, total, params, momentum, snap, local, due, into=()):
     width = params.shape[1]
-    whole = pl.BlockSpec((16, width), lambda i, c: (i, 0))
-    part = pl.BlockSpec((16, width), lambda i, c: (i % 4, 0))
+    whole = pl.BlockSpec((16, width), lambda i, h: (h[0] * 4 + i, 0))
+    part = pl.BlockSpec((16, width), lambda i, h: (i, 0))
     return pl.pallas_call(
         outer_kernel,
         out_shape=[
-            jax.ShapeDtypeStruct(params.shape, F32),
-            jax.ShapeDtypeStruct(params.shape, F32),
-            jax.ShapeDtypeStruct(params.shape, BF16),
+            pltpu.HBM(params.shape, F32),
+            pltpu.HBM(params.shape, F32),
+            pltpu.HBM(params.shape, BF16),
         ],
         grid_spec=pltpu.PrefetchScalarGridSpec(
             num_scalar_prefetch=1,
-            grid=(8,),
-            in_specs=[part, part, whole, whole, whole, whole, pl.BlockSpec((16, 128), lambda i, c: (i, 0))],
+            grid=(4,),
+            in_specs=[part, whole, whole, whole, whole, pl.BlockSpec((16, 128), lambda i, h: (h[0] * 4 + i, 0))]
+            + [ANY] * len(into),
             out_specs=[whole, whole, whole],
         ),
+        input_output_aliases={7 + i: i for i in range(len(into))},
         compiler_params=pltpu.CompilerParams(vmem_limit_bytes=16 << 20),
-        cost_estimate=pl.CostEstimate(flops=10 << 20, bytes_accessed=26 << 20, transcendentals=0),
+        cost_estimate=pl.CostEstimate(flops=5 << 20, bytes_accessed=12 << 20, transcendentals=0),
         name="outer",
-    )(core, mine, other, params, momentum, snap, local, due)
+    )(half[None], total, params, momentum, snap, local, due, *into)
 
 
 def after(array, others):
@@ -300,42 +331,49 @@
         size = array.shape[0] // 2
         return lax.dynamic_slice_in_dim(array, at * size, size, 0)
 
-    sends = pick(block_ids, tokens, out_grads)
-    got = [to_owner(a, dx, dz) for a, (dx, dz) in zip(sends, SHIFTS)]
-    left, right = left_basis[0, 0], right_basis[0, 0]
-
     def difference(half):
         at = half * 64
         params = lax.dynamic_slice_in_dim(outer_params, at, 64, 0)
         return (params - lax.dynamic_slice_in_dim(snapshot[0], at, 64, 0).astype(F32)).astype(BF16)
 
-    def along_y(pair):
+    def along_y(pair, ids):
         quad = added(part(pair, at_a), to_y(part(pair, 1 - at_a), (1, 3)))
-        return added(part(quad, at_b), to_y(part(quad, 1 - at_b), (3, 1)))
-
-    def along_x(octet):
-        total = added(octet, to_x(octet))
-        return joined(total, to_y(total, (3, 1)), at_b)
-
-    def nothing(rows):
-        return lambda array: jnp.zeros((rows, array.shape[1]), BF16)
+        rest = pick(ids, tokens, out_grads, (*SHIFTS[FIRST:], (0, 0)))
+        return added(part(quad, at_b), to_y(part(quad, 1 - at_b), (3, 1))), *rest
+
+    def no_along_y(pair, ids):
+        return (pair[:16], *[pair[:32].reshape(-1, 2 * BLOCK)] * (len(SHIFTS) - FIRST + 1))
+
+    def along_x(octet, sources):
+        return added(octet, to_x(octet)), early(sources, left, right)
+
+    def no_along_x(octet, sources):
+        return octet, jnp.zeros((BLOCK, BLOCK), F32)
+
+    def back(total, sources, acc):
+        return joined(total, to_y(total, (3, 1)), at_b), early(sources, left, right, [acc])
+
+    def no_back(total, sources, acc):
+        return jnp.concatenate([total, total]), jnp.zeros((BLOCK, BLOCK), F32)
 
     always = replica >= 0
+    left, right = left_basis[0, 0], right_basis[0, 0]
     pair = added(difference(core), to_core(difference(1 - core)))
-    octet = lax.cond(always, along_y, nothing(16), after(pair, sends))
-    rows = lax.cond(always, along_x, nothing(32), after(octet, got[:2]))
-    rows = after(rows, got[2:4])
+    sends = pick(block_ids, tokens, out_grads, SHIFTS[:FIRST])
+    got = [to_owner(a, dx, dz) for a, (dx, dz) in zip(sends, SHIFTS)]
+    octet, *rest = lax.cond(always, along_y, no_along_y, after(pair, sends), block_ids)
+    got += [to_owner(a, dx, dz) for a, (dx, dz) in zip(rest, SHIFTS[FIRST:])]
+    total, acc = lax.cond(always, along_x, no_along_x, after(octet, got[:2]), [rest[-1], *got[:2]])
+    rows, acc = lax.cond(always, back, no_back, after(total, got[2:FIRST]), got[2:FIRST], acc)
+    rows = after(rows, got[FIRST:])
     rows = joined(rows, to_y(rows, (1, 3)), at_a)
+    update, first_next, second_next = final(got[FIRST:], acc, left, right, first_moment[0, 0], second_moment[0, 0])
+    rows = after(rows, [update])
     other = to_core(rows)
     due = jnp.broadcast_to(due_rows[:, None], (due_rows.shape[0], 128))
-    outer_next, momentum_next, local_next = outer(
-        core[None], rows, other, outer_params, outer_momentum, snapshot[0], local_params[0], due
-    )
-
-    acc = early([sends[-1]] + got[:EARLY], left, right)
-    update, first_next, second_next = final(
-        got[EARLY:], acc, left, right, first_moment[0, 0], second_moment[0, 0]
-    )
+    state = (outer_params, outer_momentum, snapshot[0], local_params[0], due)
+    halves = outer(core, rows, *state)
+    outer_next, momentum_next, local_next = outer(1 - core, other, *state, into=halves)
     return (
         update[None, None],
         first_next[None, None],

time: 113 us -> 95.2 us (0.84)
  waiting for transfers between devices: 38.8 us -> 18.1 us
  Pallas kernels: 32.4 us -> 42.5 us
  other arithmetic: 9.18 us -> 5.91 us
  starting transfers between devices: 27.2 us -> 25 us
    ppermute x14, waiting for transfers between devices: 38.8 us -> 18.1 us  [moved(): lax.ppermute(array, AXES, [(s, index_of(*where(*place(s)))) for s in rang...]
    pallas_call x3 -> x6, Pallas kernels: 19.2 us -> 27.7 us  [the longest x2 15.3 us: early(): pl.pallas_call(functools.partial(early_kernel, n, len(acc)), out_shape=pl...]
    select_n x2, other arithmetic: 2.66 us -> 0.26 us  [joined(): lax.select(at == 0, jnp.concatenate([mine, other]), jnp.concatenate([othe...]
    ppermute x14, starting transfers between devices: 27.2 us -> 25 us  [moved(): lax.ppermute(array, AXES, [(s, index_of(*where(*place(s)))) for s in rang...]
    pallas_call x1, Pallas kernels: 13.2 us -> 14.8 us  [final(): pl.pallas_call(functools.partial(final_kernel, n), out_shape=[square] * 3...]
  transfers between devices with their start and end apart: 14 -> 14, of which waited for: 6 -> 4; matrix products, arithmetic and copies ran while one was open for 7% -> 5% of each run, Pallas kernels for 23% -> 41%
where the time goes in v3:
time: 95.2 us; the launch traced here: 95 us
  Pallas kernels  42.5 us (45%)
  starting transfers between devices  25 us (26%)
  waiting for transfers between devices  18.1 us (19%)
  other arithmetic  5.91 us (6%)
  local copies, waits for them, and re-layouts  2.56 us (3%)
    ppermute x14, starting transfers between devices, moved(): lax.ppermute(array, AXES, [(s, index_of(*where(*place(s)))) for s in rang...  25 us
    ppermute x14, waiting for transfers between devices, moved(): lax.ppermute(array, AXES, [(s, index_of(*where(*place(s)))) for s in rang...  18.1 us
    pallas_call x2, Pallas kernels, early(): pl.pallas_call(functools.partial(early_kernel, n, len(acc)), out_shape=pl...  15.3 us
    pallas_call x1, Pallas kernels, final(): pl.pallas_call(functools.partial(final_kernel, n), out_shape=[square] * 3...  14.8 us
    pallas_call x2, Pallas kernels, outer(): pl.pallas_call(outer_kernel, out_shape=[pltpu.HBM(params.shape, F32), plt...  6.34 us
    pallas_call x2, Pallas kernels, pick(): pl.pallas_call(functools.partial(pick_kernel, shifts), out_shape=[pltpu.H...  6.05 us
    convert_element_type x4, other arithmetic, added(): return (one.astype(F32) + two.astype(F32)).astype(BF16)  3.61 us
    convert_element_type x1, other arithmetic, difference(): (params - lax.dynamic_slice_in_dim(snapshot[0], at, 64, 0).astype(F32)).a...  2.04 us
  transfers between devices with their start and end apart: 14, of which 4 were waited for; matrix products, arithmetic and copies ran while one was open for 5% of the time, Pallas kernels for 41%

profile of v3, /device:TPU:1, one launch (start us, length us, event | category | flops | bytes accessed | tf_op | source)
XLA Modules:
  0.0 95.0 jit_solution(7052759738751961781)
XLA Ops:
  0.6 0.0 copy-start.6
  0.7 2.0 %fusion = bf16[64,8192]{1,0:T(8,128)(2,1)S(1)} fusion(f32[128,8192]{1,0:T(8,128)} %params.3, s32[]{:T(128)S(6)} %select_n.58, bf16[1,128,8192]{2,1,0:T(8,128)(2,1)} %param.27), kind=kLoop, calls=%fused_computation.8 | loop fusion | flops 1572864 | bytes 4194308 | tf_op jit(solution)/shard_map/convert_element_type | solution.py:337
  2.7 0.0 copy-start.1
  2.7 1.5 %collective-permute-start.4 = (bf16[64,8192]{1,0:T(8,128)(2,1)S(1)}, bf16[64,8192]{1,0:T(8,128)(2,1)}, u32[]{:S(2)}, u32[]{:S(2)}) collective-permute-start(bf16[64,8192]{1,0:T(8,128)(2,1)S(1)} %fusion), channel_id=1, source_target_pairs={{0,8},{1,9},{2,10},{3,11},{4,12},{5,13},{6,14},{7,15},{8,0},{9,1},... | collective-permute-start | bytes 3145736 | tf_op jit(solution)/shard_map/ppermute | solution.py:33
  4.2 0.0 copy-done.6
  4.2 3.0 %pick.3 = (bf16[128,2048]{1,0:T(8,128)(2,1)}, bf16[128,2048]{1,0:T(8,128)(2,1)}, bf16[128,2048]{1,0:T(8,128)(2,1)}, bf16[128,2048]{1,0:T(8,128)(2,1)}) custom-call(s32[8]{0:T(128)S(1)} %copy-done.6, bf16[128,4096]{1,0:T(8,128)(2,1)} %tokens.1, bf16[128,14336]{1,0:T(8,128)(2,1)} %out_grads.1), custom_call_target="tpu_custom_call" | custom-call | bytes 8388608 | tf_op jit(solution)/shard_map/pick/pallas_call | solution.py:90
  7.2 6.2 %collective-permute-start.8 = (bf16[128,2048]{1,0:T(8,128)(2,1)}, bf16[128,2048]{1,0:T(8,128)(2,1)}, u32[]{:S(2)}, u32[]{:S(2)}) collective-permute-start(bf16[128,2048]{1,0:T(8,128)(2,1)} %get-tuple-element.97), channel_id=1, source_target_pairs={{0,6},{1,7},{2,4},{3,5},{4,2},{5,3},{6,0},{7,1},{8,14},{9,15},{10,... | collective-permute-start | bytes 1572872 | tf_op jit(solution)/shard_map/ppermute | solution.py:33
  13.5 0.7 collective-permute-start.9
  14.1 4.4 %collective-permute-start.10 = (bf16[128,2048]{1,0:T(8,128)(2,1)}, bf16[128,2048]{1,0:T(8,128)(2,1)}, u32[]{:S(2)}, u32[]{:S(2)}) collective-permute-start(bf16[128,2048]{1,0:T(8,128)(2,1)} %get-tuple-element.99), channel_id=1, source_target_pairs={{0,7},{1,4},{2,5},{3,6},{4,3},{5,0},{6,1},{7,2},{8,15},{9,12},{10,... | collective-permute-start | bytes 1572872 | tf_op jit(solution)/shard_map/ppermute | solution.py:33
  18.5 0.0 collective-permute-start.11
  18.5 0.0 collective-permute-done.4
  18.6 0.0 copy-done.1
  18.6 2.2 %add_convert_fusion.3 = bf16[64,8192]{1,0:T(8,128)(2,1)S(1)} fusion(bf16[64,8192]{1,0:T(8,128)(2,1)} %collective-permute-done.4, f32[128,8192]{1,0:T(8,128)} %params.3, s32[]{:T(128)S(6)} %select_n.57, bf16[1,128,8192]{2,1,0:T(8,128)(2,1)S(1)} %copy-done.1), kind=kLoop, calls=%fused_computation.11 | loop fusion | flops 3670016 | bytes 5242884 | tf_op jit(solution)/shard_map/convert_element_type | solution.py:303
  20.8 18.5 %conditional.3 = (bf16[16,8192]{1,0:T(8,128)(2,1)S(1)}, bf16[128,2048]{1,0:T(8,128)(2,1)}, bf16[128,2048]{1,0:T(8,128)(2,1)}, bf16[128,2048]{1,0:T(8,128)(2,1)}, bf16[128,2048]{1,0:T(8,128)(2,1)}) conditional(s32[]{:T(128)} %convert_element_type.59, bf16[64,8192]{1,0:T(8,128)(2,1)S(1)} %add_convert_fusion.3, (s32[]{:T(128)}, ...), branch_computations={%region_0.1_spmd, %region_1.2_spmd} | conditional | flops 1572882 | bytes 19661200 | solution.py:364
  20.8 0.8 constant_dynamic-slice_fusion.1
  21.6 2.7 %collective-permute-start = (bf16[32,8192]{1,0:T(8,128)(2,1)}, bf16[32,8192]{1,0:T(8,128)(2,1)}, u32[]{:S(2)}, u32[]{:S(2)}) collective-permute-start(bf16[32,8192]{1,0:T(8,128)(2,1)} %constant_dynamic-slice_fusion.1), channel_id=1, source_target_pairs={{0,32},{1,33},{2,34},{3,35},{4,36},{5,37},{6,38},{7,39},{8,104},{9... | collective-permute-start | bytes 1572872 | tf_op jit(solution)/shard_map/cond/branch_1_fun/ppermute | solution.py:33
  24.4 7.2 %collective-permute-done = bf16[32,8192]{1,0:T(8,128)(2,1)} collective-permute-done((bf16[32,8192]{1,0:T(8,128)(2,1)}, bf16[32,8192]{1,0:T(8,128)(2,1)}, u32[]{:S(2)}, u32[]{:S(2)}) %collective-permute-start) | collective-permute-done | bytes 524320 | tf_op jit(solution)/shard_map/cond/branch_1_fun/ppermute | solution.py:33
  31.6 1.2 %add_convert_fusion = bf16[32,8192]{1,0:T(8,128)(2,1)S(1)} fusion(bf16[32,8192]{1,0:T(8,128)(2,1)} %collective-permute-done, bf16[64,8192]{1,0:T(8,128)(2,1)S(1)} %get-tuple-element.41, s32[]{:T(128)S(6)} %select_n.40), kind=kLoop, calls=%fused_computation | loop fusion | flops 1048576 | bytes 1572868 | tf_op jit(solution)/shard_map/cond/branch_1_fun/convert_element_type | solution.py:303
  32.7 0.0 copy-start.4
  32.7 0.8 copy-done.4
  33.6 0.1 collective-permute-start.1
  33.7 0.0 copy-start.5
  33.7 3.0 %pick.2 = (bf16[128,2048]{1,0:T(8,128)(2,1)}, bf16[128,2048]{1,0:T(8,128)(2,1)}, bf16[128,2048]{1,0:T(8,128)(2,1)}, bf16[128,2048]{1,0:T(8,128)(2,1)}) custom-call(s32[8]{0:T(128)S(1)} %get-tuple-element.44.ids, bf16[128,4096]{1,0:T(8,128)(2,1)} %get-tuple-element.45.tokens, bf16[128,14336]{1,0:T(8,128)(2,1)} %get-tuple-element.46.out_grads), custom_call_target="tpu_custom_call" | custom-call | bytes 8388608 | tf_op jit(solution)/shard_map/cond/branch_1_fun/pick/pallas_call | solution.py:90
  36.7 2.6 %collective-permute-done.1 = bf16[16,8192]{1,0:T(8,128)(2,1)S(1)} collective-permute-done((bf16[16,8192]{1,0:T(8,128)(2,1)S(1)}, bf16[16,8192]{1,0:T(8,128)(2,1)S(1)}, u32[]{:S(2)}, u32[]{:S(2)}) %collective-permute-start.1) | collective-permute-done | bytes 262176 | tf_op jit(solution)/shard_map/cond/branch_1_fun/ppermute | solution.py:33
  39.3 0.0 copy-done.5
  39.3 0.1 add_convert_fusion.1
  39.3 0.0 collective-permute-done.8
  39.3 0.0 collective-permute-done.9
  39.4 0.1 collective-permute-start.5
  39.4 2.7 %collective-permute-start.6 = (bf16[128,2048]{1,0:T(8,128)(2,1)}, bf16[128,2048]{1,0:T(8,128)(2,1)}, u32[]{:S(2)}, u32[]{:S(2)}) collective-permute-start(bf16[128,2048]{1,0:T(8,128)(2,1)} %get-tuple-element.103), channel_id=1, source_target_pairs={{0,3},{1,0},{2,1},{3,2},{4,7},{5,4},{6,5},{7,6},{8,11},{9,8},{10,9... | collective-permute-start | bytes 1572872 | tf_op jit(solution)/shard_map/ppermute | solution.py:33
  42.1 12.7 %conditional.4 = (bf16[16,8192]{1,0:T(8,128)(2,1)S(1)}, f32[1024,1024]{1,0:T(8,128)}) conditional(s32[]{:T(128)} %convert_element_type.59, bf16[16,8192]{1,0:T(8,128)(2,1)S(1)} %get-tuple-element.106, (bf16[16,8192]{1,0:T(8,128)(2,1)S(1)}, bf16[128,2048]{1,0:T(8,128)(2,1)}, bf16[128,2048]{1,0:T(8,128)(2,1)}, bf16[128,2048]{1,0:T(8,128)(2,1)}, ...), branch_computations={%region_2.3_spmd, %region_3.4_spmd} | conditional | flops 2416443392 | bytes 6029368 | solution.py:366
  42.1 0.3 collective-permute-start.2
  42.4 8.2 %early.2 = f32[1024,1024]{1,0:T(8,128)} custom-call(bf16[128,2048]{1,0:T(8,128)(2,1)} %get-tuple-element.52.refs_0_, bf16[128,2048]{1,0:T(8,128)(2,1)} %get-tuple-element.53.refs_1_, bf16[128,2048]{1,0:T(8,128)(2,1)} %get-tuple-element.54.refs_2_, bf16[1024,1024]{1,0:T(8,128)(2,1)} %get-tuple-element.55.refs_3_, bf16[1024,1024]{1,0:T(8,128)(2,1)} %get-tuple-element.56.refs_4_), custom_call_target="tpu_custom_call" | custom-call | flops 2415919104 | bytes 4194304 | tf_op jit(solution)/shard_map/cond/branch_1_fun/early/pallas_call | solution.py:154
  50.6 4.1 %collective-permute-done.2 = bf16[16,8192]{1,0:T(8,128)(2,1)S(1)} collective-permute-done((bf16[16,8192]{1,0:T(8,128)(2,1)S(1)}, bf16[16,8192]{1,0:T(8,128)(2,1)S(1)}, u32[]{:S(2)}, u32[]{:S(2)}) %collective-permute-start.2) | collective-permute-done | bytes 262176 | tf_op jit(solution)/shard_map/cond/branch_1_fun/ppermute | solution.py:33
  54.7 0.2 add_convert_fusion.2
  54.8 1.8 %collective-permute-start.7 = (bf16[128,2048]{1,0:T(8,128)(2,1)}, bf16[128,2048]{1,0:T(8,128)(2,1)}, u32[]{:S(2)}, u32[]{:S(2)}) collective-permute-start(bf16[128,2048]{1,0:T(8,128)(2,1)} %get-tuple-element.104), channel_id=1, source_target_pairs={{0,4},{1,5},{2,6},{3,7},{4,0},{5,1},{6,2},{7,3},{8,12},{9,13},{10,... | collective-permute-start | bytes 1572872 | tf_op jit(solution)/shard_map/ppermute | solution.py:33
  56.7 0.0 collective-permute-done.10
  56.7 0.0 collective-permute-done.11
  56.7 8.5 %conditional.5 = (bf16[32,8192]{1,0:T(8,128)(2,1)S(1)}, f32[1024,1024]{1,0:T(8,128)}) conditional(s32[]{:T(128)} %convert_element_type.59, bf16[16,8192]{1,0:T(8,128)(2,1)S(1)} %get-tuple-element.109, (s32[]{:T(128)}, bf16[16,8192]{1,0:T(8,128)(2,1)S(1)}, bf16[128,2048]{1,0:T(8,128)(2,1)}, bf16[128,2048]{1,0:T(8,128)(2,1)}, ...), branch_computations={%region_4.5_spmd, %region_5.6_spmd} | conditional | flops 1612972032 | bytes 6291522 | solution.py:367
  56.7 1.3 %collective-permute-start.3 = (bf16[16,8192]{1,0:T(8,128)(2,1)S(1)}, bf16[16,8192]{1,0:T(8,128)(2,1)S(1)}, u32[]{:S(2)}, u32[]{:S(2)}) collective-permute-start(bf16[16,8192]{1,0:T(8,128)(2,1)S(1)} %get-tuple-element.58), channel_id=1, source_target_pairs={{0,96},{1,97},{2,98},{3,99},{4,100},{5,101},{6,102},{7,103},{8,40}... | collective-permute-start | bytes 786440 | tf_op jit(solution)/shard_map/cond/branch_1_fun/ppermute | solution.py:33
  58.0 7.1 %early.3 = f32[1024,1024]{1,0:T(8,128)} custom-call(bf16[128,2048]{1,0:T(8,128)(2,1)} %get-tuple-element.59.refs_0_, bf16[128,2048]{1,0:T(8,128)(2,1)} %get-tuple-element.60.refs_1_, bf16[1024,1024]{1,0:T(8,128)(2,1)} %get-tuple-element.61.refs_2_, bf16[1024,1024]{1,0:T(8,128)(2,1)} %get-tuple-element.62.refs_3_, f32[1024,1024]{1,0:T(8,128)} %get-tuple-element.63.refs_4_), custom_call_target="tpu_custom_call" | custom-call | flops 1610612736 | bytes 4194304 | tf_op jit(solution)/shard_map/cond/branch_1_fun/early/pallas_call | solution.py:154
  65.1 0.0 collective-permute-done.3
  65.1 0.1 maximum_select_fusion
  65.2 0.0 collective-permute-done.5.refs_0_
  65.2 0.0 collective-permute-done.6.refs_1_
  65.2 4.3 %collective-permute-done.7.refs_2_ = bf16[128,2048]{1,0:T(8,128)(2,1)} collective-permute-done((bf16[128,2048]{1,0:T(8,128)(2,1)}, bf16[128,2048]{1,0:T(8,128)(2,1)}, u32[]{:S(2)}, u32[]{:S(2)}) %collective-permute-start.7) | collective-permute-done | bytes 524320 | tf_op jit(solution)/shard_map/ppermute | solution.py:33
  69.5 2.7 %collective-permute-start.12 = (bf16[32,8192]{1,0:T(8,128)(2,1)S(1)}, bf16[32,8192]{1,0:T(8,128)(2,1)S(1)}, u32[]{:S(2)}, u32[]{:S(2)}) collective-permute-start(bf16[32,8192]{1,0:T(8,128)(2,1)S(1)} %get-tuple-element.116), channel_id=1, source_target_pairs={{0,32},{1,33},{2,34},{3,35},{4,36},{5,37},{6,38},{7,39},{8,104},{9... | collective-permute-start | bytes 1572872 | tf_op jit(solution)/shard_map/ppermute | solution.py:33
  72.2 0.0 copy-start
  72.2 0.0 copy-start.2
  72.2 14.8 %final.1 = (bf16[1024,1024]{1,0:T(8,128)(2,1)}, bf16[1024,1024]{1,0:T(8,128)(2,1)}, bf16[1024,1024]{1,0:T(8,128)(2,1)}) custom-call(bf16[128,2048]{1,0:T(8,128)(2,1)} %collective-permute-done.5.refs_0_, bf16[128,2048]{1,0:T(8,128)(2,1)} %collective-permute-done.6.refs_1_, bf16[128,2048]{1,0:T(8,128)(2,1)} %collective-permute-done.7.refs_2_, ...), custom_call_target="tpu_custom_call" | custom-call | flops 6710886400 | bytes 6291456 | tf_op jit(solution)/shard_map/final/pallas_call | solution.py:237
  87.0 0.0 copy-start.7
  87.0 0.0 copy-start.3
  87.0 0.0 collective-permute-done.12
  87.0 0.2 maximum_select_fusion.1.total
  87.2 0.5 collective-permute-start.13
  87.7 0.0 copy-done.7
  87.7 0.1 broadcast_in_dim.28.due
  87.8 0.0 copy-done
  87.8 0.0 copy-done.2
  87.8 0.8 copy-done.3
  88.6 3.2 %outer.2 = (f32[128,8192]{1,0:T(8,128)}, f32[128,8192]{1,0:T(8,128)}, bf16[128,8192]{1,0:T(8,128)(2,1)}) custom-call(s32[1]{0:T(128)} %bitcast.12.half, bf16[64,8192]{1,0:T(8,128)(2,1)S(1)} %maximum_select_fusion.1.total, f32[128,8192]{1,0:T(8,128)S(1)} %copy-done, f32[128,8192]{1,0:T(8,128)S(1)} %copy-done.2, bf16[128,8192]{1,0:T(8,128)(2,1)S(1)} %bitcast.18, ...), custom_call_target="tpu_custom_call" | custom-call | flops 5242880 | bytes 12582912 | tf_op jit(solution)/shard_map/outer/pallas_call | solution.py:277
  91.8 0.0 collective-permute-done.13.total
  91.8 3.2 %outer.3 = (f32[128,8192]{1,0:T(8,128)}, f32[128,8192]{1,0:T(8,128)}, bf16[128,8192]{1,0:T(8,128)(2,1)}) custom-call(s32[1]{0:T(128)} %bitcast.9.half, bf16[64,8192]{1,0:T(8,128)(2,1)S(1)} %collective-permute-done.13.total, f32[128,8192]{1,0:T(8,128)S(1)} %copy-done, ...), custom_call_target="tpu_custom_call", output_to_operand_aliasing={{0}: (7, {}), {1}: (8, {}), {2}: (9, {})} | custom-call | flops 5242880 | bytes 12582912 | tf_op jit(solution)/shard_map/outer/pallas_call | solution.py:277
  (1 shorter events, 0.0 us)
Async XLA Ops:
  0.6 3.6 %copy-start.6 = (s32[8]{0:T(128)S(1)}, s32[8]{0:T(128)}, u32[]{:S(2)}) copy-start(s32[8]{0:T(128)} %ids.1) | copy-start | bytes 100
  2.7 15.9 %copy-start.1 = (bf16[1,128,8192]{2,1,0:T(8,128)(2,1)S(1)}, bf16[1,128,8192]{2,1,0:T(8,128)(2,1)}, u32[]{:S(2)}) copy-start(bf16[1,128,8192]{2,1,0:T(8,128)(2,1)} %param.27) | copy-start | bytes 6291460
  2.7 15.8 %collective-permute-start.4 = (bf16[64,8192]{1,0:T(8,128)(2,1)S(1)}, bf16[64,8192]{1,0:T(8,128)(2,1)}, u32[]{:S(2)}, u32[]{:S(2)}) collective-permute-start(bf16[64,8192]{1,0:T(8,128)(2,1)S(1)} %fusion), channel_id=1, source_target_pairs={{0,8},{1,9},{2,10},{3,11},{4,12},{5,13},{6,14},{7,15},{8,0},{9,1},... | collective-permute-start | bytes 3145736 | tf_op jit(solution)/shard_map/ppermute | solution.py:33
  7.2 32.1 %collective-permute-start.8 = (bf16[128,2048]{1,0:T(8,128)(2,1)}, bf16[128,2048]{1,0:T(8,128)(2,1)}, u32[]{:S(2)}, u32[]{:S(2)}) collective-permute-start(bf16[128,2048]{1,0:T(8,128)(2,1)} %get-tuple-element.97), channel_id=1, source_target_pairs={{0,6},{1,7},{2,4},{3,5},{4,2},{5,3},{6,0},{7,1},{8,14},{9,15},{10,... | collective-permute-start | bytes 1572872 | tf_op jit(solution)/shard_map/ppermute | solution.py:33
  13.5 25.9 %collective-permute-start.9 = (bf16[128,2048]{1,0:T(8,128)(2,1)}, bf16[128,2048]{1,0:T(8,128)(2,1)}, u32[]{:S(2)}, u32[]{:S(2)}) collective-permute-start(bf16[128,2048]{1,0:T(8,128)(2,1)} %get-tuple-element.98), channel_id=1, source_target_pairs={{0,5},{1,6},{2,7},{3,4},{4,1},{5,2},{6,3},{7,0},{8,13},{9,14},{10,... | collective-permute-start | bytes 1572872 | tf_op jit(solution)/shard_map/ppermute | solution.py:33
  14.1 42.5 %collective-permute-start.10 = (bf16[128,2048]{1,0:T(8,128)(2,1)}, bf16[128,2048]{1,0:T(8,128)(2,1)}, u32[]{:S(2)}, u32[]{:S(2)}) collective-permute-start(bf16[128,2048]{1,0:T(8,128)(2,1)} %get-tuple-element.99), channel_id=1, source_target_pairs={{0,7},{1,4},{2,5},{3,6},{4,3},{5,0},{6,1},{7,2},{8,15},{9,12},{10,... | collective-permute-start | bytes 1572872 | tf_op jit(solution)/shard_map/ppermute | solution.py:33
  18.5 38.1 %collective-permute-start.11 = (bf16[128,2048]{1,0:T(8,128)(2,1)}, bf16[128,2048]{1,0:T(8,128)(2,1)}, u32[]{:S(2)}, u32[]{:S(2)}) collective-permute-start(bf16[128,2048]{1,0:T(8,128)(2,1)} %get-tuple-element.100), channel_id=1, source_target_pairs={{0,2},{1,3},{2,0},{3,1},{4,6},{5,7},{6,4},{7,5},{8,10},{9,11},{10,... | collective-permute-start | bytes 1572872 | tf_op jit(solution)/shard_map/ppermute | solution.py:33
  21.6 9.9 %collective-permute-start = (bf16[32,8192]{1,0:T(8,128)(2,1)}, bf16[32,8192]{1,0:T(8,128)(2,1)}, u32[]{:S(2)}, u32[]{:S(2)}) collective-permute-start(bf16[32,8192]{1,0:T(8,128)(2,1)} %constant_dynamic-slice_fusion.1), channel_id=1, source_target_pairs={{0,32},{1,33},{2,34},{3,35},{4,36},{5,37},{6,38},{7,39},{8,104},{9... | collective-permute-start | bytes 1572872 | tf_op jit(solution)/shard_map/cond/branch_1_fun/ppermute | solution.py:33
  32.7 0.8 copy-start.4
  33.6 5.7 %collective-permute-start.1 = (bf16[16,8192]{1,0:T(8,128)(2,1)S(1)}, bf16[16,8192]{1,0:T(8,128)(2,1)S(1)}, u32[]{:S(2)}, u32[]{:S(2)}) collective-permute-start(bf16[16,8192]{1,0:T(8,128)(2,1)S(1)} %constant_dynamic-slice_fusion), channel_id=1, source_target_pairs={{0,96},{1,97},{2,98},{3,99},{4,100},{5,101},{6,102},{7,103},{8,40}... | collective-permute-start | bytes 786440 | tf_op jit(solution)/shard_map/cond/branch_1_fun/ppermute | solution.py:33
  33.7 5.6 %copy-start.5 = (bf16[32,8192]{1,0:T(8,128)(2,1)S(1)}, bf16[32,8192]{1,0:T(8,128)(2,1)}, u32[]{:S(2)}) copy-start(bf16[32,8192]{1,0:T(8,128)(2,1)} %copy-done.4) | copy-start | bytes 1572868 | tf_op jit(solution)/shard_map/cond
  39.4 25.8 %collective-permute-start.5 = (bf16[128,2048]{1,0:T(8,128)(2,1)}, bf16[128,2048]{1,0:T(8,128)(2,1)}, u32[]{:S(2)}, u32[]{:S(2)}) collective-permute-start(bf16[128,2048]{1,0:T(8,128)(2,1)} %get-tuple-element.102), channel_id=1, source_target_pairs={{0,1},{1,2},{2,3},{3,0},{4,5},{5,6},{6,7},{7,4},{8,9},{9,10},{10,1... | collective-permute-start | bytes 1572872 | tf_op jit(solution)/shard_map/ppermute | solution.py:33
  39.4 25.8 %collective-permute-start.6 = (bf16[128,2048]{1,0:T(8,128)(2,1)}, bf16[128,2048]{1,0:T(8,128)(2,1)}, u32[]{:S(2)}, u32[]{:S(2)}) collective-permute-start(bf16[128,2048]{1,0:T(8,128)(2,1)} %get-tuple-element.103), channel_id=1, source_target_pairs={{0,3},{1,0},{2,1},{3,2},{4,7},{5,4},{6,5},{7,6},{8,11},{9,8},{10,9... | collective-permute-start | bytes 1572872 | tf_op jit(solution)/shard_map/ppermute | solution.py:33
  42.1 12.6 %collective-permute-start.2 = (bf16[16,8192]{1,0:T(8,128)(2,1)S(1)}, bf16[16,8192]{1,0:T(8,128)(2,1)S(1)}, u32[]{:S(2)}, u32[]{:S(2)}) collective-permute-start(bf16[16,8192]{1,0:T(8,128)(2,1)S(1)} %get-tuple-element.51), channel_id=1, source_target_pairs={{0,16},{1,17},{2,18},{3,19},{4,20},{5,21},{6,22},{7,23},{8,24},{9,... | collective-permute-start | bytes 786440 | tf_op jit(solution)/shard_map/cond/branch_1_fun/ppermute | solution.py:33
  54.8 14.7 %collective-permute-start.7 = (bf16[128,2048]{1,0:T(8,128)(2,1)}, bf16[128,2048]{1,0:T(8,128)(2,1)}, u32[]{:S(2)}, u32[]{:S(2)}) collective-permute-start(bf16[128,2048]{1,0:T(8,128)(2,1)} %get-tuple-element.104), channel_id=1, source_target_pairs={{0,4},{1,5},{2,6},{3,7},{4,0},{5,1},{6,2},{7,3},{8,12},{9,13},{10,... | collective-permute-start | bytes 1572872 | tf_op jit(solution)/shard_map/ppermute | solution.py:33
  56.7 8.4 %collective-permute-start.3 = (bf16[16,8192]{1,0:T(8,128)(2,1)S(1)}, bf16[16,8192]{1,0:T(8,128)(2,1)S(1)}, u32[]{:S(2)}, u32[]{:S(2)}) collective-permute-start(bf16[16,8192]{1,0:T(8,128)(2,1)S(1)} %get-tuple-element.58), channel_id=1, source_target_pairs={{0,96},{1,97},{2,98},{3,99},{4,100},{5,101},{6,102},{7,103},{8,40}... | collective-permute-start | bytes 786440 | tf_op jit(solution)/shard_map/cond/branch_1_fun/ppermute | solution.py:33
  69.5 17.5 %collective-permute-start.12 = (bf16[32,8192]{1,0:T(8,128)(2,1)S(1)}, bf16[32,8192]{1,0:T(8,128)(2,1)S(1)}, u32[]{:S(2)}, u32[]{:S(2)}) collective-permute-start(bf16[32,8192]{1,0:T(8,128)(2,1)S(1)} %get-tuple-element.116), channel_id=1, source_target_pairs={{0,32},{1,33},{2,34},{3,35},{4,36},{5,37},{6,38},{7,39},{8,104},{9... | collective-permute-start | bytes 1572872 | tf_op jit(solution)/shard_map/ppermute | solution.py:33
  72.2 15.6 %copy-start = (f32[128,8192]{1,0:T(8,128)S(1)}, f32[128,8192]{1,0:T(8,128)}, u32[]{:S(2)}) copy-start(f32[128,8192]{1,0:T(8,128)} %params.3) | copy-start | bytes 12582916
  72.2 15.6 %copy-start.2 = (f32[128,8192]{1,0:T(8,128)S(1)}, f32[128,8192]{1,0:T(8,128)}, u32[]{:S(2)}) copy-start(f32[128,8192]{1,0:T(8,128)} %momentum.3) | copy-start | bytes 12582916
  87.0 0.7 copy-start.7
  87.0 1.6 %copy-start.3 = (bf16[1,128,8192]{2,1,0:T(8,128)(2,1)S(1)}, bf16[1,128,8192]{2,1,0:T(8,128)(2,1)}, u32[]{:S(2)}) copy-start(bf16[1,128,8192]{2,1,0:T(8,128)(2,1)} %param.28) | copy-start | bytes 6291460
  87.2 4.6 %collective-permute-start.13 = (bf16[64,8192]{1,0:T(8,128)(2,1)S(1)}, bf16[64,8192]{1,0:T(8,128)(2,1)S(1)}, u32[]{:S(2)}, u32[]{:S(2)}) collective-permute-start(bf16[64,8192]{1,0:T(8,128)(2,1)S(1)} %maximum_select_fusion.1.total), channel_id=1, source_target_pairs={{0,8},{1,9},{2,10},{3,11},{4,12},{5,13},{6,14},{7,15},{8,0},{9,1},... | collective-permute-start | bytes 3145736 | tf_op jit(solution)/shard_map/ppermute | solution.py:33

commit v4 on v3

--- a/solution.py
+++ b/solution.py
@@ -13,6 +13,7 @@
 AXES = ("replica", "fsdp")
 SHIFTS = ((1, 2), (1, 1), (1, 3), (0, 2), (0, 1), (0, 3), (1, 0))
 FIRST = 4
+EARLY = 4
 CORRECT = 1.0 - 0.95**10
 F32 = jnp.float32
 BF16 = jnp.bfloat16
@@ -124,10 +125,12 @@
     copies.append(pltpu.make_async_copy(right_in, right, sems.at[n + 1]))
     if more:
         copies.append(pltpu.make_async_copy(acc_in, acc, sems.at[n + 2]))
-    for copy in copies:
+    for copy in copies[: n + 2]:
         copy.start()
     for copy in copies[: n + 2]:
         copy.wait()
+    if more:
+        copies[-1].start()
     rotate([held.at[i] for i in range(n)], left, right, yt, zz)
     if more:
         copies[-1].wait()
@@ -171,17 +174,44 @@
     )(*[hbm(a) for a in (*bufs, left, right, *acc)])
 
 
+def hold_kernel(gate, *refs):
+    sources, outs, sems = refs[:2], refs[2:4], refs[4]
+    copies = [pltpu.make_async_copy(a, b, sems.at[i]) for i, (a, b) in enumerate(zip(sources, outs))]
+    for copy in copies:
+        copy.start()
+    for copy in copies:
+        copy.wait()
+
+
+def hold(gate, arrays):
+    return pl.pallas_call(
+        hold_kernel,
+        out_shape=[pltpu.VMEM(a.shape, a.dtype) for a in arrays],
+        in_specs=[ANY] * 3,
+        out_specs=[VM] * 2,
+        scratch_shapes=[pltpu.SemaphoreType.DMA((2,))],
+        compiler_params=pltpu.CompilerParams(vmem_limit_bytes=1 << 20),
+        cost_estimate=pl.CostEstimate(flops=0, bytes_accessed=8 << 20, transcendentals=0),
+        name="hold",
+    )(*[hbm(a) for a in (gate, *arrays)])
+
+
 def final_kernel(n, *refs):
-    operands, (update, first_next, second_next) = refs[: n + 5], refs[n + 5 : n + 8]
-    held, yt, zz, direction, m_out, v_out, u_out, left, right, acc, first, second, sems, in_sems = refs[n + 8 :]
-    places = [held.at[i] for i in range(n)] + [left, right, acc, first, second]
-    loads = [pltpu.make_async_copy(a, b, in_sems.at[i]) for i, (a, b) in enumerate(zip(operands, places))]
-    for load in loads:
+    left, right, refs = refs[0], refs[1], refs[2:]
+    operands, carried, refs = refs[: n + 3], refs[n + 3 : n + 7], refs[n + 7 :]
+    (update, first_next, second_next), kept, refs = refs[:3], refs[3:7], refs[7:]
+    held, yt, zz, direction, m_out, v_out, u_out, acc, first, second, sems, in_sems = refs
+    places = [held.at[i] for i in range(n)] + [acc, first, second]
+    pairs = [*zip(operands, places), *zip(carried, kept)]
+    loads = [pltpu.make_async_copy(a, b, in_sems.at[i]) for i, (a, b) in enumerate(pairs)]
+    for load in loads[:n]:
         load.start()
-    for load in loads[: n + 2]:
+    for load in loads[:n]:
         load.wait()
+    for load in loads[n:]:
+        load.start()
     rotate(places[:n], left, right, yt, zz)
-    for load in loads[n + 2 :]:
+    for load in loads[n : n + 3]:
         load.wait()
     rows = 256
 
@@ -192,7 +222,7 @@
             pltpu.make_async_copy(v_out.at[at, :], second_next.at[at, :], sems.at[4 + i]),
         )
 
-    @pl.loop(0, BLOCK // rows)
+    @pl.loop(0, BLOCK // rows, unroll=True)
     def _(i):
         at = pl.ds(pl.multiple_of(i * rows, rows), rows)
         rotated = acc[at, :] + jnp.dot(yt[at, :], zz[...], preferred_element_type=F32)
@@ -229,51 +259,72 @@
     def _(i):
         update_copy(i).wait()
 
-
-def final(bufs, acc, left, right, first, second):
+    for load in loads[n + 3 :]:
+        load.wait()
+
+
+def final(bufs, acc, left, right, first, second, carried):
     n = len(bufs)
     square = jax.ShapeDtypeStruct((BLOCK, BLOCK), BF16)
     block = pltpu.VMEM((BLOCK, BLOCK), BF16)
     return pl.pallas_call(
         functools.partial(final_kernel, n),
-        out_shape=[square] * 3,
-        in_specs=[ANY] * (n + 5),
-        out_specs=[ANY] * 3,
+        out_shape=[square] * 3 + [pltpu.VMEM(a.shape, a.dtype) for a in carried],
+        in_specs=[VM] * 2 + [ANY] * (n + 7),
+        out_specs=[ANY] * 3 + [VM] * 4,
         scratch_shapes=[
             pltpu.VMEM((n, TOK, 2 * BLOCK), BF16),
             pltpu.VMEM((BLOCK, n * TOK), BF16),
             pltpu.VMEM((n * TOK, BLOCK), BF16),
-            *[block] * 6,
+            *[block] * 4,
             pltpu.VMEM((BLOCK, BLOCK), F32),
             *[block] * 2,
             pltpu.SemaphoreType.DMA((12,)),
-            pltpu.SemaphoreType.DMA((n + 5,)),
+            pltpu.SemaphoreType.DMA((n + 7,)),
         ],
         compiler_params=pltpu.CompilerParams(vmem_limit_bytes=28 << 20),
         cost_estimate=pl.CostEstimate(
             flops=(6 * n * TOK + 4 * BLOCK) * BLOCK * BLOCK, bytes_accessed=6 << 20, transcendentals=2 << 20
         ),
         name="final",
-    )(*[hbm(a) for a in (*bufs, left, right, acc, first, second)])
+    )(vmem(left), vmem(right), *[hbm(a) for a in (*bufs, acc, first, second, *carried)])
 
 
 def outer_kernel(half, total, params, momentum, snap, local, due, *rest):
-    params_next, momentum_next, local_next = rest[-3:]
-    pseudo = total[...].astype(F32) * (1.0 / 16)
-    old, old_momentum = params[...], momentum[...]
-    moment = 0.9 * old_momentum + pseudo
-    stepped = old - 0.7 * (pseudo + 0.9 * moment)
-    on = jnp.broadcast_to(due[:, :1], old.shape) == 1
-    params_next[...] = jnp.where(on, stepped, old)
-    momentum_next[...] = jnp.where(on, moment, old_momentum)
-    kept = local[...].astype(F32)
-    local_next[...] = jnp.where(on, stepped + (kept - snap[...].astype(F32)), kept).astype(BF16)
+    nexts, (params_out, momentum_out, local_out, sems) = rest[-7:-4], rest[-4:]
+
+    def stores(i):
+        at = pl.ds(pl.multiple_of((half[0] * 4 + i) * 16, 16), 16)
+        mine = pl.ds(pl.multiple_of(i * 16, 16), 16)
+        return [
+            pltpu.make_async_copy(out.at[mine, :], to.at[at, :], sems.at[3 * i + k])
+            for k, (out, to) in enumerate(zip((params_out, momentum_out, local_out), nexts))
+        ]
+
+    @pl.loop(0, 4)
+    def _(i):
+        at = pl.ds(pl.multiple_of((half[0] * 4 + i) * 16, 16), 16)
+        mine = pl.ds(pl.multiple_of(i * 16, 16), 16)
+        pseudo = total[mine, :].astype(F32) * (1.0 / 16)
+        old, old_momentum = params[at, :], momentum[at, :]
+        moment = 0.9 * old_momentum + pseudo
+        stepped = old - 0.7 * (pseudo + 0.9 * moment)
+        on = jnp.concatenate([due[at, :]] * (old.shape[1] // 128), axis=1) == 1
+        params_out[mine, :] = jnp.where(on, stepped, old)
+        momentum_out[mine, :] = jnp.where(on, moment, old_momentum)
+        kept = local[at, :].astype(F32)
+        local_out[mine, :] = jnp.where(on, stepped + (kept - snap[at, :].astype(F32)), kept).astype(BF16)
+        for store in stores(i):
+            store.start()
+
+    @pl.loop(0, 4)
+    def _(i):
+        for store in stores(i):
+            store.wait()
 
 
 def outer(half, total, params, momentum, snap, local, due, into=()):
-    width = params.shape[1]
-    whole = pl.BlockSpec((16, width), lambda i, h: (h[0] * 4 + i, 0))
-    part = pl.BlockSpec((16, width), lambda i, h: (i, 0))
+    rows, width = total.shape
     return pl.pallas_call(
         outer_kernel,
         out_shape=[
@@ -281,18 +332,19 @@
             pltpu.HBM(params.shape, F32),
             pltpu.HBM(params.shape, BF16),
         ],
-        grid_spec=pltpu.PrefetchScalarGridSpec(
-            num_scalar_prefetch=1,
-            grid=(4,),
-            in_specs=[part, whole, whole, whole, whole, pl.BlockSpec((16, 128), lambda i, h: (h[0] * 4 + i, 0))]
-            + [ANY] * len(into),
-            out_specs=[whole, whole, whole],
-        ),
+        in_specs=[pl.BlockSpec(memory_space=pltpu.SMEM)] + [VM] * 6 + [ANY] * len(into),
+        out_specs=[ANY] * 3,
+        scratch_shapes=[
+            pltpu.VMEM((rows, width), F32),
+            pltpu.VMEM((rows, width), F32),
+            pltpu.VMEM((rows, width), BF16),
+            pltpu.SemaphoreType.DMA((12,)),
+        ],
         input_output_aliases={7 + i: i for i in range(len(into))},
         compiler_params=pltpu.CompilerParams(vmem_limit_bytes=16 << 20),
         cost_estimate=pl.CostEstimate(flops=5 << 20, bytes_accessed=12 << 20, transcendentals=0),
         name="outer",
-    )(half[None], total, params, momentum, snap, local, due, *into)
+    )(half[None], *[vmem(a) for a in (total, params, momentum, snap, local, due)], *into)
 
 
 def after(array, others):
@@ -364,14 +416,18 @@
     octet, *rest = lax.cond(always, along_y, no_along_y, after(pair, sends), block_ids)
     got += [to_owner(a, dx, dz) for a, (dx, dz) in zip(rest, SHIFTS[FIRST:])]
     total, acc = lax.cond(always, along_x, no_along_x, after(octet, got[:2]), [rest[-1], *got[:2]])
-    rows, acc = lax.cond(always, back, no_back, after(total, got[2:FIRST]), got[2:FIRST], acc)
-    rows = after(rows, got[FIRST:])
+    rows, acc = lax.cond(always, back, no_back, after(total, got[2:EARLY]), got[2:EARLY], acc)
+    left, right = hold(acc, (left, right))
+    rows = after(rows, [*got[EARLY:], left])
     rows = joined(rows, to_y(rows, (1, 3)), at_a)
-    update, first_next, second_next = final(got[FIRST:], acc, left, right, first_moment[0, 0], second_moment[0, 0])
+    carried = (outer_params, outer_momentum, snapshot[0], local_params[0])
+    update, first_next, second_next, *carried = final(
+        got[EARLY:], acc, left, right, first_moment[0, 0], second_moment[0, 0], carried
+    )
     rows = after(rows, [update])
     other = to_core(rows)
     due = jnp.broadcast_to(due_rows[:, None], (due_rows.shape[0], 128))
-    state = (outer_params, outer_momentum, snapshot[0], local_params[0], due)
+    state = (*carried, due)
     halves = outer(core, rows, *state)
     outer_next, momentum_next, local_next = outer(1 - core, other, *state, into=halves)
     return (

time: 95.2 us -> 92.4 us (0.971)
  waiting for transfers between devices: 18.1 us -> 15.3 us
  other arithmetic: 5.91 us -> 6.96 us
    ppermute x14, waiting for transfers between devices: 18.1 us -> 15.3 us  [moved(): lax.ppermute(array, AXES, [(s, index_of(*where(*place(s)))) for s in rang...]
    pallas_call x0 -> x1, Pallas kernels: none -> 2.24 us  [hold(): pl.pallas_call(hold_kernel, out_shape=[pltpu.VMEM(a.shape, a.dtype) for a...]
    pallas_call x1, Pallas kernels: 14.8 us -> 13.7 us  [final(): pl.pallas_call(functools.partial(final_kernel, n), out_shape=[square] * 3...]
    select_n x2, other arithmetic: 0.26 us -> 1.31 us  [joined(): lax.select(at == 0, jnp.concatenate([mine, other]), jnp.concatenate([othe...]
    pallas_call x2, Pallas kernels: 6.34 us -> 5.34 us  [outer(): pl.pallas_call(outer_kernel, out_shape=[pltpu.HBM(params.shape, F32), plt...]
  transfers between devices with their start and end apart: 14 -> 14, of which waited for: 4 -> 4; matrix products, arithmetic and copies ran while one was open for 5% -> 6% of each run, Pallas kernels for 41% -> 43%
where the time goes in v4:
time: 92.4 us; the launch traced here: 92.1 us
  Pallas kernels  42 us (45%)
  starting transfers between devices  25.1 us (27%)
  waiting for transfers between devices  15.3 us (17%)
  other arithmetic  6.96 us (8%)
  local copies, waits for them, and re-layouts  1.74 us (2%)
    ppermute x14, starting transfers between devices, moved(): lax.ppermute(array, AXES, [(s, index_of(*where(*place(s)))) for s in rang...  25.1 us
    ppermute x14, waiting for transfers between devices, moved(): lax.ppermute(array, AXES, [(s, index_of(*where(*place(s)))) for s in rang...  15.3 us
    pallas_call x2, Pallas kernels, early(): pl.pallas_call(functools.partial(early_kernel, n, len(acc)), out_shape=pl...  14.7 us
    pallas_call x1, Pallas kernels, final(): pl.pallas_call(functools.partial(final_kernel, n), out_shape=[square] * 3...  13.7 us
    pallas_call x2, Pallas kernels, pick(): pl.pallas_call(functools.partial(pick_kernel, shifts), out_shape=[pltpu.H...  6.04 us
    pallas_call x2, Pallas kernels, outer(): pl.pallas_call(outer_kernel, out_shape=[pltpu.HBM(params.shape, F32), plt...  5.34 us
    convert_element_type x4, other arithmetic, added(): return (one.astype(F32) + two.astype(F32)).astype(BF16)  3.61 us
    pallas_call x1, Pallas kernels, hold(): pl.pallas_call(hold_kernel, out_shape=[pltpu.VMEM(a.shape, a.dtype) for a...  2.24 us
  transfers between devices with their start and end apart: 14, of which 4 were waited for; matrix products, arithmetic and copies ran while one was open for 6% of the time, Pallas kernels for 43%

profile of v4, /device:TPU:1, one launch (start us, length us, event | category | flops | bytes accessed | tf_op | source)
XLA Modules:
  0.0 92.1 jit_solution(6980234628072652888)
XLA Ops:
  0.6 0.0 copy-start.6
  0.7 2.0 %fusion = bf16[64,8192]{1,0:T(8,128)(2,1)S(1)} fusion(f32[128,8192]{1,0:T(8,128)} %refs_8_.1, s32[]{:T(128)S(6)} %select_n.58, bf16[1,128,8192]{2,1,0:T(8,128)(2,1)} %param.27), kind=kLoop, calls=%fused_computation.8 | loop fusion | flops 1572864 | bytes 4194308 | tf_op jit(solution)/shard_map/convert_element_type | solution.py:389
  2.7 0.0 copy-start.2
  2.7 1.5 %collective-permute-start.4 = (bf16[64,8192]{1,0:T(8,128)(2,1)S(1)}, bf16[64,8192]{1,0:T(8,128)(2,1)}, u32[]{:S(2)}, u32[]{:S(2)}) collective-permute-start(bf16[64,8192]{1,0:T(8,128)(2,1)S(1)} %fusion), channel_id=1, source_target_pairs={{0,8},{1,9},{2,10},{3,11},{4,12},{5,13},{6,14},{7,15},{8,0},{9,1},... | collective-permute-start | bytes 3145736 | tf_op jit(solution)/shard_map/ppermute | solution.py:34
  4.2 0.0 copy-done.6
  4.2 3.0 %pick.3 = (bf16[128,2048]{1,0:T(8,128)(2,1)}, bf16[128,2048]{1,0:T(8,128)(2,1)}, bf16[128,2048]{1,0:T(8,128)(2,1)}, bf16[128,2048]{1,0:T(8,128)(2,1)}) custom-call(s32[8]{0:T(128)S(1)} %copy-done.6, bf16[128,4096]{1,0:T(8,128)(2,1)} %tokens.1, bf16[128,14336]{1,0:T(8,128)(2,1)} %out_grads.1), custom_call_target="tpu_custom_call" | custom-call | bytes 8388608 | tf_op jit(solution)/shard_map/pick/pallas_call | solution.py:91
  7.2 6.2 %collective-permute-start.5 = (bf16[128,2048]{1,0:T(8,128)(2,1)}, bf16[128,2048]{1,0:T(8,128)(2,1)}, u32[]{:S(2)}, u32[]{:S(2)}) collective-permute-start(bf16[128,2048]{1,0:T(8,128)(2,1)} %get-tuple-element.103), channel_id=1, source_target_pairs={{0,6},{1,7},{2,4},{3,5},{4,2},{5,3},{6,0},{7,1},{8,14},{9,15},{10,... | collective-permute-start | bytes 1572872 | tf_op jit(solution)/shard_map/ppermute | solution.py:34
  13.5 0.7 collective-permute-start.6
  14.1 4.4 %collective-permute-start.7 = (bf16[128,2048]{1,0:T(8,128)(2,1)}, bf16[128,2048]{1,0:T(8,128)(2,1)}, u32[]{:S(2)}, u32[]{:S(2)}) collective-permute-start(bf16[128,2048]{1,0:T(8,128)(2,1)} %get-tuple-element.105), channel_id=1, source_target_pairs={{0,7},{1,4},{2,5},{3,6},{4,3},{5,0},{6,1},{7,2},{8,15},{9,12},{10,... | collective-permute-start | bytes 1572872 | tf_op jit(solution)/shard_map/ppermute | solution.py:34
  18.5 0.0 collective-permute-start.8
  18.5 0.0 collective-permute-done.4
  18.5 0.0 copy-done.2
  18.6 2.2 %add_convert_fusion.3 = bf16[64,8192]{1,0:T(8,128)(2,1)S(1)} fusion(bf16[64,8192]{1,0:T(8,128)(2,1)} %collective-permute-done.4, f32[128,8192]{1,0:T(8,128)} %refs_8_.1, s32[]{:T(128)S(6)} %select_n.57, bf16[1,128,8192]{2,1,0:T(8,128)(2,1)S(1)} %copy-done.2), kind=kLoop, calls=%fused_computation.11 | loop fusion | flops 3670016 | bytes 5242884 | tf_op jit(solution)/shard_map/convert_element_type | solution.py:355
  20.8 0.0 copy-start
  20.8 18.5 %conditional.3 = (bf16[16,8192]{1,0:T(8,128)(2,1)S(1)}, bf16[128,2048]{1,0:T(8,128)(2,1)}, bf16[128,2048]{1,0:T(8,128)(2,1)}, bf16[128,2048]{1,0:T(8,128)(2,1)}, bf16[128,2048]{1,0:T(8,128)(2,1)}) conditional(s32[]{:T(128)} %convert_element_type.59, bf16[64,8192]{1,0:T(8,128)(2,1)S(1)} %add_convert_fusion.3, (s32[]{:T(128)}, ...), branch_computations={%region_0.1_spmd, %region_1.2_spmd} | conditional | flops 1572882 | bytes 19661200 | solution.py:416
  20.8 0.8 constant_dynamic-slice_fusion.1
  21.7 2.7 %collective-permute-start = (bf16[32,8192]{1,0:T(8,128)(2,1)}, bf16[32,8192]{1,0:T(8,128)(2,1)}, u32[]{:S(2)}, u32[]{:S(2)}) collective-permute-start(bf16[32,8192]{1,0:T(8,128)(2,1)} %constant_dynamic-slice_fusion.1), channel_id=1, source_target_pairs={{0,32},{1,33},{2,34},{3,35},{4,36},{5,37},{6,38},{7,39},{8,104},{9... | collective-permute-start | bytes 1572872 | tf_op jit(solution)/shard_map/cond/branch_1_fun/ppermute | solution.py:34
  24.4 7.2 %collective-permute-done = bf16[32,8192]{1,0:T(8,128)(2,1)} collective-permute-done((bf16[32,8192]{1,0:T(8,128)(2,1)}, bf16[32,8192]{1,0:T(8,128)(2,1)}, u32[]{:S(2)}, u32[]{:S(2)}) %collective-permute-start) | collective-permute-done | bytes 524320 | tf_op jit(solution)/shard_map/cond/branch_1_fun/ppermute | solution.py:34
  31.6 1.2 %add_convert_fusion = bf16[32,8192]{1,0:T(8,128)(2,1)S(1)} fusion(bf16[32,8192]{1,0:T(8,128)(2,1)} %collective-permute-done, bf16[64,8192]{1,0:T(8,128)(2,1)S(1)} %get-tuple-element.41, s32[]{:T(128)S(6)} %select_n.40), kind=kLoop, calls=%fused_computation | loop fusion | flops 1048576 | bytes 1572868 | tf_op jit(solution)/shard_map/cond/branch_1_fun/convert_element_type | solution.py:355
  32.7 0.0 copy-start.3
  32.7 0.8 copy-done.3
  33.5 0.1 collective-permute-start.1
  33.6 0.0 copy-start.4
  33.7 3.0 %pick.2 = (bf16[128,2048]{1,0:T(8,128)(2,1)}, bf16[128,2048]{1,0:T(8,128)(2,1)}, bf16[128,2048]{1,0:T(8,128)(2,1)}, bf16[128,2048]{1,0:T(8,128)(2,1)}) custom-call(s32[8]{0:T(128)S(1)} %get-tuple-element.44.ids, bf16[128,4096]{1,0:T(8,128)(2,1)} %get-tuple-element.45.tokens, bf16[128,14336]{1,0:T(8,128)(2,1)} %get-tuple-element.46.out_grads), custom_call_target="tpu_custom_call" | custom-call | bytes 8388608 | tf_op jit(solution)/shard_map/cond/branch_1_fun/pick/pallas_call | solution.py:91
  36.7 2.6 %collective-permute-done.1 = bf16[16,8192]{1,0:T(8,128)(2,1)S(1)} collective-permute-done((bf16[16,8192]{1,0:T(8,128)(2,1)S(1)}, bf16[16,8192]{1,0:T(8,128)(2,1)S(1)}, u32[]{:S(2)}, u32[]{:S(2)}) %collective-permute-start.1) | collective-permute-done | bytes 262176 | tf_op jit(solution)/shard_map/cond/branch_1_fun/ppermute | solution.py:34
  39.2 0.0 copy-done.4
  39.2 0.1 add_convert_fusion.1
  39.3 0.0 collective-permute-done.5
  39.3 0.0 collective-permute-done.6
  39.3 0.1 collective-permute-start.9
  39.4 2.7 %collective-permute-start.10 = (bf16[128,2048]{1,0:T(8,128)(2,1)}, bf16[128,2048]{1,0:T(8,128)(2,1)}, u32[]{:S(2)}, u32[]{:S(2)}) collective-permute-start(bf16[128,2048]{1,0:T(8,128)(2,1)} %get-tuple-element.118), channel_id=1, source_target_pairs={{0,3},{1,0},{2,1},{3,2},{4,7},{5,4},{6,5},{7,6},{8,11},{9,8},{10,9... | collective-permute-start | bytes 1572872 | tf_op jit(solution)/shard_map/ppermute | solution.py:34
  42.1 0.0 copy-done
  42.1 12.7 %conditional.4 = (bf16[16,8192]{1,0:T(8,128)(2,1)S(1)}, f32[1024,1024]{1,0:T(8,128)}) conditional(s32[]{:T(128)} %convert_element_type.59, bf16[16,8192]{1,0:T(8,128)(2,1)S(1)} %get-tuple-element.109, (bf16[16,8192]{1,0:T(8,128)(2,1)S(1)}, bf16[128,2048]{1,0:T(8,128)(2,1)}, bf16[128,2048]{1,0:T(8,128)(2,1)}, bf16[128,2048]{1,0:T(8,128)(2,1)}, ...), branch_computations={%region_2.3_spmd, %region_3.4_spmd} | conditional | flops 2416443392 | bytes 6029368 | solution.py:418
  42.1 0.3 collective-permute-start.2
  42.4 7.6 %early.2 = f32[1024,1024]{1,0:T(8,128)} custom-call(bf16[128,2048]{1,0:T(8,128)(2,1)} %get-tuple-element.52.refs_0_, bf16[128,2048]{1,0:T(8,128)(2,1)} %get-tuple-element.53.refs_1_, bf16[128,2048]{1,0:T(8,128)(2,1)} %get-tuple-element.54.refs_2_, bf16[1024,1024]{1,0:T(8,128)(2,1)S(1)} %get-tuple-element.55.refs_3_, bf16[1024,1024]{1,0:T(8,128)(2,1)} %get-tuple-element.56.refs_4_), custom_call_target="tpu_custom_call" | custom-call | flops 2415919104 | bytes 4194304 | tf_op jit(solution)/shard_map/cond/branch_1_fun/early/pallas_call | solution.py:157
  50.0 4.7 %collective-permute-done.2 = bf16[16,8192]{1,0:T(8,128)(2,1)S(1)} collective-permute-done((bf16[16,8192]{1,0:T(8,128)(2,1)S(1)}, bf16[16,8192]{1,0:T(8,128)(2,1)S(1)}, u32[]{:S(2)}, u32[]{:S(2)}) %collective-permute-start.2) | collective-permute-done | bytes 262176 | tf_op jit(solution)/shard_map/cond/branch_1_fun/ppermute | solution.py:34
  54.7 0.2 add_convert_fusion.2
  54.8 1.8 %collective-permute-start.11 = (bf16[128,2048]{1,0:T(8,128)(2,1)}, bf16[128,2048]{1,0:T(8,128)(2,1)}, u32[]{:S(2)}, u32[]{:S(2)}) collective-permute-start(bf16[128,2048]{1,0:T(8,128)(2,1)} %get-tuple-element.119), channel_id=1, source_target_pairs={{0,4},{1,5},{2,6},{3,7},{4,0},{5,1},{6,2},{7,3},{8,12},{9,13},{10,... | collective-permute-start | bytes 1572872 | tf_op jit(solution)/shard_map/ppermute | solution.py:34
  56.6 0.0 collective-permute-done.7
  56.7 0.0 collective-permute-done.8
  56.7 9.7 %conditional.5 = (bf16[32,8192]{1,0:T(8,128)(2,1)S(1)}, f32[1024,1024]{1,0:T(8,128)}) conditional(s32[]{:T(128)} %convert_element_type.59, bf16[16,8192]{1,0:T(8,128)(2,1)S(1)} %get-tuple-element.112, (s32[]{:T(128)}, bf16[16,8192]{1,0:T(8,128)(2,1)S(1)}, bf16[128,2048]{1,0:T(8,128)(2,1)}, bf16[128,2048]{1,0:T(8,128)(2,1)}, ...), branch_computations={%region_4.5_spmd, %region_5.6_spmd} | conditional | flops 1612972032 | bytes 14680158 | solution.py:419
  56.7 0.0 copy-start.1
  56.7 1.4 %collective-permute-start.3 = (bf16[16,8192]{1,0:T(8,128)(2,1)S(1)}, bf16[16,8192]{1,0:T(8,128)(2,1)}, u32[]{:S(2)}, u32[]{:S(2)}) collective-permute-start(bf16[16,8192]{1,0:T(8,128)(2,1)S(1)} %get-tuple-element.58), channel_id=1, source_target_pairs={{0,96},{1,97},{2,98},{3,99},{4,100},{5,101},{6,102},{7,103},{8,40}... | collective-permute-start | bytes 786440 | tf_op jit(solution)/shard_map/cond/branch_1_fun/ppermute | solution.py:34
  58.0 0.0 copy-done.1
  58.0 7.1 %early.3 = f32[1024,1024]{1,0:T(8,128)} custom-call(bf16[128,2048]{1,0:T(8,128)(2,1)} %get-tuple-element.59.refs_0_, bf16[128,2048]{1,0:T(8,128)(2,1)} %get-tuple-element.60.refs_1_, bf16[1024,1024]{1,0:T(8,128)(2,1)} %copy-done.1, bf16[1024,1024]{1,0:T(8,128)(2,1)} %get-tuple-element.62.refs_3_, f32[1024,1024]{1,0:T(8,128)} %get-tuple-element.63.refs_4_), custom_call_target="tpu_custom_call" | custom-call | flops 1610612736 | bytes 4194304 | tf_op jit(solution)/shard_map/cond/branch_1_fun/early/pallas_call | solution.py:157
  65.2 0.0 collective-permute-done.3
  65.2 1.1 %maximum_select_fusion = bf16[32,8192]{1,0:T(8,128)(2,1)S(1)} fusion(bf16[16,8192]{1,0:T(8,128)(2,1)} %collective-permute-done.3, bf16[16,8192]{1,0:T(8,128)(2,1)S(1)} %get-tuple-element.58, pred[]{:T(512)S(6)} %eq.10), kind=kLoop, calls=%fused_computation.6 | loop fusion | flops 2359296 | bytes 1048577 | tf_op jit(solution)/shard_map/cond/branch_1_fun/select_n | solution.py:359
  66.3 2.2 %hold.1 = (bf16[1024,1024]{1,0:T(8,128)(2,1)S(1)}, bf16[1024,1024]{1,0:T(8,128)(2,1)S(1)}) custom-call(f32[1024,1024]{1,0:T(8,128)} %get-tuple-element.114.gate.refs_5_, bf16[1024,1024]{1,0:T(8,128)(2,1)} %bitcast.18, bf16[1024,1024]{1,0:T(8,128)(2,1)} %bitcast.23), custom_call_target="tpu_custom_call" | custom-call | bytes 8388608 | tf_op jit(solution)/shard_map/hold/pallas_call | solution.py:187
  68.6 0.0 collective-permute-done.9.refs_2_
  68.6 0.0 copy-start.5
  68.6 0.0 collective-permute-done.10.refs_3_
  68.6 0.9 collective-permute-done.11.refs_4_
  69.5 2.7 %collective-permute-start.12 = (bf16[32,8192]{1,0:T(8,128)(2,1)S(1)}, bf16[32,8192]{1,0:T(8,128)(2,1)S(1)}, u32[]{:S(2)}, u32[]{:S(2)}) collective-permute-start(bf16[32,8192]{1,0:T(8,128)(2,1)S(1)} %get-tuple-element.124), channel_id=1, source_target_pairs={{0,32},{1,33},{2,34},{3,35},{4,36},{5,37},{6,38},{7,39},{8,104},{9... | collective-permute-start | bytes 1572872 | tf_op jit(solution)/shard_map/ppermute | solution.py:34
  72.2 0.0 copy-done.5
  72.2 13.7 %final.1 = (bf16[1024,1024]{1,0:T(8,128)(2,1)}, bf16[1024,1024]{1,0:T(8,128)(2,1)}, bf16[1024,1024]{1,0:T(8,128)(2,1)}, f32[128,8192]{1,0:T(8,128)S(1)}, f32[128...) custom-call(bf16[1024,1024]{1,0:T(8,128)(2,1)S(1)} %get-tuple-element.115.refs_0_, ...), custom_call_target="tpu_custom_call" | custom-call | flops 6710886400 | bytes 6291456 | tf_op jit(solution)/shard_map/final/pallas_call | solution.py:270
  85.9 0.0 copy-start.7
  85.9 0.0 collective-permute-done.12
  85.9 0.2 maximum_select_fusion.1.total
  86.1 0.5 collective-permute-start.13
  86.6 0.0 copy-done.7
  86.6 0.1 broadcast_in_dim.28.due
  86.7 2.7 %outer.2 = (f32[128,8192]{1,0:T(8,128)}, f32[128,8192]{1,0:T(8,128)}, bf16[128,8192]{1,0:T(8,128)(2,1)}) custom-call(s32[1]{0:T(128)} %bitcast.12.half, bf16[64,8192]{1,0:T(8,128)(2,1)S(1)} %maximum_select_fusion.1.total, f32[128,8192]{1,0:T(8,128)S(1)} %get-tuple-element.126.params, f32[128,8192]{1,0:T(8,128)S(1)} %get-tuple-element.127.momentum, ...), custom_call_target="tpu_custom_call" | custom-call | flops 5242880 | bytes 12582912 | tf_op jit(solution)/shard_map/outer/pallas_call | solution.py:328
  89.4 0.0 collective-permute-done.13.total
  89.4 2.7 %outer.3 = (f32[128,8192]{1,0:T(8,128)}, f32[128,8192]{1,0:T(8,128)}, bf16[128,8192]{1,0:T(8,128)(2,1)}) custom-call(s32[1]{0:T(128)} %bitcast.11.half, bf16[64,8192]{1,0:T(8,128)(2,1)S(1)} %collective-permute-done.13.total, f32[128,8192]{1,0:T(8,128)S(1)} %get-tuple-element.126.params, ...), custom_call_target="tpu_custom_call", output_to_operand_aliasing={{0}: (7, {}), {1}: (8, {}), {2}: (9, {})} | custom-call | flops 5242880 | bytes 12582912 | tf_op jit(solution)/shard_map/outer/pallas_call | solution.py:328
  (1 shorter events, 0.0 us)
Async XLA Ops:
  0.6 3.6 %copy-start.6 = (s32[8]{0:T(128)S(1)}, s32[8]{0:T(128)}, u32[]{:S(2)}) copy-start(s32[8]{0:T(128)} %ids.1) | copy-start | bytes 100
  2.7 15.8 %copy-start.2 = (bf16[1,128,8192]{2,1,0:T(8,128)(2,1)S(1)}, bf16[1,128,8192]{2,1,0:T(8,128)(2,1)}, u32[]{:S(2)}) copy-start(bf16[1,128,8192]{2,1,0:T(8,128)(2,1)} %param.27) | copy-start | bytes 6291460
  2.7 15.8 %collective-permute-start.4 = (bf16[64,8192]{1,0:T(8,128)(2,1)S(1)}, bf16[64,8192]{1,0:T(8,128)(2,1)}, u32[]{:S(2)}, u32[]{:S(2)}) collective-permute-start(bf16[64,8192]{1,0:T(8,128)(2,1)S(1)} %fusion), channel_id=1, source_target_pairs={{0,8},{1,9},{2,10},{3,11},{4,12},{5,13},{6,14},{7,15},{8,0},{9,1},... | collective-permute-start | bytes 3145736 | tf_op jit(solution)/shard_map/ppermute | solution.py:34
  7.2 32.1 %collective-permute-start.5 = (bf16[128,2048]{1,0:T(8,128)(2,1)}, bf16[128,2048]{1,0:T(8,128)(2,1)}, u32[]{:S(2)}, u32[]{:S(2)}) collective-permute-start(bf16[128,2048]{1,0:T(8,128)(2,1)} %get-tuple-element.103), channel_id=1, source_target_pairs={{0,6},{1,7},{2,4},{3,5},{4,2},{5,3},{6,0},{7,1},{8,14},{9,15},{10,... | collective-permute-start | bytes 1572872 | tf_op jit(solution)/shard_map/ppermute | solution.py:34
  13.5 25.9 %collective-permute-start.6 = (bf16[128,2048]{1,0:T(8,128)(2,1)}, bf16[128,2048]{1,0:T(8,128)(2,1)}, u32[]{:S(2)}, u32[]{:S(2)}) collective-permute-start(bf16[128,2048]{1,0:T(8,128)(2,1)} %get-tuple-element.104), channel_id=1, source_target_pairs={{0,5},{1,6},{2,7},{3,4},{4,1},{5,2},{6,3},{7,0},{8,13},{9,14},{10,... | collective-permute-start | bytes 1572872 | tf_op jit(solution)/shard_map/ppermute | solution.py:34
  14.1 42.5 %collective-permute-start.7 = (bf16[128,2048]{1,0:T(8,128)(2,1)}, bf16[128,2048]{1,0:T(8,128)(2,1)}, u32[]{:S(2)}, u32[]{:S(2)}) collective-permute-start(bf16[128,2048]{1,0:T(8,128)(2,1)} %get-tuple-element.105), channel_id=1, source_target_pairs={{0,7},{1,4},{2,5},{3,6},{4,3},{5,0},{6,1},{7,2},{8,15},{9,12},{10,... | collective-permute-start | bytes 1572872 | tf_op jit(solution)/shard_map/ppermute | solution.py:34
  18.5 38.1 %collective-permute-start.8 = (bf16[128,2048]{1,0:T(8,128)(2,1)}, bf16[128,2048]{1,0:T(8,128)(2,1)}, u32[]{:S(2)}, u32[]{:S(2)}) collective-permute-start(bf16[128,2048]{1,0:T(8,128)(2,1)} %get-tuple-element.106), channel_id=1, source_target_pairs={{0,2},{1,3},{2,0},{3,1},{4,6},{5,7},{6,4},{7,5},{8,10},{9,11},{10,... | collective-permute-start | bytes 1572872 | tf_op jit(solution)/shard_map/ppermute | solution.py:34
  20.8 21.3 %copy-start = (bf16[1,1,1024,1024]{3,2,1,0:T(8,128)(2,1)S(1)}, bf16[1,1,1024,1024]{3,2,1,0:T(8,128)(2,1)}, u32[]{:S(2)}) copy-start(bf16[1,1,1024,1024]{3,2,1,0:T(8,128)(2,1)} %param.21) | copy-start | bytes 6291460
  21.7 9.9 %collective-permute-start = (bf16[32,8192]{1,0:T(8,128)(2,1)}, bf16[32,8192]{1,0:T(8,128)(2,1)}, u32[]{:S(2)}, u32[]{:S(2)}) collective-permute-start(bf16[32,8192]{1,0:T(8,128)(2,1)} %constant_dynamic-slice_fusion.1), channel_id=1, source_target_pairs={{0,32},{1,33},{2,34},{3,35},{4,36},{5,37},{6,38},{7,39},{8,104},{9... | collective-permute-start | bytes 1572872 | tf_op jit(solution)/shard_map/cond/branch_1_fun/ppermute | solution.py:34
  32.7 0.8 copy-start.3
  33.5 5.7 %collective-permute-start.1 = (bf16[16,8192]{1,0:T(8,128)(2,1)S(1)}, bf16[16,8192]{1,0:T(8,128)(2,1)S(1)}, u32[]{:S(2)}, u32[]{:S(2)}) collective-permute-start(bf16[16,8192]{1,0:T(8,128)(2,1)S(1)} %constant_dynamic-slice_fusion), channel_id=1, source_target_pairs={{0,96},{1,97},{2,98},{3,99},{4,100},{5,101},{6,102},{7,103},{8,40}... | collective-permute-start | bytes 786440 | tf_op jit(solution)/shard_map/cond/branch_1_fun/ppermute | solution.py:34
  33.6 5.6 %copy-start.4 = (bf16[32,8192]{1,0:T(8,128)(2,1)S(1)}, bf16[32,8192]{1,0:T(8,128)(2,1)}, u32[]{:S(2)}) copy-start(bf16[32,8192]{1,0:T(8,128)(2,1)} %copy-done.3) | copy-start | bytes 1572868 | tf_op jit(solution)/shard_map/cond
  39.3 29.2 %collective-permute-start.9 = (bf16[128,2048]{1,0:T(8,128)(2,1)}, bf16[128,2048]{1,0:T(8,128)(2,1)S(1)}, u32[]{:S(2)}, u32[]{:S(2)}) collective-permute-start(bf16[128,2048]{1,0:T(8,128)(2,1)} %get-tuple-element.117), channel_id=1, source_target_pairs={{0,1},{1,2},{2,3},{3,0},{4,5},{5,6},{6,7},{7,4},{8,9},{9,10},{10,1... | collective-permute-start | bytes 1572872 | tf_op jit(solution)/shard_map/ppermute | solution.py:34
  39.4 29.2 %collective-permute-start.10 = (bf16[128,2048]{1,0:T(8,128)(2,1)}, bf16[128,2048]{1,0:T(8,128)(2,1)}, u32[]{:S(2)}, u32[]{:S(2)}) collective-permute-start(bf16[128,2048]{1,0:T(8,128)(2,1)} %get-tuple-element.118), channel_id=1, source_target_pairs={{0,3},{1,0},{2,1},{3,2},{4,7},{5,4},{6,5},{7,6},{8,11},{9,8},{10,9... | collective-permute-start | bytes 1572872 | tf_op jit(solution)/shard_map/ppermute | solution.py:34
  42.1 12.6 %collective-permute-start.2 = (bf16[16,8192]{1,0:T(8,128)(2,1)S(1)}, bf16[16,8192]{1,0:T(8,128)(2,1)S(1)}, u32[]{:S(2)}, u32[]{:S(2)}) collective-permute-start(bf16[16,8192]{1,0:T(8,128)(2,1)S(1)} %get-tuple-element.51), channel_id=1, source_target_pairs={{0,16},{1,17},{2,18},{3,19},{4,20},{5,21},{6,22},{7,23},{8,24},{9,... | collective-permute-start | bytes 786440 | tf_op jit(solution)/shard_map/cond/branch_1_fun/ppermute | solution.py:34
  54.8 14.7 %collective-permute-start.11 = (bf16[128,2048]{1,0:T(8,128)(2,1)}, bf16[128,2048]{1,0:T(8,128)(2,1)}, u32[]{:S(2)}, u32[]{:S(2)}) collective-permute-start(bf16[128,2048]{1,0:T(8,128)(2,1)} %get-tuple-element.119), channel_id=1, source_target_pairs={{0,4},{1,5},{2,6},{3,7},{4,0},{5,1},{6,2},{7,3},{8,12},{9,13},{10,... | collective-permute-start | bytes 1572872 | tf_op jit(solution)/shard_map/ppermute | solution.py:34
  56.7 1.4 %copy-start.1 = (bf16[1024,1024]{1,0:T(8,128)(2,1)}, bf16[1024,1024]{1,0:T(8,128)(2,1)S(1)}, u32[]{:S(2)}) copy-start(bf16[1024,1024]{1,0:T(8,128)(2,1)S(1)} %get-tuple-element.61.refs_2_) | copy-start | bytes 6291460 | tf_op jit(solution)/shard_map/cond
  56.7 8.5 %collective-permute-start.3 = (bf16[16,8192]{1,0:T(8,128)(2,1)S(1)}, bf16[16,8192]{1,0:T(8,128)(2,1)}, u32[]{:S(2)}, u32[]{:S(2)}) collective-permute-start(bf16[16,8192]{1,0:T(8,128)(2,1)S(1)} %get-tuple-element.58), channel_id=1, source_target_pairs={{0,96},{1,97},{2,98},{3,99},{4,100},{5,101},{6,102},{7,103},{8,40}... | collective-permute-start | bytes 786440 | tf_op jit(solution)/shard_map/cond/branch_1_fun/ppermute | solution.py:34
  68.6 3.6 %copy-start.5 = (bf16[128,2048]{1,0:T(8,128)(2,1)}, bf16[128,2048]{1,0:T(8,128)(2,1)S(1)}, u32[]{:S(2)}) copy-start(bf16[128,2048]{1,0:T(8,128)(2,1)S(1)} %collective-permute-done.9.refs_2_) | copy-start | bytes 1572868
  69.5 16.4 %collective-permute-start.12 = (bf16[32,8192]{1,0:T(8,128)(2,1)S(1)}, bf16[32,8192]{1,0:T(8,128)(2,1)S(1)}, u32[]{:S(2)}, u32[]{:S(2)}) collective-permute-start(bf16[32,8192]{1,0:T(8,128)(2,1)S(1)} %get-tuple-element.124), channel_id=1, source_target_pairs={{0,32},{1,33},{2,34},{3,35},{4,36},{5,37},{6,38},{7,39},{8,104},{9... | collective-permute-start | bytes 1572872 | tf_op jit(solution)/shard_map/ppermute | solution.py:34
  85.9 0.7 copy-start.7
  86.1 3.3 %collective-permute-start.13 = (bf16[64,8192]{1,0:T(8,128)(2,1)S(1)}, bf16[64,8192]{1,0:T(8,128)(2,1)S(1)}, u32[]{:S(2)}, u32[]{:S(2)}) collective-permute-start(bf16[64,8192]{1,0:T(8,128)(2,1)S(1)} %maximum_select_fusion.1.total), channel_id=1, source_target_pairs={{0,8},{1,9},{2,10},{3,11},{4,12},{5,13},{6,14},{7,15},{8,0},{9,1},... | collective-permute-start | bytes 3145736 | tf_op jit(solution)/shard_map/ppermute | solution.py:34

commit v5 on v4

--- a/solution.py
+++ b/solution.py
@@ -105,14 +105,11 @@
 
 
 def rotate(bufs, left, right, yt, zz):
-    step = 256
-
-    @pl.loop(0, BLOCK // step)
-    def _(j):
-        at = pl.ds(pl.multiple_of(j * step, step), step)
-        xs = jnp.concatenate([b[:, :BLOCK] for b in bufs], axis=0)
-        ds = jnp.concatenate([b[:, BLOCK:] for b in bufs], axis=0)
-        yt[at, :] = jnp.dot(xs, left[:, at], preferred_element_type=F32).T.astype(BF16)
+    xs = jnp.concatenate([b[:, :BLOCK] for b in bufs], axis=0)
+    ds = jnp.concatenate([b[:, BLOCK:] for b in bufs], axis=0)
+    for start in range(0, BLOCK, 512):
+        at = slice(start, start + 512)
+        yt[at, :] = jnp.dot(xs, left[:, at], preferred_element_type=F32).astype(BF16).T
         zz[:, at] = jnp.dot(ds, right[:, at], preferred_element_type=F32).astype(BF16)
 
 
@@ -175,7 +172,8 @@
 
 
 def hold_kernel(gate, *refs):
-    sources, outs, sems = refs[:2], refs[2:4], refs[4]
+    n = len(refs) // 2
+    sources, outs, sems = refs[:n], refs[n : 2 * n], refs[2 * n]
     copies = [pltpu.make_async_copy(a, b, sems.at[i]) for i, (a, b) in enumerate(zip(sources, outs))]
     for copy in copies:
         copy.start()
@@ -187,9 +185,9 @@
     return pl.pallas_call(
         hold_kernel,
         out_shape=[pltpu.VMEM(a.shape, a.dtype) for a in arrays],
-        in_specs=[ANY] * 3,
-        out_specs=[VM] * 2,
-        scratch_shapes=[pltpu.SemaphoreType.DMA((2,))],
+        in_specs=[ANY] * (len(arrays) + 1),
+        out_specs=[VM] * len(arrays),
+        scratch_shapes=[pltpu.SemaphoreType.DMA((len(arrays),))],
         compiler_params=pltpu.CompilerParams(vmem_limit_bytes=1 << 20),
         cost_estimate=pl.CostEstimate(flops=0, bytes_accessed=8 << 20, transcendentals=0),
         name="hold",
@@ -197,22 +195,21 @@
 
 
 def final_kernel(n, *refs):
-    left, right, refs = refs[0], refs[1], refs[2:]
-    operands, carried, refs = refs[: n + 3], refs[n + 3 : n + 7], refs[n + 7 :]
+    (left, right, first, second), refs = refs[:4], refs[4:]
+    operands, carried, refs = refs[: n + 1], refs[n + 1 : n + 5], refs[n + 5 :]
     (update, first_next, second_next), kept, refs = refs[:3], refs[3:7], refs[7:]
-    held, yt, zz, direction, m_out, v_out, u_out, acc, first, second, sems, in_sems = refs
-    places = [held.at[i] for i in range(n)] + [acc, first, second]
+    held, yt, zz, direction, m_out, v_out, u_out, acc, sems, in_sems = refs
+    places = [held.at[i] for i in range(n)] + [acc]
     pairs = [*zip(operands, places), *zip(carried, kept)]
     loads = [pltpu.make_async_copy(a, b, in_sems.at[i]) for i, (a, b) in enumerate(pairs)]
-    for load in loads[:n]:
+    for load in loads[: n + 1]:
         load.start()
     for load in loads[:n]:
         load.wait()
-    for load in loads[n:]:
+    rotate(places[:n], left, right, yt, zz)
+    loads[n].wait()
+    for load in loads[n + 1 :]:
         load.start()
-    rotate(places[:n], left, right, yt, zz)
-    for load in loads[n : n + 3]:
-        load.wait()
     rows = 256
 
     def moment_copies(i):
@@ -259,7 +256,7 @@
     def _(i):
         update_copy(i).wait()
 
-    for load in loads[n + 3 :]:
+    for load in loads[n + 1 :]:
         load.wait()
 
 
@@ -270,7 +267,7 @@
     return pl.pallas_call(
         functools.partial(final_kernel, n),
         out_shape=[square] * 3 + [pltpu.VMEM(a.shape, a.dtype) for a in carried],
-        in_specs=[VM] * 2 + [ANY] * (n + 7),
+        in_specs=[VM] * 4 + [ANY] * (n + 5),
         out_specs=[ANY] * 3 + [VM] * 4,
         scratch_shapes=[
             pltpu.VMEM((n, TOK, 2 * BLOCK), BF16),
@@ -278,16 +275,18 @@
             pltpu.VMEM((n * TOK, BLOCK), BF16),
             *[block] * 4,
             pltpu.VMEM((BLOCK, BLOCK), F32),
-            *[block] * 2,
             pltpu.SemaphoreType.DMA((12,)),
-            pltpu.SemaphoreType.DMA((n + 7,)),
+            pltpu.SemaphoreType.DMA((n + 5,)),
         ],
         compiler_params=pltpu.CompilerParams(vmem_limit_bytes=28 << 20),
         cost_estimate=pl.CostEstimate(
             flops=(6 * n * TOK + 4 * BLOCK) * BLOCK * BLOCK, bytes_accessed=6 << 20, transcendentals=2 << 20
         ),
         name="final",
-    )(vmem(left), vmem(right), *[hbm(a) for a in (*bufs, acc, first, second, *carried)])
+    )(
+        *[vmem(a) for a in (left, right, first, second)],
+        *[hbm(a) for a in (*bufs, acc, *carried)],
+    )
 
 
 def outer_kernel(half, total, params, momentum, snap, local, due, *rest):
@@ -417,12 +416,12 @@
     got += [to_owner(a, dx, dz) for a, (dx, dz) in zip(rest, SHIFTS[FIRST:])]
     total, acc = lax.cond(always, along_x, no_along_x, after(octet, got[:2]), [rest[-1], *got[:2]])
     rows, acc = lax.cond(always, back, no_back, after(total, got[2:EARLY]), got[2:EARLY], acc)
-    left, right = hold(acc, (left, right))
+    left, right, first, second = hold(acc, (left, right, first_moment[0, 0], second_moment[0, 0]))
     rows = after(rows, [*got[EARLY:], left])
     rows = joined(rows, to_y(rows, (1, 3)), at_a)
     carried = (outer_params, outer_momentum, snapshot[0], local_params[0])
     update, first_next, second_next, *carried = final(
-        got[EARLY:], acc, left, right, first_moment[0, 0], second_moment[0, 0], carried
+        got[EARLY:], acc, left, right, first, second, carried
     )
     rows = after(rows, [update])
     other = to_core(rows)

time: 92.4 us -> 91.4 us (0.989)
  Pallas kernels: 42 us -> 40.6 us
    pallas_call x1, Pallas kernels: 13.7 us -> 11.9 us  [final(): pl.pallas_call(functools.partial(final_kernel, n), out_shape=[square] * 3...]
    pallas_call x1, Pallas kernels: 2.24 us -> 3.51 us  [hold(): pl.pallas_call(hold_kernel, out_shape=[pltpu.VMEM(a.shape, a.dtype) for a...]
  transfers between devices with their start and end apart: 14 -> 14, of which waited for: 4 -> 3; matrix products, arithmetic and copies ran while one was open for 6% -> 6% of each run, Pallas kernels for 43% -> 42%
where the time goes in v5:
time: 91.4 us; the launch traced here: 91.1 us
  Pallas kernels  40.6 us (44%)
  starting transfers between devices  25.4 us (28%)
  waiting for transfers between devices  15.4 us (17%)
  other arithmetic  6.96 us (8%)
  local copies, waits for them, and re-layouts  1.74 us (2%)
  between operations  0.98 us (1%)
    ppermute x14, starting transfers between devices, moved(): lax.ppermute(array, AXES, [(s, index_of(*where(*place(s)))) for s in rang...  25.4 us
    ppermute x14, waiting for transfers between devices, moved(): lax.ppermute(array, AXES, [(s, index_of(*where(*place(s)))) for s in rang...  15.4 us
    pallas_call x2, Pallas kernels, early(): pl.pallas_call(functools.partial(early_kernel, n, len(acc)), out_shape=pl...  13.8 us
    pallas_call x1, Pallas kernels, final(): pl.pallas_call(functools.partial(final_kernel, n), out_shape=[square] * 3...  11.9 us
    pallas_call x2, Pallas kernels, pick(): pl.pallas_call(functools.partial(pick_kernel, shifts), out_shape=[pltpu.H...  6.04 us
    pallas_call x2, Pallas kernels, outer(): pl.pallas_call(outer_kernel, out_shape=[pltpu.HBM(params.shape, F32), plt...  5.34 us
    convert_element_type x4, other arithmetic, added(): return (one.astype(F32) + two.astype(F32)).astype(BF16)  3.61 us
    pallas_call x1, Pallas kernels, hold(): pl.pallas_call(hold_kernel, out_shape=[pltpu.VMEM(a.shape, a.dtype) for a...  3.51 us
  transfers between devices with their start and end apart: 14, of which 3 were waited for; matrix products, arithmetic and copies ran while one was open for 6% of the time, Pallas kernels for 42%

profile of v5, /device:TPU:1, one launch (start us, length us, event | category | flops | bytes accessed | tf_op | source)
XLA Modules:
  0.0 91.1 jit_solution(17785466562716027960)
XLA Ops:
  0.6 0.0 copy-start.6
  0.7 2.0 %fusion = bf16[64,8192]{1,0:T(8,128)(2,1)S(1)} fusion(f32[128,8192]{1,0:T(8,128)} %refs_8_.1, s32[]{:T(128)S(6)} %select_n.58, bf16[1,128,8192]{2,1,0:T(8,128)(2,1)} %param.27), kind=kLoop, calls=%fused_computation.8 | loop fusion | flops 1572864 | bytes 4194308 | tf_op jit(solution)/shard_map/convert_element_type | solution.py:388
  2.7 0.0 copy-start.2
  2.7 1.5 %collective-permute-start.4 = (bf16[64,8192]{1,0:T(8,128)(2,1)S(1)}, bf16[64,8192]{1,0:T(8,128)(2,1)}, u32[]{:S(2)}, u32[]{:S(2)}) collective-permute-start(bf16[64,8192]{1,0:T(8,128)(2,1)S(1)} %fusion), channel_id=1, source_target_pairs={{0,8},{1,9},{2,10},{3,11},{4,12},{5,13},{6,14},{7,15},{8,0},{9,1},... | collective-permute-start | bytes 3145736 | tf_op jit(solution)/shard_map/ppermute | solution.py:34
  4.2 0.0 copy-done.6
  4.2 3.0 %pick.3 = (bf16[128,2048]{1,0:T(8,128)(2,1)}, bf16[128,2048]{1,0:T(8,128)(2,1)}, bf16[128,2048]{1,0:T(8,128)(2,1)}, bf16[128,2048]{1,0:T(8,128)(2,1)}) custom-call(s32[8]{0:T(128)S(1)} %copy-done.6, bf16[128,4096]{1,0:T(8,128)(2,1)} %tokens.1, bf16[128,14336]{1,0:T(8,128)(2,1)} %out_grads.1), custom_call_target="tpu_custom_call" | custom-call | bytes 8388608 | tf_op jit(solution)/shard_map/pick/pallas_call | solution.py:91
  7.2 6.2 %collective-permute-start.5 = (bf16[128,2048]{1,0:T(8,128)(2,1)}, bf16[128,2048]{1,0:T(8,128)(2,1)}, u32[]{:S(2)}, u32[]{:S(2)}) collective-permute-start(bf16[128,2048]{1,0:T(8,128)(2,1)} %get-tuple-element.105), channel_id=1, source_target_pairs={{0,6},{1,7},{2,4},{3,5},{4,2},{5,3},{6,0},{7,1},{8,14},{9,15},{10,... | collective-permute-start | bytes 1572872 | tf_op jit(solution)/shard_map/ppermute | solution.py:34
  13.5 0.7 collective-permute-start.6
  14.1 4.4 %collective-permute-start.7 = (bf16[128,2048]{1,0:T(8,128)(2,1)}, bf16[128,2048]{1,0:T(8,128)(2,1)}, u32[]{:S(2)}, u32[]{:S(2)}) collective-permute-start(bf16[128,2048]{1,0:T(8,128)(2,1)} %get-tuple-element.107), channel_id=1, source_target_pairs={{0,7},{1,4},{2,5},{3,6},{4,3},{5,0},{6,1},{7,2},{8,15},{9,12},{10,... | collective-permute-start | bytes 1572872 | tf_op jit(solution)/shard_map/ppermute | solution.py:34
  18.5 0.0 collective-permute-start.8
  18.5 0.0 collective-permute-done.4
  18.5 0.0 copy-done.2
  18.6 2.2 %add_convert_fusion.3 = bf16[64,8192]{1,0:T(8,128)(2,1)S(1)} fusion(bf16[64,8192]{1,0:T(8,128)(2,1)} %collective-permute-done.4, f32[128,8192]{1,0:T(8,128)} %refs_8_.1, s32[]{:T(128)S(6)} %select_n.57, bf16[1,128,8192]{2,1,0:T(8,128)(2,1)S(1)} %copy-done.2), kind=kLoop, calls=%fused_computation.11 | loop fusion | flops 3670016 | bytes 5242884 | tf_op jit(solution)/shard_map/convert_element_type | solution.py:354
  20.8 0.0 copy-start
  20.8 18.5 %conditional.3 = (bf16[16,8192]{1,0:T(8,128)(2,1)S(1)}, bf16[128,2048]{1,0:T(8,128)(2,1)}, bf16[128,2048]{1,0:T(8,128)(2,1)}, bf16[128,2048]{1,0:T(8,128)(2,1)}, bf16[128,2048]{1,0:T(8,128)(2,1)}) conditional(s32[]{:T(128)} %convert_element_type.59, bf16[64,8192]{1,0:T(8,128)(2,1)S(1)} %add_convert_fusion.3, (s32[]{:T(128)}, ...), branch_computations={%region_0.1_spmd, %region_1.2_spmd} | conditional | flops 1572882 | bytes 19661200 | solution.py:415
  20.8 0.8 constant_dynamic-slice_fusion.1
  21.7 2.7 %collective-permute-start = (bf16[32,8192]{1,0:T(8,128)(2,1)}, bf16[32,8192]{1,0:T(8,128)(2,1)}, u32[]{:S(2)}, u32[]{:S(2)}) collective-permute-start(bf16[32,8192]{1,0:T(8,128)(2,1)} %constant_dynamic-slice_fusion.1), channel_id=1, source_target_pairs={{0,32},{1,33},{2,34},{3,35},{4,36},{5,37},{6,38},{7,39},{8,104},{9... | collective-permute-start | bytes 1572872 | tf_op jit(solution)/shard_map/cond/branch_1_fun/ppermute | solution.py:34
  24.4 7.2 %collective-permute-done = bf16[32,8192]{1,0:T(8,128)(2,1)} collective-permute-done((bf16[32,8192]{1,0:T(8,128)(2,1)}, bf16[32,8192]{1,0:T(8,128)(2,1)}, u32[]{:S(2)}, u32[]{:S(2)}) %collective-permute-start) | collective-permute-done | bytes 524320 | tf_op jit(solution)/shard_map/cond/branch_1_fun/ppermute | solution.py:34
  31.6 1.2 %add_convert_fusion = bf16[32,8192]{1,0:T(8,128)(2,1)S(1)} fusion(bf16[32,8192]{1,0:T(8,128)(2,1)} %collective-permute-done, bf16[64,8192]{1,0:T(8,128)(2,1)S(1)} %get-tuple-element.41, s32[]{:T(128)S(6)} %select_n.40), kind=kLoop, calls=%fused_computation | loop fusion | flops 1048576 | bytes 1572868 | tf_op jit(solution)/shard_map/cond/branch_1_fun/convert_element_type | solution.py:354
  32.7 0.0 copy-start.3
  32.7 0.8 copy-done.3
  33.5 0.1 collective-permute-start.1
  33.6 0.0 copy-start.4
  33.7 3.0 %pick.2 = (bf16[128,2048]{1,0:T(8,128)(2,1)}, bf16[128,2048]{1,0:T(8,128)(2,1)}, bf16[128,2048]{1,0:T(8,128)(2,1)}, bf16[128,2048]{1,0:T(8,128)(2,1)}) custom-call(s32[8]{0:T(128)S(1)} %get-tuple-element.44.ids, bf16[128,4096]{1,0:T(8,128)(2,1)} %get-tuple-element.45.tokens, bf16[128,14336]{1,0:T(8,128)(2,1)} %get-tuple-element.46.out_grads), custom_call_target="tpu_custom_call" | custom-call | bytes 8388608 | tf_op jit(solution)/shard_map/cond/branch_1_fun/pick/pallas_call | solution.py:91
  36.7 2.6 %collective-permute-done.1 = bf16[16,8192]{1,0:T(8,128)(2,1)S(1)} collective-permute-done((bf16[16,8192]{1,0:T(8,128)(2,1)S(1)}, bf16[16,8192]{1,0:T(8,128)(2,1)S(1)}, u32[]{:S(2)}, u32[]{:S(2)}) %collective-permute-start.1) | collective-permute-done | bytes 262176 | tf_op jit(solution)/shard_map/cond/branch_1_fun/ppermute | solution.py:34
  39.2 0.0 copy-done.4
  39.2 0.1 add_convert_fusion.1
  39.3 0.0 collective-permute-done.5
  39.3 0.0 collective-permute-done.6
  39.3 0.1 collective-permute-start.9
  39.4 2.7 %collective-permute-start.10 = (bf16[128,2048]{1,0:T(8,128)(2,1)}, bf16[128,2048]{1,0:T(8,128)(2,1)}, u32[]{:S(2)}, u32[]{:S(2)}) collective-permute-start(bf16[128,2048]{1,0:T(8,128)(2,1)} %get-tuple-element.122), channel_id=1, source_target_pairs={{0,3},{1,0},{2,1},{3,2},{4,7},{5,4},{6,5},{7,6},{8,11},{9,8},{10,9... | collective-permute-start | bytes 1572872 | tf_op jit(solution)/shard_map/ppermute | solution.py:34
  42.1 0.0 copy-done
  42.1 12.8 %conditional.4 = (bf16[16,8192]{1,0:T(8,128)(2,1)S(1)}, f32[1024,1024]{1,0:T(8,128)}) conditional(s32[]{:T(128)} %convert_element_type.59, bf16[16,8192]{1,0:T(8,128)(2,1)S(1)} %get-tuple-element.111, (bf16[16,8192]{1,0:T(8,128)(2,1)S(1)}, bf16[128,2048]{1,0:T(8,128)(2,1)}, bf16[128,2048]{1,0:T(8,128)(2,1)}, bf16[128,2048]{1,0:T(8,128)(2,1)}, ...), branch_computations={%region_2.3_spmd, %region_3.4_spmd} | conditional | flops 2416443392 | bytes 6029368 | solution.py:417
  42.1 0.3 collective-permute-start.2
  42.4 6.7 %early.2 = f32[1024,1024]{1,0:T(8,128)} custom-call(bf16[128,2048]{1,0:T(8,128)(2,1)} %get-tuple-element.52.refs_0_, bf16[128,2048]{1,0:T(8,128)(2,1)} %get-tuple-element.53.refs_1_, bf16[128,2048]{1,0:T(8,128)(2,1)} %get-tuple-element.54.refs_2_, bf16[1024,1024]{1,0:T(8,128)(2,1)S(1)} %get-tuple-element.55.refs_3_, bf16[1024,1024]{1,0:T(8,128)(2,1)} %get-tuple-element.56.refs_4_), custom_call_target="tpu_custom_call" | custom-call | flops 2415919104 | bytes 4194304 | tf_op jit(solution)/shard_map/cond/branch_1_fun/early/pallas_call | solution.py:154
  49.1 5.6 %collective-permute-done.2 = bf16[16,8192]{1,0:T(8,128)(2,1)S(1)} collective-permute-done((bf16[16,8192]{1,0:T(8,128)(2,1)S(1)}, bf16[16,8192]{1,0:T(8,128)(2,1)S(1)}, u32[]{:S(2)}, u32[]{:S(2)}) %collective-permute-start.2) | collective-permute-done | bytes 262176 | tf_op jit(solution)/shard_map/cond/branch_1_fun/ppermute | solution.py:34
  54.7 0.2 add_convert_fusion.2
  54.9 1.8 %collective-permute-start.11 = (bf16[128,2048]{1,0:T(8,128)(2,1)}, bf16[128,2048]{1,0:T(8,128)(2,1)}, u32[]{:S(2)}, u32[]{:S(2)}) collective-permute-start(bf16[128,2048]{1,0:T(8,128)(2,1)} %get-tuple-element.123), channel_id=1, source_target_pairs={{0,4},{1,5},{2,6},{3,7},{4,0},{5,1},{6,2},{7,3},{8,12},{9,13},{10,... | collective-permute-start | bytes 1572872 | tf_op jit(solution)/shard_map/ppermute | solution.py:34
  56.6 0.0 collective-permute-done.7
  56.7 0.0 collective-permute-done.8
  56.7 9.7 %conditional.5 = (bf16[32,8192]{1,0:T(8,128)(2,1)S(1)}, f32[1024,1024]{1,0:T(8,128)}) conditional(s32[]{:T(128)} %convert_element_type.59, bf16[16,8192]{1,0:T(8,128)(2,1)S(1)} %get-tuple-element.114, (s32[]{:T(128)}, bf16[16,8192]{1,0:T(8,128)(2,1)S(1)}, bf16[128,2048]{1,0:T(8,128)(2,1)}, bf16[128,2048]{1,0:T(8,128)(2,1)}, ...), branch_computations={%region_4.5_spmd, %region_5.6_spmd} | conditional | flops 1612972032 | bytes 14680158 | solution.py:418
  56.7 0.0 copy-start.1
  56.7 1.4 %collective-permute-start.3 = (bf16[16,8192]{1,0:T(8,128)(2,1)S(1)}, bf16[16,8192]{1,0:T(8,128)(2,1)}, u32[]{:S(2)}, u32[]{:S(2)}) collective-permute-start(bf16[16,8192]{1,0:T(8,128)(2,1)S(1)} %get-tuple-element.58), channel_id=1, source_target_pairs={{0,96},{1,97},{2,98},{3,99},{4,100},{5,101},{6,102},{7,103},{8,40}... | collective-permute-start | bytes 786440 | tf_op jit(solution)/shard_map/cond/branch_1_fun/ppermute | solution.py:34
  58.0 0.0 copy-done.1
  58.0 7.1 %early.3 = f32[1024,1024]{1,0:T(8,128)} custom-call(bf16[128,2048]{1,0:T(8,128)(2,1)} %get-tuple-element.59.refs_0_, bf16[128,2048]{1,0:T(8,128)(2,1)} %get-tuple-element.60.refs_1_, bf16[1024,1024]{1,0:T(8,128)(2,1)} %copy-done.1, bf16[1024,1024]{1,0:T(8,128)(2,1)} %get-tuple-element.62.refs_3_, f32[1024,1024]{1,0:T(8,128)} %get-tuple-element.63.refs_4_), custom_call_target="tpu_custom_call" | custom-call | flops 1610612736 | bytes 4194304 | tf_op jit(solution)/shard_map/cond/branch_1_fun/early/pallas_call | solution.py:154
  65.2 0.0 collective-permute-done.3
  65.2 1.1 %maximum_select_fusion = bf16[32,8192]{1,0:T(8,128)(2,1)S(1)} fusion(bf16[16,8192]{1,0:T(8,128)(2,1)} %collective-permute-done.3, bf16[16,8192]{1,0:T(8,128)(2,1)S(1)} %get-tuple-element.58, pred[]{:T(512)S(6)} %eq.10), kind=kLoop, calls=%fused_computation.6 | loop fusion | flops 2359296 | bytes 1048577 | tf_op jit(solution)/shard_map/cond/branch_1_fun/select_n | solution.py:358
  66.3 3.5 %hold.1 = (bf16[1024,1024]{1,0:T(8,128)(2,1)S(1)}, bf16[1024,1024]{1,0:T(8,128)(2,1)S(1)}, bf16[1024,1024]{1,0:T(8,128)(2,1)S(1)}, bf16[1024,1024]{1,0:T(8,128)(2,1)S(1)}) custom-call(f32[1024,1024]{1,0:T(8,128)} %get-tuple-element.116.gate.refs_7_, bf16[1024,1024]{1,0:T(8,128)(2,1)} %bitcast.18, bf16[1024,1024]{1,0:T(8,128)(2,1)} %bitcast.23, ...), custom_call_target="tpu_custom_call" | custom-call | bytes 8388608 | tf_op jit(solution)/shard_map/hold/pallas_call | solution.py:185
  69.8 0.0 collective-permute-done.9.refs_4_
  69.9 0.0 copy-start.5
  69.9 0.0 collective-permute-done.10.refs_5_
  69.9 0.0 collective-permute-done.11.refs_6_
  69.9 2.9 %collective-permute-start.12 = (bf16[32,8192]{1,0:T(8,128)(2,1)S(1)}, bf16[32,8192]{1,0:T(8,128)(2,1)S(1)}, u32[]{:S(2)}, u32[]{:S(2)}) collective-permute-start(bf16[32,8192]{1,0:T(8,128)(2,1)S(1)} %get-tuple-element.128), channel_id=1, source_target_pairs={{0,32},{1,33},{2,34},{3,35},{4,36},{5,37},{6,38},{7,39},{8,104},{9... | collective-permute-start | bytes 1572872 | tf_op jit(solution)/shard_map/ppermute | solution.py:34
  72.8 0.0 copy-done.5
  72.8 11.9 %final.1 = (bf16[1024,1024]{1,0:T(8,128)(2,1)}, bf16[1024,1024]{1,0:T(8,128)(2,1)}, bf16[1024,1024]{1,0:T(8,128)(2,1)}, f32[128,8192]{1,0:T(8,128)S(1)}, f32[128...) custom-call(bf16[1024,1024]{1,0:T(8,128)(2,1)S(1)} %get-tuple-element.117.refs_0_, ...), custom_call_target="tpu_custom_call" | custom-call | flops 6710886400 | bytes 6291456 | tf_op jit(solution)/shard_map/final/pallas_call | solution.py:267
  84.7 0.0 copy-start.7
  84.7 0.0 collective-permute-done.12
  84.7 0.2 maximum_select_fusion.1.total
  84.9 0.6 collective-permute-start.13
  85.5 0.0 copy-done.7
  85.5 0.1 broadcast_in_dim.28.due
  85.6 2.7 %outer.2 = (f32[128,8192]{1,0:T(8,128)}, f32[128,8192]{1,0:T(8,128)}, bf16[128,8192]{1,0:T(8,128)(2,1)}) custom-call(s32[1]{0:T(128)} %bitcast.12.half, bf16[64,8192]{1,0:T(8,128)(2,1)S(1)} %maximum_select_fusion.1.total, f32[128,8192]{1,0:T(8,128)S(1)} %get-tuple-element.130.params, f32[128,8192]{1,0:T(8,128)S(1)} %get-tuple-element.131.momentum, ...), custom_call_target="tpu_custom_call" | custom-call | flops 5242880 | bytes 12582912 | tf_op jit(solution)/shard_map/outer/pallas_call | solution.py:327
  88.3 0.0 collective-permute-done.13.total
  88.3 2.7 %outer.3 = (f32[128,8192]{1,0:T(8,128)}, f32[128,8192]{1,0:T(8,128)}, bf16[128,8192]{1,0:T(8,128)(2,1)}) custom-call(s32[1]{0:T(128)} %bitcast.11.half, bf16[64,8192]{1,0:T(8,128)(2,1)S(1)} %collective-permute-done.13.total, f32[128,8192]{1,0:T(8,128)S(1)} %get-tuple-element.130.params, ...), custom_call_target="tpu_custom_call", output_to_operand_aliasing={{0}: (7, {}), {1}: (8, {}), {2}: (9, {})} | custom-call | flops 5242880 | bytes 12582912 | tf_op jit(solution)/shard_map/outer/pallas_call | solution.py:327
  (1 shorter events, 0.0 us)
Async XLA Ops:
  0.6 3.6 %copy-start.6 = (s32[8]{0:T(128)S(1)}, s32[8]{0:T(128)}, u32[]{:S(2)}) copy-start(s32[8]{0:T(128)} %ids.1) | copy-start | bytes 100
  2.7 15.8 %copy-start.2 = (bf16[1,128,8192]{2,1,0:T(8,128)(2,1)S(1)}, bf16[1,128,8192]{2,1,0:T(8,128)(2,1)}, u32[]{:S(2)}) copy-start(bf16[1,128,8192]{2,1,0:T(8,128)(2,1)} %param.27) | copy-start | bytes 6291460
  2.7 15.8 %collective-permute-start.4 = (bf16[64,8192]{1,0:T(8,128)(2,1)S(1)}, bf16[64,8192]{1,0:T(8,128)(2,1)}, u32[]{:S(2)}, u32[]{:S(2)}) collective-permute-start(bf16[64,8192]{1,0:T(8,128)(2,1)S(1)} %fusion), channel_id=1, source_target_pairs={{0,8},{1,9},{2,10},{3,11},{4,12},{5,13},{6,14},{7,15},{8,0},{9,1},... | collective-permute-start | bytes 3145736 | tf_op jit(solution)/shard_map/ppermute | solution.py:34
  7.2 32.1 %collective-permute-start.5 = (bf16[128,2048]{1,0:T(8,128)(2,1)}, bf16[128,2048]{1,0:T(8,128)(2,1)}, u32[]{:S(2)}, u32[]{:S(2)}) collective-permute-start(bf16[128,2048]{1,0:T(8,128)(2,1)} %get-tuple-element.105), channel_id=1, source_target_pairs={{0,6},{1,7},{2,4},{3,5},{4,2},{5,3},{6,0},{7,1},{8,14},{9,15},{10,... | collective-permute-start | bytes 1572872 | tf_op jit(solution)/shard_map/ppermute | solution.py:34
  13.5 25.9 %collective-permute-start.6 = (bf16[128,2048]{1,0:T(8,128)(2,1)}, bf16[128,2048]{1,0:T(8,128)(2,1)}, u32[]{:S(2)}, u32[]{:S(2)}) collective-permute-start(bf16[128,2048]{1,0:T(8,128)(2,1)} %get-tuple-element.106), channel_id=1, source_target_pairs={{0,5},{1,6},{2,7},{3,4},{4,1},{5,2},{6,3},{7,0},{8,13},{9,14},{10,... | collective-permute-start | bytes 1572872 | tf_op jit(solution)/shard_map/ppermute | solution.py:34
  14.1 42.5 %collective-permute-start.7 = (bf16[128,2048]{1,0:T(8,128)(2,1)}, bf16[128,2048]{1,0:T(8,128)(2,1)}, u32[]{:S(2)}, u32[]{:S(2)}) collective-permute-start(bf16[128,2048]{1,0:T(8,128)(2,1)} %get-tuple-element.107), channel_id=1, source_target_pairs={{0,7},{1,4},{2,5},{3,6},{4,3},{5,0},{6,1},{7,2},{8,15},{9,12},{10,... | collective-permute-start | bytes 1572872 | tf_op jit(solution)/shard_map/ppermute | solution.py:34
  18.5 38.1 %collective-permute-start.8 = (bf16[128,2048]{1,0:T(8,128)(2,1)}, bf16[128,2048]{1,0:T(8,128)(2,1)}, u32[]{:S(2)}, u32[]{:S(2)}) collective-permute-start(bf16[128,2048]{1,0:T(8,128)(2,1)} %get-tuple-element.108), channel_id=1, source_target_pairs={{0,2},{1,3},{2,0},{3,1},{4,6},{5,7},{6,4},{7,5},{8,10},{9,11},{10,... | collective-permute-start | bytes 1572872 | tf_op jit(solution)/shard_map/ppermute | solution.py:34
  20.8 21.3 %copy-start = (bf16[1,1,1024,1024]{3,2,1,0:T(8,128)(2,1)S(1)}, bf16[1,1,1024,1024]{3,2,1,0:T(8,128)(2,1)}, u32[]{:S(2)}) copy-start(bf16[1,1,1024,1024]{3,2,1,0:T(8,128)(2,1)} %param.21) | copy-start | bytes 6291460
  21.7 9.9 %collective-permute-start = (bf16[32,8192]{1,0:T(8,128)(2,1)}, bf16[32,8192]{1,0:T(8,128)(2,1)}, u32[]{:S(2)}, u32[]{:S(2)}) collective-permute-start(bf16[32,8192]{1,0:T(8,128)(2,1)} %constant_dynamic-slice_fusion.1), channel_id=1, source_target_pairs={{0,32},{1,33},{2,34},{3,35},{4,36},{5,37},{6,38},{7,39},{8,104},{9... | collective-permute-start | bytes 1572872 | tf_op jit(solution)/shard_map/cond/branch_1_fun/ppermute | solution.py:34
  32.7 0.8 copy-start.3
  33.5 5.7 %collective-permute-start.1 = (bf16[16,8192]{1,0:T(8,128)(2,1)S(1)}, bf16[16,8192]{1,0:T(8,128)(2,1)S(1)}, u32[]{:S(2)}, u32[]{:S(2)}) collective-permute-start(bf16[16,8192]{1,0:T(8,128)(2,1)S(1)} %constant_dynamic-slice_fusion), channel_id=1, source_target_pairs={{0,96},{1,97},{2,98},{3,99},{4,100},{5,101},{6,102},{7,103},{8,40}... | collective-permute-start | bytes 786440 | tf_op jit(solution)/shard_map/cond/branch_1_fun/ppermute | solution.py:34
  33.6 5.6 %copy-start.4 = (bf16[32,8192]{1,0:T(8,128)(2,1)S(1)}, bf16[32,8192]{1,0:T(8,128)(2,1)}, u32[]{:S(2)}) copy-start(bf16[32,8192]{1,0:T(8,128)(2,1)} %copy-done.3) | copy-start | bytes 1572868 | tf_op jit(solution)/shard_map/cond
  39.3 30.5 %collective-permute-start.9 = (bf16[128,2048]{1,0:T(8,128)(2,1)}, bf16[128,2048]{1,0:T(8,128)(2,1)S(1)}, u32[]{:S(2)}, u32[]{:S(2)}) collective-permute-start(bf16[128,2048]{1,0:T(8,128)(2,1)} %get-tuple-element.121), channel_id=1, source_target_pairs={{0,1},{1,2},{2,3},{3,0},{4,5},{5,6},{6,7},{7,4},{8,9},{9,10},{10,1... | collective-permute-start | bytes 1572872 | tf_op jit(solution)/shard_map/ppermute | solution.py:34
  39.4 30.4 %collective-permute-start.10 = (bf16[128,2048]{1,0:T(8,128)(2,1)}, bf16[128,2048]{1,0:T(8,128)(2,1)}, u32[]{:S(2)}, u32[]{:S(2)}) collective-permute-start(bf16[128,2048]{1,0:T(8,128)(2,1)} %get-tuple-element.122), channel_id=1, source_target_pairs={{0,3},{1,0},{2,1},{3,2},{4,7},{5,4},{6,5},{7,6},{8,11},{9,8},{10,9... | collective-permute-start | bytes 1572872 | tf_op jit(solution)/shard_map/ppermute | solution.py:34
  42.1 12.6 %collective-permute-start.2 = (bf16[16,8192]{1,0:T(8,128)(2,1)S(1)}, bf16[16,8192]{1,0:T(8,128)(2,1)S(1)}, u32[]{:S(2)}, u32[]{:S(2)}) collective-permute-start(bf16[16,8192]{1,0:T(8,128)(2,1)S(1)} %get-tuple-element.51), channel_id=1, source_target_pairs={{0,16},{1,17},{2,18},{3,19},{4,20},{5,21},{6,22},{7,23},{8,24},{9,... | collective-permute-start | bytes 786440 | tf_op jit(solution)/shard_map/cond/branch_1_fun/ppermute | solution.py:34
  54.9 15.0 %collective-permute-start.11 = (bf16[128,2048]{1,0:T(8,128)(2,1)}, bf16[128,2048]{1,0:T(8,128)(2,1)}, u32[]{:S(2)}, u32[]{:S(2)}) collective-permute-start(bf16[128,2048]{1,0:T(8,128)(2,1)} %get-tuple-element.123), channel_id=1, source_target_pairs={{0,4},{1,5},{2,6},{3,7},{4,0},{5,1},{6,2},{7,3},{8,12},{9,13},{10,... | collective-permute-start | bytes 1572872 | tf_op jit(solution)/shard_map/ppermute | solution.py:34
  56.7 1.4 %copy-start.1 = (bf16[1024,1024]{1,0:T(8,128)(2,1)}, bf16[1024,1024]{1,0:T(8,128)(2,1)S(1)}, u32[]{:S(2)}) copy-start(bf16[1024,1024]{1,0:T(8,128)(2,1)S(1)} %get-tuple-element.61.refs_2_) | copy-start | bytes 6291460 | tf_op jit(solution)/shard_map/cond
  56.7 8.5 %collective-permute-start.3 = (bf16[16,8192]{1,0:T(8,128)(2,1)S(1)}, bf16[16,8192]{1,0:T(8,128)(2,1)}, u32[]{:S(2)}, u32[]{:S(2)}) collective-permute-start(bf16[16,8192]{1,0:T(8,128)(2,1)S(1)} %get-tuple-element.58), channel_id=1, source_target_pairs={{0,96},{1,97},{2,98},{3,99},{4,100},{5,101},{6,102},{7,103},{8,40}... | collective-permute-start | bytes 786440 | tf_op jit(solution)/shard_map/cond/branch_1_fun/ppermute | solution.py:34
  69.9 3.0 %copy-start.5 = (bf16[128,2048]{1,0:T(8,128)(2,1)}, bf16[128,2048]{1,0:T(8,128)(2,1)S(1)}, u32[]{:S(2)}) copy-start(bf16[128,2048]{1,0:T(8,128)(2,1)S(1)} %collective-permute-done.9.refs_4_) | copy-start | bytes 1572868
  69.9 14.8 %collective-permute-start.12 = (bf16[32,8192]{1,0:T(8,128)(2,1)S(1)}, bf16[32,8192]{1,0:T(8,128)(2,1)S(1)}, u32[]{:S(2)}, u32[]{:S(2)}) collective-permute-start(bf16[32,8192]{1,0:T(8,128)(2,1)S(1)} %get-tuple-element.128), channel_id=1, source_target_pairs={{0,32},{1,33},{2,34},{3,35},{4,36},{5,37},{6,38},{7,39},{8,104},{9... | collective-permute-start | bytes 1572872 | tf_op jit(solution)/shard_map/ppermute | solution.py:34
  84.7 0.8 copy-start.7
  84.9 3.4 %collective-permute-start.13 = (bf16[64,8192]{1,0:T(8,128)(2,1)S(1)}, bf16[64,8192]{1,0:T(8,128)(2,1)S(1)}, u32[]{:S(2)}, u32[]{:S(2)}) collective-permute-start(bf16[64,8192]{1,0:T(8,128)(2,1)S(1)} %maximum_select_fusion.1.total), channel_id=1, source_target_pairs={{0,8},{1,9},{2,10},{3,11},{4,12},{5,13},{6,14},{7,15},{8,0},{9,1},... | collective-permute-start | bytes 3145736 | tf_op jit(solution)/shard_map/ppermute | solution.py:34

commit v6 on v5

--- a/solution.py
+++ b/solution.py
@@ -235,12 +235,12 @@
             copy.start()
 
     def update_copy(i):
-        at = pl.ds(pl.multiple_of(i * 256, 256), 256)
+        at = pl.ds(pl.multiple_of(i * 512, 512), 512)
         return pltpu.make_async_copy(u_out.at[at, :], update.at[at, :], sems.at[8 + i])
 
-    @pl.loop(0, 4)
-    def _(i):
-        at = pl.ds(pl.multiple_of(i * 256, 256), 256)
+    @pl.loop(0, 2)
+    def _(i):
+        at = pl.ds(pl.multiple_of(i * 512, 512), 512)
         back = jnp.dot(left[at, :], direction[...], preferred_element_type=F32).astype(BF16)
         u_out[at, :] = lax.dot_general(
             back, right[...], (((1,), (1,)), ((), ())), preferred_element_type=F32
@@ -252,7 +252,7 @@
         for copy in moment_copies(i):
             copy.wait()
 
-    @pl.loop(0, 4)
+    @pl.loop(0, 2)
     def _(i):
         update_copy(i).wait()
 

time: 91.4 us -> 91.2 us (level)
  no operation moved by 1% of the time
where the time goes in v6:
time: 91.2 us; the launch traced here: 90.9 us
  Pallas kernels  40.4 us (44%)
  starting transfers between devices  25.4 us (28%)
  waiting for transfers between devices  15.3 us (17%)
  other arithmetic  6.96 us (8%)
  local copies, waits for them, and re-layouts  1.74 us (2%)
  between operations  0.98 us (1%)
    ppermute x14, starting transfers between devices, moved(): lax.ppermute(array, AXES, [(s, index_of(*where(*place(s)))) for s in rang...  25.4 us
    ppermute x14, waiting for transfers between devices, moved(): lax.ppermute(array, AXES, [(s, index_of(*where(*place(s)))) for s in rang...  15.3 us
    pallas_call x2, Pallas kernels, early(): pl.pallas_call(functools.partial(early_kernel, n, len(acc)), out_shape=pl...  13.8 us
    pallas_call x1, Pallas kernels, final(): pl.pallas_call(functools.partial(final_kernel, n), out_shape=[square] * 3...  11.7 us
    pallas_call x2, Pallas kernels, pick(): pl.pallas_call(functools.partial(pick_kernel, shifts), out_shape=[pltpu.H...  6.04 us
    pallas_call x2, Pallas kernels, outer(): pl.pallas_call(outer_kernel, out_shape=[pltpu.HBM(params.shape, F32), plt...  5.34 us
    convert_element_type x4, other arithmetic, added(): return (one.astype(F32) + two.astype(F32)).astype(BF16)  3.61 us
    pallas_call x1, Pallas kernels, hold(): pl.pallas_call(hold_kernel, out_shape=[pltpu.VMEM(a.shape, a.dtype) for a...  3.51 us
  transfers between devices with their start and end apart: 14, of which 3 were waited for; matrix products, arithmetic and copies ran while one was open for 6% of the time, Pallas kernels for 42%

profile of v6, /device:TPU:1, one launch (start us, length us, event | category | flops | bytes accessed | tf_op | source)
XLA Modules:
  0.0 90.9 jit_solution(15822943339165870531)
XLA Ops:
  0.6 0.0 copy-start.6
  0.7 2.0 %fusion = bf16[64,8192]{1,0:T(8,128)(2,1)S(1)} fusion(f32[128,8192]{1,0:T(8,128)} %refs_8_.1, s32[]{:T(128)S(6)} %select_n.58, bf16[1,128,8192]{2,1,0:T(8,128)(2,1)} %param.27), kind=kLoop, calls=%fused_computation.8 | loop fusion | flops 1572864 | bytes 4194308 | tf_op jit(solution)/shard_map/convert_element_type | solution.py:388
  2.7 0.0 copy-start.2
  2.7 1.5 %collective-permute-start.4 = (bf16[64,8192]{1,0:T(8,128)(2,1)S(1)}, bf16[64,8192]{1,0:T(8,128)(2,1)}, u32[]{:S(2)}, u32[]{:S(2)}) collective-permute-start(bf16[64,8192]{1,0:T(8,128)(2,1)S(1)} %fusion), channel_id=1, source_target_pairs={{0,8},{1,9},{2,10},{3,11},{4,12},{5,13},{6,14},{7,15},{8,0},{9,1},... | collective-permute-start | bytes 3145736 | tf_op jit(solution)/shard_map/ppermute | solution.py:34
  4.2 0.0 copy-done.6
  4.2 3.0 %pick.3 = (bf16[128,2048]{1,0:T(8,128)(2,1)}, bf16[128,2048]{1,0:T(8,128)(2,1)}, bf16[128,2048]{1,0:T(8,128)(2,1)}, bf16[128,2048]{1,0:T(8,128)(2,1)}) custom-call(s32[8]{0:T(128)S(1)} %copy-done.6, bf16[128,4096]{1,0:T(8,128)(2,1)} %tokens.1, bf16[128,14336]{1,0:T(8,128)(2,1)} %out_grads.1), custom_call_target="tpu_custom_call" | custom-call | bytes 8388608 | tf_op jit(solution)/shard_map/pick/pallas_call | solution.py:91
  7.2 6.2 %collective-permute-start.5 = (bf16[128,2048]{1,0:T(8,128)(2,1)}, bf16[128,2048]{1,0:T(8,128)(2,1)}, u32[]{:S(2)}, u32[]{:S(2)}) collective-permute-start(bf16[128,2048]{1,0:T(8,128)(2,1)} %get-tuple-element.105), channel_id=1, source_target_pairs={{0,6},{1,7},{2,4},{3,5},{4,2},{5,3},{6,0},{7,1},{8,14},{9,15},{10,... | collective-permute-start | bytes 1572872 | tf_op jit(solution)/shard_map/ppermute | solution.py:34
  13.5 0.7 collective-permute-start.6
  14.1 4.4 %collective-permute-start.7 = (bf16[128,2048]{1,0:T(8,128)(2,1)}, bf16[128,2048]{1,0:T(8,128)(2,1)}, u32[]{:S(2)}, u32[]{:S(2)}) collective-permute-start(bf16[128,2048]{1,0:T(8,128)(2,1)} %get-tuple-element.107), channel_id=1, source_target_pairs={{0,7},{1,4},{2,5},{3,6},{4,3},{5,0},{6,1},{7,2},{8,15},{9,12},{10,... | collective-permute-start | bytes 1572872 | tf_op jit(solution)/shard_map/ppermute | solution.py:34
  18.5 0.0 collective-permute-start.8
  18.5 0.0 collective-permute-done.4
  18.5 0.0 copy-done.2
  18.6 2.2 %add_convert_fusion.3 = bf16[64,8192]{1,0:T(8,128)(2,1)S(1)} fusion(bf16[64,8192]{1,0:T(8,128)(2,1)} %collective-permute-done.4, f32[128,8192]{1,0:T(8,128)} %refs_8_.1, s32[]{:T(128)S(6)} %select_n.57, bf16[1,128,8192]{2,1,0:T(8,128)(2,1)S(1)} %copy-done.2), kind=kLoop, calls=%fused_computation.11 | loop fusion | flops 3670016 | bytes 5242884 | tf_op jit(solution)/shard_map/convert_element_type | solution.py:354
  20.8 0.0 copy-start
  20.8 18.5 %conditional.3 = (bf16[16,8192]{1,0:T(8,128)(2,1)S(1)}, bf16[128,2048]{1,0:T(8,128)(2,1)}, bf16[128,2048]{1,0:T(8,128)(2,1)}, bf16[128,2048]{1,0:T(8,128)(2,1)}, bf16[128,2048]{1,0:T(8,128)(2,1)}) conditional(s32[]{:T(128)} %convert_element_type.59, bf16[64,8192]{1,0:T(8,128)(2,1)S(1)} %add_convert_fusion.3, (s32[]{:T(128)}, ...), branch_computations={%region_0.1_spmd, %region_1.2_spmd} | conditional | flops 1572882 | bytes 19661200 | solution.py:415
  20.8 0.8 constant_dynamic-slice_fusion.1
  21.7 2.7 %collective-permute-start = (bf16[32,8192]{1,0:T(8,128)(2,1)}, bf16[32,8192]{1,0:T(8,128)(2,1)}, u32[]{:S(2)}, u32[]{:S(2)}) collective-permute-start(bf16[32,8192]{1,0:T(8,128)(2,1)} %constant_dynamic-slice_fusion.1), channel_id=1, source_target_pairs={{0,32},{1,33},{2,34},{3,35},{4,36},{5,37},{6,38},{7,39},{8,104},{9... | collective-permute-start | bytes 1572872 | tf_op jit(solution)/shard_map/cond/branch_1_fun/ppermute | solution.py:34
  24.4 7.2 %collective-permute-done = bf16[32,8192]{1,0:T(8,128)(2,1)} collective-permute-done((bf16[32,8192]{1,0:T(8,128)(2,1)}, bf16[32,8192]{1,0:T(8,128)(2,1)}, u32[]{:S(2)}, u32[]{:S(2)}) %collective-permute-start) | collective-permute-done | bytes 524320 | tf_op jit(solution)/shard_map/cond/branch_1_fun/ppermute | solution.py:34
  31.6 1.2 %add_convert_fusion = bf16[32,8192]{1,0:T(8,128)(2,1)S(1)} fusion(bf16[32,8192]{1,0:T(8,128)(2,1)} %collective-permute-done, bf16[64,8192]{1,0:T(8,128)(2,1)S(1)} %get-tuple-element.41, s32[]{:T(128)S(6)} %select_n.40), kind=kLoop, calls=%fused_computation | loop fusion | flops 1048576 | bytes 1572868 | tf_op jit(solution)/shard_map/cond/branch_1_fun/convert_element_type | solution.py:354
  32.7 0.0 copy-start.3
  32.7 0.8 copy-done.3
  33.5 0.1 collective-permute-start.1
  33.6 0.0 copy-start.4
  33.7 3.0 %pick.2 = (bf16[128,2048]{1,0:T(8,128)(2,1)}, bf16[128,2048]{1,0:T(8,128)(2,1)}, bf16[128,2048]{1,0:T(8,128)(2,1)}, bf16[128,2048]{1,0:T(8,128)(2,1)}) custom-call(s32[8]{0:T(128)S(1)} %get-tuple-element.44.ids, bf16[128,4096]{1,0:T(8,128)(2,1)} %get-tuple-element.45.tokens, bf16[128,14336]{1,0:T(8,128)(2,1)} %get-tuple-element.46.out_grads), custom_call_target="tpu_custom_call" | custom-call | bytes 8388608 | tf_op jit(solution)/shard_map/cond/branch_1_fun/pick/pallas_call | solution.py:91
  36.7 2.6 %collective-permute-done.1 = bf16[16,8192]{1,0:T(8,128)(2,1)S(1)} collective-permute-done((bf16[16,8192]{1,0:T(8,128)(2,1)S(1)}, bf16[16,8192]{1,0:T(8,128)(2,1)S(1)}, u32[]{:S(2)}, u32[]{:S(2)}) %collective-permute-start.1) | collective-permute-done | bytes 262176 | tf_op jit(solution)/shard_map/cond/branch_1_fun/ppermute | solution.py:34
  39.2 0.0 copy-done.4
  39.2 0.1 add_convert_fusion.1
  39.3 0.0 collective-permute-done.5
  39.3 0.0 collective-permute-done.6
  39.3 0.1 collective-permute-start.9
  39.4 2.7 %collective-permute-start.10 = (bf16[128,2048]{1,0:T(8,128)(2,1)}, bf16[128,2048]{1,0:T(8,128)(2,1)}, u32[]{:S(2)}, u32[]{:S(2)}) collective-permute-start(bf16[128,2048]{1,0:T(8,128)(2,1)} %get-tuple-element.122), channel_id=1, source_target_pairs={{0,3},{1,0},{2,1},{3,2},{4,7},{5,4},{6,5},{7,6},{8,11},{9,8},{10,9... | collective-permute-start | bytes 1572872 | tf_op jit(solution)/shard_map/ppermute | solution.py:34
  42.1 0.0 copy-done
  42.1 12.7 %conditional.4 = (bf16[16,8192]{1,0:T(8,128)(2,1)S(1)}, f32[1024,1024]{1,0:T(8,128)}) conditional(s32[]{:T(128)} %convert_element_type.59, bf16[16,8192]{1,0:T(8,128)(2,1)S(1)} %get-tuple-element.111, (bf16[16,8192]{1,0:T(8,128)(2,1)S(1)}, bf16[128,2048]{1,0:T(8,128)(2,1)}, bf16[128,2048]{1,0:T(8,128)(2,1)}, bf16[128,2048]{1,0:T(8,128)(2,1)}, ...), branch_computations={%region_2.3_spmd, %region_3.4_spmd} | conditional | flops 2416443392 | bytes 6029368 | solution.py:417
  42.1 0.3 collective-permute-start.2
  42.4 6.7 %early.2 = f32[1024,1024]{1,0:T(8,128)} custom-call(bf16[128,2048]{1,0:T(8,128)(2,1)} %get-tuple-element.52.refs_0_, bf16[128,2048]{1,0:T(8,128)(2,1)} %get-tuple-element.53.refs_1_, bf16[128,2048]{1,0:T(8,128)(2,1)} %get-tuple-element.54.refs_2_, bf16[1024,1024]{1,0:T(8,128)(2,1)S(1)} %get-tuple-element.55.refs_3_, bf16[1024,1024]{1,0:T(8,128)(2,1)} %get-tuple-element.56.refs_4_), custom_call_target="tpu_custom_call" | custom-call | flops 2415919104 | bytes 4194304 | tf_op jit(solution)/shard_map/cond/branch_1_fun/early/pallas_call | solution.py:154
  49.1 5.6 %collective-permute-done.2 = bf16[16,8192]{1,0:T(8,128)(2,1)S(1)} collective-permute-done((bf16[16,8192]{1,0:T(8,128)(2,1)S(1)}, bf16[16,8192]{1,0:T(8,128)(2,1)S(1)}, u32[]{:S(2)}, u32[]{:S(2)}) %collective-permute-start.2) | collective-permute-done | bytes 262176 | tf_op jit(solution)/shard_map/cond/branch_1_fun/ppermute | solution.py:34
  54.7 0.2 add_convert_fusion.2
  54.8 1.8 %collective-permute-start.11 = (bf16[128,2048]{1,0:T(8,128)(2,1)}, bf16[128,2048]{1,0:T(8,128)(2,1)}, u32[]{:S(2)}, u32[]{:S(2)}) collective-permute-start(bf16[128,2048]{1,0:T(8,128)(2,1)} %get-tuple-element.123), channel_id=1, source_target_pairs={{0,4},{1,5},{2,6},{3,7},{4,0},{5,1},{6,2},{7,3},{8,12},{9,13},{10,... | collective-permute-start | bytes 1572872 | tf_op jit(solution)/shard_map/ppermute | solution.py:34
  56.6 0.0 collective-permute-done.7
  56.7 0.0 collective-permute-done.8
  56.7 9.7 %conditional.5 = (bf16[32,8192]{1,0:T(8,128)(2,1)S(1)}, f32[1024,1024]{1,0:T(8,128)}) conditional(s32[]{:T(128)} %convert_element_type.59, bf16[16,8192]{1,0:T(8,128)(2,1)S(1)} %get-tuple-element.114, (s32[]{:T(128)}, bf16[16,8192]{1,0:T(8,128)(2,1)S(1)}, bf16[128,2048]{1,0:T(8,128)(2,1)}, bf16[128,2048]{1,0:T(8,128)(2,1)}, ...), branch_computations={%region_4.5_spmd, %region_5.6_spmd} | conditional | flops 1612972032 | bytes 14680158 | solution.py:418
  56.7 0.0 copy-start.1
  56.7 1.4 %collective-permute-start.3 = (bf16[16,8192]{1,0:T(8,128)(2,1)S(1)}, bf16[16,8192]{1,0:T(8,128)(2,1)}, u32[]{:S(2)}, u32[]{:S(2)}) collective-permute-start(bf16[16,8192]{1,0:T(8,128)(2,1)S(1)} %get-tuple-element.58), channel_id=1, source_target_pairs={{0,96},{1,97},{2,98},{3,99},{4,100},{5,101},{6,102},{7,103},{8,40}... | collective-permute-start | bytes 786440 | tf_op jit(solution)/shard_map/cond/branch_1_fun/ppermute | solution.py:34
  58.0 0.0 copy-done.1
  58.0 7.1 %early.3 = f32[1024,1024]{1,0:T(8,128)} custom-call(bf16[128,2048]{1,0:T(8,128)(2,1)} %get-tuple-element.59.refs_0_, bf16[128,2048]{1,0:T(8,128)(2,1)} %get-tuple-element.60.refs_1_, bf16[1024,1024]{1,0:T(8,128)(2,1)} %copy-done.1, bf16[1024,1024]{1,0:T(8,128)(2,1)} %get-tuple-element.62.refs_3_, f32[1024,1024]{1,0:T(8,128)} %get-tuple-element.63.refs_4_), custom_call_target="tpu_custom_call" | custom-call | flops 1610612736 | bytes 4194304 | tf_op jit(solution)/shard_map/cond/branch_1_fun/early/pallas_call | solution.py:154
  65.2 0.0 collective-permute-done.3
  65.2 1.1 %maximum_select_fusion = bf16[32,8192]{1,0:T(8,128)(2,1)S(1)} fusion(bf16[16,8192]{1,0:T(8,128)(2,1)} %collective-permute-done.3, bf16[16,8192]{1,0:T(8,128)(2,1)S(1)} %get-tuple-element.58, pred[]{:T(512)S(6)} %eq.10), kind=kLoop, calls=%fused_computation.6 | loop fusion | flops 2359296 | bytes 1048577 | tf_op jit(solution)/shard_map/cond/branch_1_fun/select_n | solution.py:358
  66.3 3.5 %hold.1 = (bf16[1024,1024]{1,0:T(8,128)(2,1)S(1)}, bf16[1024,1024]{1,0:T(8,128)(2,1)S(1)}, bf16[1024,1024]{1,0:T(8,128)(2,1)S(1)}, bf16[1024,1024]{1,0:T(8,128)(2,1)S(1)}) custom-call(f32[1024,1024]{1,0:T(8,128)} %get-tuple-element.116.gate.refs_7_, bf16[1024,1024]{1,0:T(8,128)(2,1)} %bitcast.18, bf16[1024,1024]{1,0:T(8,128)(2,1)} %bitcast.23, ...), custom_call_target="tpu_custom_call" | custom-call | bytes 8388608 | tf_op jit(solution)/shard_map/hold/pallas_call | solution.py:185
  69.8 0.0 collective-permute-done.9.refs_4_
  69.9 0.0 copy-start.5
  69.9 0.0 collective-permute-done.10.refs_5_
  69.9 0.0 collective-permute-done.11.refs_6_
  69.9 2.9 %collective-permute-start.12 = (bf16[32,8192]{1,0:T(8,128)(2,1)S(1)}, bf16[32,8192]{1,0:T(8,128)(2,1)S(1)}, u32[]{:S(2)}, u32[]{:S(2)}) collective-permute-start(bf16[32,8192]{1,0:T(8,128)(2,1)S(1)} %get-tuple-element.128), channel_id=1, source_target_pairs={{0,32},{1,33},{2,34},{3,35},{4,36},{5,37},{6,38},{7,39},{8,104},{9... | collective-permute-start | bytes 1572872 | tf_op jit(solution)/shard_map/ppermute | solution.py:34
  72.8 0.0 copy-done.5
  72.8 11.7 %final.1 = (bf16[1024,1024]{1,0:T(8,128)(2,1)}, bf16[1024,1024]{1,0:T(8,128)(2,1)}, bf16[1024,1024]{1,0:T(8,128)(2,1)}, f32[128,8192]{1,0:T(8,128)S(1)}, f32[128...) custom-call(bf16[1024,1024]{1,0:T(8,128)(2,1)S(1)} %get-tuple-element.117.refs_0_, ...), custom_call_target="tpu_custom_call" | custom-call | flops 6710886400 | bytes 6291456 | tf_op jit(solution)/shard_map/final/pallas_call | solution.py:267
  84.5 0.0 copy-start.7
  84.5 0.0 collective-permute-done.12
  84.5 0.2 maximum_select_fusion.1.total
  84.7 0.6 collective-permute-start.13
  85.3 0.0 copy-done.7
  85.3 0.1 broadcast_in_dim.28.due
  85.4 2.7 %outer.2 = (f32[128,8192]{1,0:T(8,128)}, f32[128,8192]{1,0:T(8,128)}, bf16[128,8192]{1,0:T(8,128)(2,1)}) custom-call(s32[1]{0:T(128)} %bitcast.12.half, bf16[64,8192]{1,0:T(8,128)(2,1)S(1)} %maximum_select_fusion.1.total, f32[128,8192]{1,0:T(8,128)S(1)} %get-tuple-element.130.params, f32[128,8192]{1,0:T(8,128)S(1)} %get-tuple-element.131.momentum, ...), custom_call_target="tpu_custom_call" | custom-call | flops 5242880 | bytes 12582912 | tf_op jit(solution)/shard_map/outer/pallas_call | solution.py:327
  88.1 0.0 collective-permute-done.13.total
  88.1 2.7 %outer.3 = (f32[128,8192]{1,0:T(8,128)}, f32[128,8192]{1,0:T(8,128)}, bf16[128,8192]{1,0:T(8,128)(2,1)}) custom-call(s32[1]{0:T(128)} %bitcast.11.half, bf16[64,8192]{1,0:T(8,128)(2,1)S(1)} %collective-permute-done.13.total, f32[128,8192]{1,0:T(8,128)S(1)} %get-tuple-element.130.params, ...), custom_call_target="tpu_custom_call", output_to_operand_aliasing={{0}: (7, {}), {1}: (8, {}), {2}: (9, {})} | custom-call | flops 5242880 | bytes 12582912 | tf_op jit(solution)/shard_map/outer/pallas_call | solution.py:327
  (1 shorter events, 0.0 us)
Async XLA Ops:
  0.6 3.6 %copy-start.6 = (s32[8]{0:T(128)S(1)}, s32[8]{0:T(128)}, u32[]{:S(2)}) copy-start(s32[8]{0:T(128)} %ids.1) | copy-start | bytes 100
  2.7 15.8 %copy-start.2 = (bf16[1,128,8192]{2,1,0:T(8,128)(2,1)S(1)}, bf16[1,128,8192]{2,1,0:T(8,128)(2,1)}, u32[]{:S(2)}) copy-start(bf16[1,128,8192]{2,1,0:T(8,128)(2,1)} %param.27) | copy-start | bytes 6291460
  2.7 15.8 %collective-permute-start.4 = (bf16[64,8192]{1,0:T(8,128)(2,1)S(1)}, bf16[64,8192]{1,0:T(8,128)(2,1)}, u32[]{:S(2)}, u32[]{:S(2)}) collective-permute-start(bf16[64,8192]{1,0:T(8,128)(2,1)S(1)} %fusion), channel_id=1, source_target_pairs={{0,8},{1,9},{2,10},{3,11},{4,12},{5,13},{6,14},{7,15},{8,0},{9,1},... | collective-permute-start | bytes 3145736 | tf_op jit(solution)/shard_map/ppermute | solution.py:34
  7.2 32.1 %collective-permute-start.5 = (bf16[128,2048]{1,0:T(8,128)(2,1)}, bf16[128,2048]{1,0:T(8,128)(2,1)}, u32[]{:S(2)}, u32[]{:S(2)}) collective-permute-start(bf16[128,2048]{1,0:T(8,128)(2,1)} %get-tuple-element.105), channel_id=1, source_target_pairs={{0,6},{1,7},{2,4},{3,5},{4,2},{5,3},{6,0},{7,1},{8,14},{9,15},{10,... | collective-permute-start | bytes 1572872 | tf_op jit(solution)/shard_map/ppermute | solution.py:34
  13.5 25.9 %collective-permute-start.6 = (bf16[128,2048]{1,0:T(8,128)(2,1)}, bf16[128,2048]{1,0:T(8,128)(2,1)}, u32[]{:S(2)}, u32[]{:S(2)}) collective-permute-start(bf16[128,2048]{1,0:T(8,128)(2,1)} %get-tuple-element.106), channel_id=1, source_target_pairs={{0,5},{1,6},{2,7},{3,4},{4,1},{5,2},{6,3},{7,0},{8,13},{9,14},{10,... | collective-permute-start | bytes 1572872 | tf_op jit(solution)/shard_map/ppermute | solution.py:34
  14.1 42.5 %collective-permute-start.7 = (bf16[128,2048]{1,0:T(8,128)(2,1)}, bf16[128,2048]{1,0:T(8,128)(2,1)}, u32[]{:S(2)}, u32[]{:S(2)}) collective-permute-start(bf16[128,2048]{1,0:T(8,128)(2,1)} %get-tuple-element.107), channel_id=1, source_target_pairs={{0,7},{1,4},{2,5},{3,6},{4,3},{5,0},{6,1},{7,2},{8,15},{9,12},{10,... | collective-permute-start | bytes 1572872 | tf_op jit(solution)/shard_map/ppermute | solution.py:34
  18.5 38.1 %collective-permute-start.8 = (bf16[128,2048]{1,0:T(8,128)(2,1)}, bf16[128,2048]{1,0:T(8,128)(2,1)}, u32[]{:S(2)}, u32[]{:S(2)}) collective-permute-start(bf16[128,2048]{1,0:T(8,128)(2,1)} %get-tuple-element.108), channel_id=1, source_target_pairs={{0,2},{1,3},{2,0},{3,1},{4,6},{5,7},{6,4},{7,5},{8,10},{9,11},{10,... | collective-permute-start | bytes 1572872 | tf_op jit(solution)/shard_map/ppermute | solution.py:34
  20.8 21.3 %copy-start = (bf16[1,1,1024,1024]{3,2,1,0:T(8,128)(2,1)S(1)}, bf16[1,1,1024,1024]{3,2,1,0:T(8,128)(2,1)}, u32[]{:S(2)}) copy-start(bf16[1,1,1024,1024]{3,2,1,0:T(8,128)(2,1)} %param.21) | copy-start | bytes 6291460
  21.7 9.9 %collective-permute-start = (bf16[32,8192]{1,0:T(8,128)(2,1)}, bf16[32,8192]{1,0:T(8,128)(2,1)}, u32[]{:S(2)}, u32[]{:S(2)}) collective-permute-start(bf16[32,8192]{1,0:T(8,128)(2,1)} %constant_dynamic-slice_fusion.1), channel_id=1, source_target_pairs={{0,32},{1,33},{2,34},{3,35},{4,36},{5,37},{6,38},{7,39},{8,104},{9... | collective-permute-start | bytes 1572872 | tf_op jit(solution)/shard_map/cond/branch_1_fun/ppermute | solution.py:34
  32.7 0.8 copy-start.3
  33.5 5.7 %collective-permute-start.1 = (bf16[16,8192]{1,0:T(8,128)(2,1)S(1)}, bf16[16,8192]{1,0:T(8,128)(2,1)S(1)}, u32[]{:S(2)}, u32[]{:S(2)}) collective-permute-start(bf16[16,8192]{1,0:T(8,128)(2,1)S(1)} %constant_dynamic-slice_fusion), channel_id=1, source_target_pairs={{0,96},{1,97},{2,98},{3,99},{4,100},{5,101},{6,102},{7,103},{8,40}... | collective-permute-start | bytes 786440 | tf_op jit(solution)/shard_map/cond/branch_1_fun/ppermute | solution.py:34
  33.6 5.6 %copy-start.4 = (bf16[32,8192]{1,0:T(8,128)(2,1)S(1)}, bf16[32,8192]{1,0:T(8,128)(2,1)}, u32[]{:S(2)}) copy-start(bf16[32,8192]{1,0:T(8,128)(2,1)} %copy-done.3) | copy-start | bytes 1572868 | tf_op jit(solution)/shard_map/cond
  39.3 30.5 %collective-permute-start.9 = (bf16[128,2048]{1,0:T(8,128)(2,1)}, bf16[128,2048]{1,0:T(8,128)(2,1)S(1)}, u32[]{:S(2)}, u32[]{:S(2)}) collective-permute-start(bf16[128,2048]{1,0:T(8,128)(2,1)} %get-tuple-element.121), channel_id=1, source_target_pairs={{0,1},{1,2},{2,3},{3,0},{4,5},{5,6},{6,7},{7,4},{8,9},{9,10},{10,1... | collective-permute-start | bytes 1572872 | tf_op jit(solution)/shard_map/ppermute | solution.py:34
  39.4 30.4 %collective-permute-start.10 = (bf16[128,2048]{1,0:T(8,128)(2,1)}, bf16[128,2048]{1,0:T(8,128)(2,1)}, u32[]{:S(2)}, u32[]{:S(2)}) collective-permute-start(bf16[128,2048]{1,0:T(8,128)(2,1)} %get-tuple-element.122), channel_id=1, source_target_pairs={{0,3},{1,0},{2,1},{3,2},{4,7},{5,4},{6,5},{7,6},{8,11},{9,8},{10,9... | collective-permute-start | bytes 1572872 | tf_op jit(solution)/shard_map/ppermute | solution.py:34
  42.1 12.6 %collective-permute-start.2 = (bf16[16,8192]{1,0:T(8,128)(2,1)S(1)}, bf16[16,8192]{1,0:T(8,128)(2,1)S(1)}, u32[]{:S(2)}, u32[]{:S(2)}) collective-permute-start(bf16[16,8192]{1,0:T(8,128)(2,1)S(1)} %get-tuple-element.51), channel_id=1, source_target_pairs={{0,16},{1,17},{2,18},{3,19},{4,20},{5,21},{6,22},{7,23},{8,24},{9,... | collective-permute-start | bytes 786440 | tf_op jit(solution)/shard_map/cond/branch_1_fun/ppermute | solution.py:34
  54.8 15.0 %collective-permute-start.11 = (bf16[128,2048]{1,0:T(8,128)(2,1)}, bf16[128,2048]{1,0:T(8,128)(2,1)}, u32[]{:S(2)}, u32[]{:S(2)}) collective-permute-start(bf16[128,2048]{1,0:T(8,128)(2,1)} %get-tuple-element.123), channel_id=1, source_target_pairs={{0,4},{1,5},{2,6},{3,7},{4,0},{5,1},{6,2},{7,3},{8,12},{9,13},{10,... | collective-permute-start | bytes 1572872 | tf_op jit(solution)/shard_map/ppermute | solution.py:34
  56.7 1.4 %copy-start.1 = (bf16[1024,1024]{1,0:T(8,128)(2,1)}, bf16[1024,1024]{1,0:T(8,128)(2,1)S(1)}, u32[]{:S(2)}) copy-start(bf16[1024,1024]{1,0:T(8,128)(2,1)S(1)} %get-tuple-element.61.refs_2_) | copy-start | bytes 6291460 | tf_op jit(solution)/shard_map/cond
  56.7 8.5 %collective-permute-start.3 = (bf16[16,8192]{1,0:T(8,128)(2,1)S(1)}, bf16[16,8192]{1,0:T(8,128)(2,1)}, u32[]{:S(2)}, u32[]{:S(2)}) collective-permute-start(bf16[16,8192]{1,0:T(8,128)(2,1)S(1)} %get-tuple-element.58), channel_id=1, source_target_pairs={{0,96},{1,97},{2,98},{3,99},{4,100},{5,101},{6,102},{7,103},{8,40}... | collective-permute-start | bytes 786440 | tf_op jit(solution)/shard_map/cond/branch_1_fun/ppermute | solution.py:34
  69.9 3.0 %copy-start.5 = (bf16[128,2048]{1,0:T(8,128)(2,1)}, bf16[128,2048]{1,0:T(8,128)(2,1)S(1)}, u32[]{:S(2)}) copy-start(bf16[128,2048]{1,0:T(8,128)(2,1)S(1)} %collective-permute-done.9.refs_4_) | copy-start | bytes 1572868
  69.9 14.7 %collective-permute-start.12 = (bf16[32,8192]{1,0:T(8,128)(2,1)S(1)}, bf16[32,8192]{1,0:T(8,128)(2,1)S(1)}, u32[]{:S(2)}, u32[]{:S(2)}) collective-permute-start(bf16[32,8192]{1,0:T(8,128)(2,1)S(1)} %get-tuple-element.128), channel_id=1, source_target_pairs={{0,32},{1,33},{2,34},{3,35},{4,36},{5,37},{6,38},{7,39},{8,104},{9... | collective-permute-start | bytes 1572872 | tf_op jit(solution)/shard_map/ppermute | solution.py:34
  84.5 0.8 copy-start.7
  84.7 3.4 %collective-permute-start.13 = (bf16[64,8192]{1,0:T(8,128)(2,1)S(1)}, bf16[64,8192]{1,0:T(8,128)(2,1)S(1)}, u32[]{:S(2)}, u32[]{:S(2)}) collective-permute-start(bf16[64,8192]{1,0:T(8,128)(2,1)S(1)} %maximum_select_fusion.1.total), channel_id=1, source_target_pairs={{0,8},{1,9},{2,10},{3,11},{4,12},{5,13},{6,14},{7,15},{8,0},{9,1},... | collective-permute-start | bytes 3145736 | tf_op jit(solution)/shard_map/ppermute | solution.py:34
